TPU v7x, 256 devices: a whole 4x4x8 slice. The times are simulated.
256 devices in a mesh: dp: 16 (over y, z_hi, core), owner: 16 (over z_lo, x).
Axes of the slice: x: 4, y: 4, z: 8 (z_hi: 2, z_lo: 4; z = z_hi * 4 + z_lo), core: 2. Of those that a mesh axis runs over, the one named last changes fastest.
Arguments:
- acts: bfloat16 [57344, 4096], P(('dp', 'owner')), may hold values from -64 to 64
- grads_out: bfloat16 [57344, 11008], P(('dp', 'owner')), may hold values from -64 to 64
- weight_grad: bfloat16 [4096, 11008], P('owner', 'dp'), may hold values from -6 to 6
Outputs:
- preconditioned: bfloat16 [4096, 11008], P('owner')
All inputs are finite; a program needn't handle non-finite values.
Results may differ from a plain program's by a relative error of at most 0.0011.
Values may be sent and summed in bfloat16 or wider, within the bound.
A program may use at most 320 MiB of HBM per device.

v0:
```python
import math

import jax
import jax.numpy as jnp
from jax import lax
from jax.sharding import PartitionSpec as P

D = 4096
FF = 11008
AB = 256
GB = 344


damping_level = 0.03


def block_grams(data, size):
    count = data.shape[1] // size
    split = data.reshape(data.shape[0], count, size)
    return jnp.einsum("tkb,tkc->kbc", split, split, preferred_element_type=jnp.float32)


def damped_inverse(blocks, damping):
    identity = jnp.eye(blocks.shape[-1], dtype=jnp.float32)
    lower = jnp.linalg.cholesky(blocks + damping * identity)

    def solve_one(factor):
        return jax.scipy.linalg.cho_solve((factor, True), identity)

    return jax.vmap(solve_one)(lower)


def trace_of(blocks):
    return jnp.sum(jnp.diagonal(blocks, axis1=1, axis2=2))


def shards(acts, grads_out, weight_grad):
    dp_count = lax.axis_size("dp")
    owner_count = lax.axis_size("owner")
    total = float(acts.shape[0] * dp_count * owner_count)
    own_act_blocks = weight_grad.shape[0] // AB
    own_grad_blocks = weight_grad.shape[1] // GB
    act_part = block_grams(acts, AB)
    grad_part = block_grams(grads_out, GB)
    own_act = lax.psum_scatter(act_part, "owner", scatter_dimension=0, tiled=True)
    own_act = lax.psum(own_act, "dp")
    own_grad = lax.psum_scatter(grad_part, "dp", scatter_dimension=0, tiled=True)
    own_grad = lax.psum(own_grad, "owner")
    own_act = own_act / total
    own_grad = own_grad / total
    act_trace = lax.psum(trace_of(own_act), "owner")
    grad_trace = lax.psum(trace_of(own_grad), "dp")
    ratio = jnp.sqrt(act_trace / D / (grad_trace / FF))
    act_inverse = damped_inverse(own_act, ratio * math.sqrt(damping_level))
    grad_inverse = damped_inverse(own_grad, math.sqrt(damping_level) / ratio)
    columns = weight_grad.shape[1]
    gradient = weight_grad.astype(jnp.float32).reshape(own_act_blocks, AB, columns)
    left = jnp.einsum("kab,kbf->kaf", act_inverse, gradient, precision=lax.Precision.HIGHEST)
    left = left.reshape(own_act_blocks * AB, own_grad_blocks, GB)
    result = jnp.einsum("rkb,kbc->rkc", left, grad_inverse, precision=lax.Precision.HIGHEST)
    result = result.reshape(own_act_blocks * AB, columns).astype(jnp.bfloat16)
    return lax.all_gather(result, "dp", axis=1, tiled=True)


def solution(mesh):
    in_specs = (P(("dp", "owner"), None), P(("dp", "owner"), None), P("owner", "dp"))
    out_specs = P("owner", None)
    return jax.shard_map(shards, mesh=mesh, in_specs=in_specs, out_specs=out_specs, check_vma=False)
```

profile of v0, /device:TPU:33, one launch (start us, length us, event | category | flops | bytes accessed | tf_op | source)
XLA Modules:
  0.0 1111.4 jit_solution(9337307943741410911)
XLA Ops:
  6.5 4.8 fusion.2
  11.4 15.6 %reshape.231 = bf16[224,32,344]{2,1,0:T(8,128)(2,1)} reshape(bf16[224,11008]{1,0:T(8,128)(2,1)} %param.4) | data formatting | bytes 9863168 | tf_op jit(solution)/shard_map/reshape | solution.py:19
  27.0 17.6 %fusion = f32[32,344,344]{1,2,0:T(8,128)} fusion(bf16[224,32,344]{2,1,0:T(8,128)(2,1)} %reshape.231), kind=kOutput, calls=%fused_computation.7 | convolution fusion | flops 1696464896 | bytes 20078592 | tf_op jit(solution)/shard_map/tkb,tkc->kbc/dot_general | solution.py:20
  44.7 45.7 %reduce-scatter.5.cloned.1.call-done = f32[1,256,256]{1,2,0:T(8,128)} async-done(((f32[16,256,256]{1,2,0:T(8,128)}), f32[1,256,256]{1,2,0:T(8,128)}) %reduce-scatter.5.cloned.1.call-update) | async-done | bytes 262160 | tf_op jit(solution)/shard_map/reduce_scatter | solution.py:45
  90.6 240.3 %reduce-scatter.3.cloned.1.call-done = f32[2,344,344]{1,2,0:T(8,128)} async-done(((f32[32,344,344]{1,2,0:T(8,128)}), f32[2,344,344]{1,2,0:T(8,128)}) %reduce-scatter.3.cloned.1.call-update) | async-done | bytes 946704 | tf_op jit(solution)/shard_map/reduce_scatter | solution.py:47
  333.1 172.3 %all-reduce.9.cloned.1.call-done = f32[1,256,256]{1,2,0:T(8,128)} async-done(((f32[1,256,256]{1,2,0:T(8,128)}), f32[1,256,256]{1,2,0:T(8,128)}) %all-reduce.9.cloned.1.call-update) | async-done | bytes 262160 | tf_op jit(solution)/shard_map/psum | solution.py:46
  509.6 29.2 %psum.30 = f32[]{:T(128)} all-reduce(f32[]{:T(128)} %reduce.36), channel_id=1, replica_groups=mesh['dp'=16,'owner'=16] {'owner'}, use_global_device_ids=true, to_apply=%region_5.6 | all-reduce | flops 1 | bytes 8 | tf_op jit(solution)/shard_map/psum | solution.py:51
  538.8 118.3 %all-reduce.7.cloned.1.call-done = f32[2,344,344]{1,2,0:T(8,128)} async-done(((f32[2,344,344]{1,2,0:T(8,128)}), f32[2,344,344]{1,2,0:T(8,128)}) %all-reduce.7.cloned.1.call-update) | async-done | bytes 946704 | tf_op jit(solution)/shard_map/psum | solution.py:48
  658.4 35.3 %copy.88 = f32[2,344,344]{0,2,1:T(8,128)} copy(f32[2,344,344]{1,2,0:T(8,128)S(1)} %broadcast_multiply_fusion) | data formatting | bytes 1893376 | tf_op jit(solution)/shard_map/div | solution.py:50
  693.7 10.2 gather_fusion.1
  705.3 52.8 %psum.31 = f32[]{:T(128)} all-reduce(f32[]{:T(128)} %reduce_sum.19), channel_id=1, replica_groups=mesh['dp'=16,'owner'=16] {'dp'}, use_global_device_ids=true, to_apply=%region_7.8 | all-reduce | flops 1 | bytes 8 | tf_op jit(solution)/shard_map/psum | solution.py:52
  762.8 23.5 %custom-call.49 = f32[2,128,128]{2,1,0:T(8,128)S(1)} custom-call(f32[2,128,128]{2,1,0:T(8,128)S(1)} %cholesky.319), custom_call_target="Cholesky" | custom-call | tf_op jit(solution)/shard_map/jit(cholesky)/cholesky | solution.py:25
  786.3 19.7 %custom-call.50 = f32[2,1,128,128]{2,3,1,0:T(8,128)S(1)} custom-call(f32[2,1,128,128]{3,2,1,0:T(8,128)S(1)} %select_bitcast_fusion.1), custom_call_target="InvertDiagBlocksLowerTriangular" | custom-call | tf_op jit(solution)/shard_map/jit(cholesky)/cholesky | solution.py:25
  807.1 23.5 %custom-call.51 = f32[2,128,128]{2,1,0:T(8,128)S(1)} custom-call(f32[2,128,128]{2,1,0:T(8,128)S(1)} %cholesky.323), custom_call_target="Cholesky" | custom-call | tf_op jit(solution)/shard_map/jit(cholesky)/cholesky | solution.py:25
  830.6 19.8 %custom-call.52 = f32[2,1,128,128]{2,3,1,0:T(8,128)S(1)} custom-call(f32[2,1,128,128]{3,2,1,0:T(8,128)S(1)} %get-tuple-element.61), custom_call_target="InvertDiagBlocksLowerTriangular" | custom-call | tf_op jit(solution)/shard_map/jit(cholesky)/cholesky | solution.py:25
  851.0 16.2 %custom-call.53 = f32[2,88,88]{2,1,0:T(8,128)S(1)} custom-call(f32[2,88,88]{2,1,0:T(8,128)S(1)} %convolution_subtract_fusion.6), custom_call_target="Cholesky" | custom-call | tf_op jit(solution)/shard_map/jit(cholesky)/cholesky | solution.py:25
  872.7 59.2 %custom-call.54 = f32[2,3,128,128]{2,3,1,0:T(8,128)S(1)} custom-call(f32[2,3,128,128]{3,2,1,0:T(8,128)S(1)} %pad_maximum_fusion), custom_call_target="InvertDiagBlocksLowerTriangular" | custom-call | tf_op jit(solution)/shard_map/vmap(jit(_cho_solve))/triangular_solve | solution.py:28
  938.6 11.7 %custom-call.55 = f32[1,128,128]{2,1,0:T(8,128)S(1)} custom-call(f32[1,128,128]{2,1,0:T(8,128)S(1)} %cholesky.327), custom_call_target="Cholesky" | custom-call | tf_op jit(solution)/shard_map/jit(cholesky)/cholesky | solution.py:25
  950.4 9.8 custom-call.56
  962.4 11.9 %custom-call.57 = f32[1,128,128]{2,1,0:T(8,128)S(1)} custom-call(f32[1,128,128]{2,1,0:T(8,128)S(1)} %fusion.7), custom_call_target="Cholesky" | custom-call | tf_op jit(solution)/shard_map/jit(cholesky)/cholesky | solution.py:25
  979.0 5.5 while.3
  984.6 20.5 %custom-call.58 = f32[1,2,128,128]{2,3,1,0:T(8,128)S(1)} custom-call(f32[1,2,128,128]{3,2,1,0:T(8,128)} %bitcast.140), custom_call_target="InvertDiagBlocksLowerTriangular" | custom-call | tf_op jit(solution)/shard_map/vmap(jit(_cho_solve))/triangular_solve | solution.py:28
  1009.5 86.6 %all-gather.2.cloned.1.call-done = bf16[256,11008]{0,1:T(8,128)(2,1)} async-done(((bf16[256,688]{0,1:T(8,128)(2,1)}), bf16[256,11008]{0,1:T(8,128)(2,1)}) %all-gather.2.cloned.1.call-update) | async-done | bytes 5636112 | tf_op jit(solution)/shard_map/all_gather | solution.py:62
  1096.1 8.3 copy.109
  (131 shorter events, 45.5 us)
Async XLA Ops:
  6.5 1000.3 %copy-start = (bf16[256,688]{0,1:T(8,128)(2,1)S(1)}, bf16[256,688]{0,1:T(8,128)(2,1)}, u32[]{:S(2)}) copy-start(bf16[256,688]{0,1:T(8,128)(2,1)} %param.5) | copy-start | bytes 1056772
  6.5 83.9 %reduce-scatter.5.cloned.1.call-start = ((), (), s32[]{:S(2)}) async-start(), calls=%async_computation.4 | async-start | bytes 4456448 | tf_op jit(solution)/shard_map/reduce_scatter | solution.py:45
  11.4 319.6 %reduce-scatter.3.cloned.1.call-start = ((), (), s32[]{:S(2)}) async-start(), calls=%async_computation.2 | async-start | bytes 17965056 | tf_op jit(solution)/shard_map/reduce_scatter | solution.py:47
  44.7 460.7 %all-reduce.9.cloned.1.call-start = ((), (), s32[]{:S(2)}) async-start(), calls=%async_computation.5 | async-start | bytes 524288 | tf_op jit(solution)/shard_map/psum | solution.py:46
  90.5 566.6 %all-reduce.7.cloned.1.call-start = ((), (), s32[]{:S(2)}) async-start(), calls=%async_computation.3 | async-start | bytes 2113536 | tf_op jit(solution)/shard_map/psum | solution.py:48
  90.6 242.5 %copy-start.5 = (f32[344,344]{0,1:T(8,128)}, f32[344,344]{0,1:T(8,128)S(1)}, u32[]{:S(2)}) copy-start(f32[344,344]{0,1:T(8,128)S(1)} %fusion.20) | copy-start | bytes 1420036
  331.0 765.1 %all-gather.2.cloned.1.call-start = ((), (), s32[]{:S(2)}) async-start(), calls=%async_computation.6 | async-start | bytes 5988352 | tf_op jit(solution)/shard_map/all_gather | solution.py:62
  505.4 4.1 slice-start
  658.4 100.5 %copy-start.1 = (f32[2,344,344]{1,2,0:T(8,128)S(1)}, f32[2,344,344]{1,2,0:T(8,128)}, u32[]{:S(2)}) copy-start(f32[2,344,344]{1,2,0:T(8,128)} %all-reduce.7.cloned.1.call-done) | copy-start | bytes 2840068
  761.7 1.0 copy-start.2
  762.7 43.3 %copy-start.3 = (f32[2,344,344]{2,1,0:T(8,128)S(1)}, f32[2,344,344]{2,1,0:T(8,128)}, u32[]{:S(2)}) copy-start(f32[2,344,344]{2,1,0:T(8,128)} %copy-done.2) | copy-start | bytes 2840068
  867.5 0.6 copy-start.11
  867.5 1.0 copy-start.9
  868.5 63.4 %copy-start.7 = (f32[128,344]{0,1:T(8,128)S(1)}, f32[128,344]{0,1:T(8,128)}, u32[]{:S(2)}) copy-start(f32[128,344]{0,1:T(8,128)} %get-tuple-element.60) | copy-start | bytes 528388
  872.5 60.1 %copy-start.8 = (f32[128,344]{0,1:T(8,128)S(1)}, f32[128,344]{0,1:T(8,128)}, u32[]{:S(2)}) copy-start(f32[128,344]{0,1:T(8,128)} %get-tuple-element.59) | copy-start | bytes 528388
  935.3 1.4 copy-start.4
  938.6 11.8 %copy-start.6 = (f32[1,256,256]{2,1,0:T(8,128)}, f32[1,256,256]{2,1,0:T(8,128)S(1)}, u32[]{:S(2)}) copy-start(f32[1,256,256]{2,1,0:T(8,128)S(1)} %fusion.25) | copy-start | bytes 786436
  979.0 26.0 %copy-start.10 = (pred[1,256,256]{1,2,0:T(32,128)(4,1)S(1)}, pred[1,256,256]{1,2,0:T(32,128)(4,1)}, u32[]{:S(2)}) copy-start(pred[1,256,256]{1,2,0:T(32,128)(4,1)} %iota_compare_fusion.2) | copy-start | bytes 196612
Sparse Core Ops, SparseCore 0:
  11.5 78.9 reduce-scatter.4
  95.2 235.7 reduce-scatter.2
  333.6 171.7 all-reduce.8
  508.1 148.9 all-reduce.6
  1009.6 86.4 all-gather.1
where the time goes:
time: 1120 us; the launch traced here: 1110 us
  waiting for transfers between devices  663 us (59%)
  other arithmetic  225 us (20%)
  local copies, waits for them, and re-layouts  86.6 us (8%)
  blocking collectives  82 us (7%)
  matrix products  37.4 us (3%)
  between operations  16.9 us (2%)
    reduce_scatter x1, waiting for transfers between devices, shards(): lax.psum_scatter(grad_part, 'dp', scatter_dimension=0, tiled=True)  240 us
    psum x1, waiting for transfers between devices, shards(): own_act = lax.psum(own_act, 'dp')  172 us
    another operation x20, other arithmetic, damped_inverse(): lower = jnp.linalg.cholesky(blocks + damping * identity)  137 us
    psum x1, waiting for transfers between devices, shards(): own_grad = lax.psum(own_grad, 'owner')  118 us
    all_gather x1, waiting for transfers between devices, shards(): return lax.all_gather(result, 'dp', axis=1, tiled=True)  86.6 us
    another operation x10, other arithmetic, solve_one(): return jax.scipy.linalg.cho_solve((factor, True), identity)  80.6 us
    psum x1, blocking collectives, shards(): grad_trace = lax.psum(trace_of(own_grad), 'dp')  52.8 us
    reduce_scatter x1, waiting for transfers between devices, shards(): lax.psum_scatter(act_part, 'owner', scatter_dimension=0, tiled=True)  45.7 us
  transfers between devices with their start and end apart: 5, of which 5 were waited for; matrix products, arithmetic and copies ran while one was open for 4% of the time, Pallas kernels for 0%

commit v1 on v0

v1 whole, which is shorter than its diff:
```python
import functools
import math

import jax
import jax.numpy as jnp
from jax import lax
from jax.experimental import pallas as pl
from jax.experimental.pallas import tpu as pltpu
from jax.sharding import PartitionSpec as P

D = 4096
FF = 11008
AB = 256
GB = 344
TOKENS = 57344
DAMP = math.sqrt(0.03)
MESH = pl.DeviceIdType.MESH
HIGH = lax.Precision.HIGHEST
F32 = jnp.float32
GROWS = 96
AROWS = 24
CH = GROWS + AROWS
HALF = 4 * CH
VLIM = 56 * 1024 * 1024


def place():
    dp = lax.axis_index("dp")
    own = lax.axis_index("owner")
    return dp, own


def swap_kernel(a_ref, g_ref, ao_ref, go_ref, local, send, recv):
    dp, own = place()
    core = lax.rem(dp, 2)
    sib = dp + 1 - 2 * core
    barrier = pltpu.get_barrier_semaphore()
    pl.semaphore_signal(barrier, inc=1, device_id=(sib, own), device_id_type=MESH)
    pl.semaphore_wait(barrier, 1)
    remote = []
    locals_ = []
    for i, (src, dst) in enumerate(((a_ref, ao_ref), (g_ref, go_ref))):
        width = dst.shape[2]
        theirs = pl.ds(pl.multiple_of((1 - core) * width, 128), width)
        mine = pl.ds(pl.multiple_of(core * width, 128), width)
        copy = pltpu.make_async_remote_copy(
            src_ref=src.at[:, theirs], dst_ref=dst.at[1], send_sem=send.at[i], recv_sem=recv.at[i],
            device_id=(sib, own), device_id_type=MESH)
        copy.start()
        remote.append(copy)
        keep = pltpu.make_async_copy(src.at[:, mine], dst.at[0], local.at[i])
        keep.start()
        locals_.append(keep)
    for copy in remote + locals_:
        copy.wait()


def swap(acts, grads):
    rows = acts.shape[0]
    return pl.pallas_call(
        swap_kernel,
        out_shape=(jax.ShapeDtypeStruct((2, rows, D // 2), acts.dtype),
                   jax.ShapeDtypeStruct((2, rows, FF // 2), acts.dtype)),
        in_specs=[pl.BlockSpec(memory_space=pl.ANY)] * 2,
        out_specs=(pl.BlockSpec(memory_space=pl.ANY),) * 2,
        scratch_shapes=[pltpu.SemaphoreType.DMA((2,))] * 3,
        compiler_params=pltpu.CompilerParams(collective_id=0, has_side_effects=True),
        name="swap",
    )(acts, grads)


def gram(block):
    return lax.dot_general(block, block, (((0,), (0,)), ((), ())), preferred_element_type=F32)


def gram_kernel(a_ref, g_ref, x_ref, y_ref, t_ref):
    def store(j, rows, start, value):
        chunk = start // CH
        px, py = j // 4, j % 4
        if chunk < 4:
            x_ref[px * 4 + py, pl.ds(start, rows), :] = value
        else:
            y_ref[py * 4 + px, pl.ds(start - HALF, rows), :] = value

    zero = jnp.zeros((128, 128), F32)
    grad_sum = jnp.zeros((8, 128), F32)
    act_sum = jnp.zeros((8, 128), F32)
    eye = (lax.broadcasted_iota(jnp.int32, (128, 128), 0)
           == lax.broadcasted_iota(jnp.int32, (128, 128), 1))

    def diag(tile):
        return jnp.sum(jnp.where(eye, tile, 0.0).reshape(16, 8, 128), axis=0)

    for j in range(16):
        g = gram(g_ref[:, j * GB:(j + 1) * GB])
        low = jnp.concatenate([g[256:344, :], jnp.zeros((40, GB), F32)], axis=0)
        low2 = jnp.concatenate([low[:, 256:344], jnp.zeros((128, 40), F32)], axis=1)
        tiles = [g[0:128, 0:128], g[128:256, 0:128], g[128:256, 128:256], low[:, 0:128], low[:, 128:256], low2]
        grad_sum += diag(tiles[0]) + diag(tiles[2]) + diag(tiles[5])
        for u in range(24):
            start = (u // 3) * CH + (u % 3) * 32
            r = (u % 4) * 32
            store(j, 32, start, tiles[u // 4][r:r + 32])
    for k in range(8):
        g = gram(a_ref[:, k * AB:(k + 1) * AB])
        tiles = [g[0:128, 0:128], g[128:256, 0:128], g[128:256, 128:256]]
        act_sum += diag(tiles[0]) + diag(tiles[2])
        for u in range(48):
            j = 2 * k + u // 24
            v = u % 24
            start = (v // 3) * CH + GROWS + (v % 3) * 8
            r = (u % 16) * 8
            store(j, 8, start, tiles[u // 16][r:r + 8])
    t_ref[0:8, :] = act_sum
    t_ref[8:16, :] = grad_sum


def grams(acts, grads):
    shape = jax.ShapeDtypeStruct((16, HALF, 128), F32)
    vmem = pl.BlockSpec(memory_space=pltpu.VMEM)
    return pl.pallas_call(
        gram_kernel,
        out_shape=(shape, shape, jax.ShapeDtypeStruct((16, 128), F32)),
        in_specs=[vmem] * 2,
        out_specs=(vmem,) * 3,
        compiler_params=pltpu.CompilerParams(vmem_limit_bytes=VLIM),
        name="grams",
    )(acts, grads)


def reduce_kernel(gx, gy, tr, fg_out, fa_out, t_out,
                  sx, sy, rx, ry, rx2, ry2, st, rz, fin, fg, fa, t1, t2, t3, q1, q2, q3, q4,
                  local, s1, r1, s2, r2, s3, r3, sg, rg, sa, ra, s4, r4):
    dp, own = place()
    core = lax.rem(dp, 2)
    zh = lax.rem(dp // 2, 2)
    y = dp // 4
    x = lax.rem(own, 4)
    zl = own // 4
    z = zh * 4 + zl
    sib = dp + 1 - 2 * core

    def at(ax, ay, az, ac):
        return ((ay * 2 + az // 4) * 2 + ac, lax.rem(az, 4) * 4 + ax)

    xs = [at(lax.rem(x + k, 4), y, z, core) for k in (1, 2, 3)]
    ys = [at(x, lax.rem(y + k, 4), z, core) for k in (1, 2, 3)]
    zs = [at(x, y, lax.rem(z + k, 8), core) for k in range(1, 8)]
    j = x * 4 + y
    unit = core * 8 + j // 2
    part = lax.rem(j, 2)

    barrier = pltpu.get_barrier_semaphore()

    def greet(device):
        pl.semaphore_signal(barrier, inc=1, device_id=device, device_id_type=MESH)

    for device in xs + ys + zs + [(sib, own)]:
        greet(device)

    def greet_sources(base):
        def body(i, _):
            js = lax.rem(base, 8) * 2 + i // 8
            device = at(js // 4, lax.rem(js, 4), lax.rem(i, 8), base // 8)

            @pl.when(jnp.logical_or(device[0] != dp, device[1] != own))
            def _():
                greet(device)
            return 0
        lax.fori_loop(0, 16, body, 0)

    greet_sources(dp)
    greet_sources(own)
    self_g = jnp.where(unit == dp, 1, 0)
    self_a = jnp.where(unit == own, 1, 0)
    pl.semaphore_wait(barrier, 14 + 32 - self_g - self_a)

    def send(src, dst, ssem, rsem, device):
        copy = pltpu.make_async_remote_copy(src_ref=src, dst_ref=dst, send_sem=ssem, recv_sem=rsem,
                                            device_id=device, device_id_type=MESH)
        copy.start()
        return copy

    copies = []
    for k in range(3):
        copies.append(send(gx.at[pl.ds(lax.rem(x + k + 1, 4) * 4, 4)], rx.at[k], s1.at[k], r1.at[k], xs[k]))
        copies.append(send(gy.at[pl.ds(lax.rem(y + k + 1, 4) * 4, 4)], ry.at[k], s1.at[3 + k], r1.at[3 + k], ys[k]))
        copies.append(send(tr, q1.at[k], s1.at[6 + k], r1.at[6 + k], xs[k]))
    copies.append(pltpu.make_async_copy(gx.at[pl.ds(x * 4, 4)], sx, local.at[0]))
    copies[-1].start()
    copies.append(pltpu.make_async_copy(gy.at[pl.ds(y * 4, 4)], sy, local.at[1]))
    copies[-1].start()
    for copy in copies:
        copy.wait()

    @pl.loop(0, 16)
    def _(i):
        a = i // 4
        rows = pl.ds(pl.multiple_of(lax.rem(i, 4) * CH, 8), CH)
        sx[a, rows, :] = (sx[a, rows, :] + rx[0, a, rows, :]) + (rx[1, a, rows, :] + rx[2, a, rows, :])
        sy[a, rows, :] = (sy[a, rows, :] + ry[0, a, rows, :]) + (ry[1, a, rows, :] + ry[2, a, rows, :])
    t1[...] = (tr[...] + q1[0]) + (q1[1] + q1[2])

    copies = []
    for k in range(3):
        copies.append(send(sx.at[lax.rem(y + k + 1, 4)], rx2.at[k], s2.at[k], r2.at[k], ys[k]))
        copies.append(send(sy.at[lax.rem(x + k + 1, 4)], ry2.at[k], s2.at[3 + k], r2.at[3 + k], xs[k]))
        copies.append(send(t1, q2.at[k], s2.at[6 + k], r2.at[6 + k], ys[k]))
    for copy in copies:
        copy.wait()

    @pl.loop(0, 4)
    def _(i):
        rows = pl.ds(pl.multiple_of(i * CH, 8), CH)
        st[i] = (sx[y, rows, :] + rx2[0, rows, :]) + (rx2[1, rows, :] + rx2[2, rows, :])
        st[4 + i] = (sy[x, rows, :] + ry2[0, rows, :]) + (ry2[1, rows, :] + ry2[2, rows, :])
    t2[...] = (t1[...] + q2[0]) + (q2[1] + q2[2])

    copies = []
    for k in range(7):
        copies.append(send(st.at[lax.rem(z + k + 1, 8)], rz.at[k], s3.at[k], r3.at[k], zs[k]))
        copies.append(send(t2, q3.at[k], s3.at[7 + k], r3.at[7 + k], zs[k]))
    for copy in copies:
        copy.wait()
    total = st[z]
    trace = t2[...]
    for k in range(7):
        total += rz[k]
        trace += q3[k]
    fin[...] = total
    t3[...] = trace

    side = send(t3, q4, s4, r4, (sib, own))
    gsrc = fin.at[pl.ds(0, GROWS)]
    asrc = fin.at[pl.ds(GROWS, AROWS)]
    gdst = fg.at[part, z]
    adst = fa.at[part, z]
    slot = part * 8 + z

    def put(src, dst, ssem, rsem, device, mine):
        @pl.when(mine)
        def _():
            pltpu.make_async_copy(src, dst, rsem).start()

        @pl.when(jnp.logical_not(mine))
        def _():
            send(src, dst, ssem, rsem, device)

    put(gsrc, gdst, sg.at[0], rg.at[slot], (unit, own), unit == dp)
    put(asrc, adst, sa.at[0], ra.at[slot], (dp, unit), unit == own)

    def out(k, _):
        send(gsrc, gdst, sg.at[k], rg.at[slot], (unit, lax.rem(own + k, 16)))
        send(asrc, adst, sa.at[k], ra.at[slot], (lax.rem(dp + k, 16), unit))
        return 0
    lax.fori_loop(1, 16, out, 0)

    def sent(src, dst, ssem):
        pltpu.make_async_remote_copy(src_ref=src, dst_ref=dst, send_sem=ssem, recv_sem=r4,
                                     device_id=(sib, own), device_id_type=MESH).wait_send()

    def got(dst, src, rsem):
        pltpu.make_async_copy(src, dst, rsem).wait()

    def arrive(k, _):
        got(fg.at[k // 8, lax.rem(k, 8)], gsrc, rg.at[k])
        got(fa.at[k // 8, lax.rem(k, 8)], asrc, ra.at[k])
        return 0
    lax.fori_loop(0, 16, arrive, 0)

    def left(k, _):
        sent(gsrc, gdst, sg.at[k])
        sent(asrc, adst, sa.at[k])
        return 0
    lax.fori_loop(1, 16, left, 0)

    @pl.when(unit != dp)
    def _():
        sent(gsrc, gdst, sg.at[0])

    @pl.when(unit != own)
    def _():
        sent(asrc, adst, sa.at[0])
    side.wait()
    fg_out[...] = fg[...]
    fa_out[...] = fa[...]
    t_out[...] = t3[...] + q4[...]


def reduce_all(gx, gy, tr):
    vmem = pl.BlockSpec(memory_space=pltpu.VMEM)
    dma = pltpu.SemaphoreType.DMA
    tile = pltpu.VMEM((16, 128), F32)
    return pl.pallas_call(
        reduce_kernel,
        out_shape=(jax.ShapeDtypeStruct((2, 8, GROWS, 128), F32),
                   jax.ShapeDtypeStruct((2, 8, AROWS, 128), F32),
                   jax.ShapeDtypeStruct((16, 128), F32)),
        in_specs=[pl.BlockSpec(memory_space=pl.ANY)] * 2 + [vmem],
        out_specs=(vmem,) * 3,
        scratch_shapes=[
            pltpu.VMEM((4, HALF, 128), F32), pltpu.VMEM((4, HALF, 128), F32),
            pltpu.VMEM((3, 4, HALF, 128), F32), pltpu.VMEM((3, 4, HALF, 128), F32),
            pltpu.VMEM((3, HALF, 128), F32), pltpu.VMEM((3, HALF, 128), F32),
            pltpu.VMEM((8, CH, 128), F32), pltpu.VMEM((7, CH, 128), F32), pltpu.VMEM((CH, 128), F32),
            pltpu.VMEM((2, 8, GROWS, 128), F32), pltpu.VMEM((2, 8, AROWS, 128), F32),
            tile, tile, tile,
            pltpu.VMEM((3, 16, 128), F32), pltpu.VMEM((3, 16, 128), F32), pltpu.VMEM((7, 16, 128), F32), tile,
            dma((2,)), dma((9,)), dma((9,)), dma((9,)), dma((9,)), dma((14,)), dma((14,)),
            dma((16,)), dma((16,)), dma((16,)), dma((16,)), dma, dma,
        ],
        compiler_params=pltpu.CompilerParams(collective_id=1, has_side_effects=True, vmem_limit_bytes=VLIM),
        name="reduce_all",
    )(gx, gy, tr)


def dot(a, b, ca=1, cb=0):
    return lax.dot_general(a, b, (((ca,), (cb,)), ((), ())), precision=HIGH, preferred_element_type=F32)


def sweep_tiles(refs, panels):
    sub = lax.broadcasted_iota(jnp.int32, (8, 128), 0)
    lane = lax.broadcasted_iota(jnp.int32, (8, 128), 1)
    lane_all = lax.broadcasted_iota(jnp.int32, (128, 128), 1)

    def panel(p, _):
        base = pl.multiple_of(p * 8, 8)
        rows = pl.ds(base, 8)
        back = lax.rem(128 - base, 128)
        olds = [ref[rows, :] for ref in refs]
        news = [pltpu.roll(old, back, 1) for old in olds]
        for s in range(8):
            for i, now in enumerate(news):
                col = jnp.broadcast_to(now[:, s:s + 1], (8, 128))
                row = jnp.broadcast_to(now[s:s + 1, :], (8, 128))
                inv = 1.0 / jnp.broadcast_to(col[s:s + 1, :], (8, 128))
                col = jnp.where(sub == s, -1.0, col)
                row = jnp.where(lane == s, -1.0, row)
                keep = jnp.where(jnp.logical_or(sub == s, lane == s), 0.0, now)
                news[i] = keep - col * (row * inv)
        inside = jnp.logical_and(lane_all >= base, lane_all < base + 8)
        for ref, old, new in zip(refs, olds, news):
            new = pltpu.roll(new, base, 1)
            ref[...] = jnp.where(inside, 0.0, ref[...]) - dot(old, new, 0, 0)
            ref[rows, :] = new
        return 0

    lax.fori_loop(0, panels, panel, 0)


def solve_kernel(fg_ref, fa_ref, t_ref, w_ref, p_ref, g_ref, a_ref, gi_ref, ai_ref):
    act_trace = jnp.sum(t_ref[0:8, :], keepdims=True) / TOKENS
    grad_trace = jnp.sum(t_ref[8:16, :], keepdims=True) / TOKENS
    ratio = jnp.sqrt(act_trace / D / (grad_trace / FF))
    act_damp = ratio * DAMP
    grad_damp = DAMP / ratio
    r = lax.broadcasted_iota(jnp.int32, (128, 128), 0)
    c = lax.broadcasted_iota(jnp.int32, (128, 128), 1)
    eye = jnp.where(r == c, 1.0, 0.0)
    last = GB - 256
    for b in range(2):
        for t in range(6):
            tile = fg_ref[b, t * 128:(t + 1) * 128, :] / TOKENS
            if t in (0, 2):
                tile = tile + grad_damp * eye
            if t in (3, 4):
                tile = jnp.where(r < last, tile, 0.0)
            if t == 5:
                tile = jnp.where(jnp.logical_and(r < last, c < last), tile + grad_damp * eye, eye)
            g_ref[b * 6 + t] = tile
    for t in range(3):
        tile = fa_ref[t * 128:(t + 1) * 128, :] / TOKENS
        if t != 1:
            tile = tile + act_damp * eye
        a_ref[t] = tile
    gs = [[g_ref.at[b * 6 + t] for t in range(6)] for b in range(2)]
    am = [a_ref.at[t] for t in range(3)]
    sweep_tiles([gs[0][0], gs[1][0], am[0]], 16)
    for m in gs:
        neg = m[0][...]
        a10, a20 = m[1][...], m[3][...]
        v10, v20 = -dot(a10, neg), -dot(a20, neg)
        m[2][...] -= dot(v10, a10, 1, 1)
        m[4][...] -= dot(v20, a10, 1, 1)
        m[5][...] -= dot(v20, a20, 1, 1)
        m[1][...] = v10
        m[3][...] = v20
    a10 = am[1][...]
    v10 = -dot(a10, am[0][...])
    am[2][...] -= dot(v10, a10, 1, 1)
    am[1][...] = v10
    sweep_tiles([gs[0][2], gs[1][2], am[2]], 16)
    for m in gs:
        neg = m[2][...]
        a10, a21 = m[1][...], m[4][...]
        v10, v21 = -dot(neg, a10), -dot(a21, neg)
        m[0][...] -= dot(a10, v10, 0, 0)
        m[3][...] -= dot(a21, v10)
        m[5][...] -= dot(v21, a21, 1, 1)
        m[1][...] = v10
        m[4][...] = v21
    a10 = am[1][...]
    v10 = -dot(am[2][...], a10)
    am[0][...] -= dot(a10, v10, 0, 0)
    am[1][...] = v10
    sweep_tiles([gs[0][5], gs[1][5]], last // 8)
    for m in gs:
        neg = m[5][...]
        a20, a21 = m[3][...], m[4][...]
        v20, v21 = -dot(neg, a20), -dot(neg, a21)
        m[0][...] -= dot(a20, v20, 0, 0)
        m[1][...] -= dot(a21, v20, 0, 0)
        m[2][...] -= dot(a21, v21, 0, 0)
        m[3][...] = v20
        m[4][...] = v21
    ai_ref[0:128, 0:128] = -am[0][...]
    ai_ref[128:256, 0:128] = -am[1][...]
    ai_ref[0:128, 128:256] = -am[1][...].T
    ai_ref[128:256, 128:256] = -am[2][...]
    for b, m in enumerate(gs):
        for t, (i, j) in enumerate(((0, 0), (1, 0), (1, 1), (2, 0), (2, 1), (2, 2))):
            tile = -m[t][...]
            gi_ref[b, i * 128:(i + 1) * 128, j * 128:(j + 1) * 128] = tile
            if i != j:
                gi_ref[b, j * 128:(j + 1) * 128, i * 128:(i + 1) * 128] = tile.T
    for b in range(2):
        left = dot(ai_ref[...], w_ref[b].astype(F32))
        p_ref[:, b * 384:(b + 1) * 384] = dot(left, gi_ref[b]).astype(jnp.bfloat16)


def solve(fg, fa, tr, w):
    vmem = pl.BlockSpec(memory_space=pltpu.VMEM)
    return pl.pallas_call(
        solve_kernel,
        out_shape=jax.ShapeDtypeStruct((256, 768), jnp.bfloat16),
        in_specs=[vmem] * 4,
        out_specs=vmem,
        scratch_shapes=[pltpu.VMEM((12, 128, 128), F32), pltpu.VMEM((3, 128, 128), F32),
                        pltpu.VMEM((2, 384, 384), F32), pltpu.VMEM((256, 256), F32)],
        compiler_params=pltpu.CompilerParams(vmem_limit_bytes=VLIM),
        name="solve",
    )(fg, fa, tr, w)


def gather_kernel(p_ref, o_ref, local, sz, rz, sy, ry, sh, rh, sc, rc):
    dp, own = place()
    core = lax.rem(dp, 2)
    y = dp // 4
    sib = dp + 1 - 2 * core
    zh = lax.rem(dp // 2, 2)
    anti = dp + 2 - 4 * zh
    up = lax.rem(y + 1, 4) * 4 + lax.rem(dp, 4)
    down = lax.rem(y + 3, 4) * 4 + lax.rem(dp, 4)
    barrier = pltpu.get_barrier_semaphore()
    for device in (sib, anti, up, down):
        pl.semaphore_signal(barrier, inc=1, device_id=(device, own), device_id_type=MESH)
    pl.semaphore_wait(barrier, 4)

    def other(d):
        return d + 2 - 4 * lax.rem(d // 2, 2)

    waits = []

    def send(d, ssem, rsem, device, src=None, half=None):
        src = o_ref.at[d] if src is None else src
        dst = o_ref.at[d]
        if half is not None:
            src = src.at[pl.ds(half * 128, 128)]
            dst = dst.at[pl.ds(half * 128, 128)]
        copy = pltpu.make_async_remote_copy(src_ref=src, dst_ref=dst, send_sem=ssem, recv_sem=rsem,
                                            device_id=(device, own), device_id_type=MESH)
        copy.start()
        waits.append(copy)

    def arrived(d, sem, half=None):
        dst = o_ref.at[d]
        if half is not None:
            dst = dst.at[pl.ds(half * 128, 128)]
        pltpu.make_async_remote_copy(src_ref=dst, dst_ref=dst, send_sem=sz, recv_sem=sem,
                                     device_id=(sib, own), device_id_type=MESH).wait_recv()

    send(dp, sz, rz, anti, p_ref)
    send(dp, sy.at[0], ry.at[0], up, p_ref)
    send(dp, sy.at[1], ry.at[1], down, p_ref)
    send(dp, sc.at[0], rc.at[0], sib, p_ref)
    keep = pltpu.make_async_copy(p_ref, o_ref.at[dp], local)
    keep.start()
    arrived(down, ry.at[0])
    send(down, sh.at[0], rh.at[0], up, half=0)
    send(down, sc.at[1], rc.at[1], sib)
    arrived(up, ry.at[1])
    send(up, sh.at[1], rh.at[1], down, half=1)
    send(up, sc.at[2], rc.at[2], sib)
    arrived(anti, rz)
    send(anti, sy.at[2], ry.at[2], up)
    send(anti, sy.at[3], ry.at[3], down)
    send(anti, sc.at[3], rc.at[3], sib)
    far = other(down) * 0 + lax.rem(y + 2, 4) * 4 + lax.rem(dp, 4)
    arrived(other(down), ry.at[2])
    send(other(down), sh.at[2], rh.at[2], up, half=0)
    send(other(down), sc.at[4], rc.at[4], sib)
    arrived(other(up), ry.at[3])
    send(other(up), sh.at[3], rh.at[3], down, half=1)
    send(other(up), sc.at[5], rc.at[5], sib)
    arrived(far, rh.at[0], half=0)
    arrived(far, rh.at[1], half=1)
    send(far, sc.at[6], rc.at[6], sib)
    arrived(other(far), rh.at[2], half=0)
    arrived(other(far), rh.at[3], half=1)
    send(other(far), sc.at[7], rc.at[7], sib)

    def twin(d):
        return d + 1 - 2 * lax.rem(d, 2)

    for i, d in enumerate((dp, down, up, anti, other(down), other(up), far, other(far))):
        arrived(twin(d), rc.at[i])
    keep.wait()
    for copy in waits:
        copy.wait_send()


def gather(p):
    dma = pltpu.SemaphoreType.DMA
    return pl.pallas_call(
        gather_kernel,
        out_shape=jax.ShapeDtypeStruct((16, 256, 768), jnp.bfloat16),
        in_specs=[pl.BlockSpec(memory_space=pl.ANY)],
        out_specs=pl.BlockSpec(memory_space=pl.ANY),
        scratch_shapes=[dma, dma, dma, dma((4,)), dma((4,)), dma((4,)), dma((4,)), dma((8,)), dma((8,))],
        compiler_params=pltpu.CompilerParams(collective_id=2, has_side_effects=True),
        name="gather",
    )(p)


def flat_kernel(i_ref, o_ref):
    for d in range(16):
        for b in range(2):
            start = (2 * d + b) * GB
            o_ref[:, start:start + GB] = i_ref[d, :, b * 384:b * 384 + GB]


def flatten(slices):
    rows = 64
    return pl.pallas_call(
        flat_kernel,
        out_shape=jax.ShapeDtypeStruct((256, FF), jnp.bfloat16),
        grid=(256 // rows,),
        in_specs=[pl.BlockSpec((16, rows, 768), lambda i: (0, i, 0))],
        out_specs=pl.BlockSpec((rows, FF), lambda i: (i, 0)),
        compiler_params=pltpu.CompilerParams(vmem_limit_bytes=VLIM),
        name="flatten",
    )(slices)


def shards(acts, grads_out, weight_grad):
    a2, g2 = swap(acts, grads_out)
    rows = 2 * acts.shape[0]
    gx, gy, tr = grams(a2.reshape(rows, D // 2), g2.reshape(rows, FF // 2))
    fg, fa, tr = reduce_all(gx, gy, tr)
    w = jnp.pad(weight_grad.reshape(256, 2, GB).transpose(1, 0, 2), ((0, 0), (0, 0), (0, 384 - GB)))
    p = solve(fg.reshape(2, 8 * GROWS, 128), fa.reshape(16 * AROWS, 128), tr, w)
    return flatten(gather(p))


def solution(mesh):
    in_specs = (P(("dp", "owner"), None), P(("dp", "owner"), None), P("owner", "dp"))
    out_specs = P("owner", None)
    return jax.shard_map(shards, mesh=mesh, in_specs=in_specs, out_specs=out_specs, check_vma=False)
```

time: 1120 us -> 361 us (0.32)
  waiting for transfers between devices: 663 us -> 0 us
  Pallas kernels: 0 us -> 360 us
  other arithmetic: 225 us -> 0 us
  local copies, waits for them, and re-layouts: 86.6 us -> 1.01 us
  blocking collectives: 82 us -> 0 us
  matrix products: 37.4 us -> 0 us
  between operations: 16.9 us -> 0.04 us
    pallas_call x0 -> x6, Pallas kernels: none -> 360 us  [the longest x1 128 us: reduce_all(): pl.pallas_call(reduce_kernel, out_shape=(jax.ShapeDtypeStruct((2, 8, GROW...]
    psum x2 -> x0, waiting for transfers between devices: 291 us -> none  [the longest x1 172 us: shards(): own_act = lax.psum(own_act, 'dp')]
    reduce_scatter x2 -> x0, waiting for transfers between devices: 286 us -> none  [the longest x1 240 us: shards(): lax.psum_scatter(grad_part, 'dp', scatter_dimension=0, tiled=True)]
    another operation x30 -> x0, other arithmetic: 218 us -> none  [the longest x20 137 us: damped_inverse(): lower = jnp.linalg.cholesky(blocks + damping * identity)]
    all_gather x1 -> x0, waiting for transfers between devices: 86.6 us -> none  [shards(): return lax.all_gather(result, 'dp', axis=1, tiled=True)]
    psum x2 -> x0, blocking collectives: 82 us -> none  [the longest x1 52.8 us: shards(): grad_trace = lax.psum(trace_of(own_grad), 'dp')]
    div x1 -> x0, local copies, waits for them, and re-layouts: 35.3 us -> none  [shards(): own_grad = own_grad / total]
    dot_general x4 -> x0, matrix products: 25 us -> none  [the longest x2 22.4 us: block_grams(): jnp.einsum('tkb,tkc->kbc', split, split, preferred_element_type=jnp.float32)]
  transfers between devices with their start and end apart: 5 -> 0, of which waited for: 5 -> 0; matrix products, arithmetic and copies ran while one was open for 4% -> 0% of each run, Pallas kernels for 0% -> 0%
where the time goes in v1:
time: 361 us
  Pallas kernels  360 us (100%)
    pallas_call x1, Pallas kernels, reduce_all(): pl.pallas_call(reduce_kernel, out_shape=(jax.ShapeDtypeStruct((2, 8, GROW...  128 us
    pallas_call x1, Pallas kernels, swap(): pl.pallas_call(swap_kernel, out_shape=(jax.ShapeDtypeStruct((2, rows, D /...  104 us
    pallas_call x1, Pallas kernels, solve(): pl.pallas_call(solve_kernel, out_shape=jax.ShapeDtypeStruct((256, 768), j...  66.8 us
    pallas_call x1, Pallas kernels, gather(): pl.pallas_call(gather_kernel, out_shape=jax.ShapeDtypeStruct((16, 256, 76...  42.4 us
    pallas_call x1, Pallas kernels, grams(): pl.pallas_call(gram_kernel, out_shape=(shape, shape, jax.ShapeDtypeStruct...  11.3 us

profile of v1, /device:TPU:33, one launch (start us, length us, event | category | flops | bytes accessed | tf_op | source)
XLA Modules:
  0.0 360.6 jit_solution(9572535197086711240)
XLA Ops:
  0.0 104.3 %swap.1 = (bf16[2,224,2048]{2,1,0:T(8,128)(2,1)}, bf16[2,224,5504]{2,1,0:T(8,128)(2,1)}) custom-call(bf16[224,4096]{1,0:T(8,128)(2,1)} %a_ref.1, bf16[224,11008]{1,0:T(8,128)(2,1)} %g_ref.1), custom_call_target="tpu_custom_call" | custom-call | tf_op jit(solution)/shard_map/swap/pallas_call | solution.py:60
  104.3 11.3 %grams.1 = (f32[16,480,128]{2,1,0:T(8,128)}, f32[16,480,128]{2,1,0:T(8,128)}, f32[16,128]{1,0:T(8,128)}) custom-call(bf16[448,2048]{1,0:T(8,128)(2,1)} %bitcast.7, bf16[448,5504]{1,0:T(8,128)(2,1)} %bitcast.6), custom_call_target="tpu_custom_call" | custom-call | tf_op jit(solution)/shard_map/grams/pallas_call | solution.py:121
  115.7 0.0 copy-start
  115.7 128.0 %reduce_all.1 = (f32[2,8,96,128]{3,2,1,0:T(8,128)}, f32[2,8,24,128]{3,2,1,0:T(8,128)}, f32[16,128]{1,0:T(8,128)}) custom-call(f32[16,480,128]{2,1,0:T(8,128)} %get-tuple-element.15.gx, f32[16,480,128]{2,1,0:T(8,128)} %get-tuple-element.16.gy, f32[16,128]{1,0:T(8,128)} %get-tuple-element.17.tr), custom_call_target="tpu_custom_call" | custom-call | tf_op jit(solution)/shard_map/reduce_all/pallas_call | solution.py:294
  243.7 0.0 copy-done
  243.7 0.2 copy.4
  243.9 0.8 pad.4.w_ref
  244.7 66.8 %solve.1.p_ref = bf16[256,768]{1,0:T(8,128)(2,1)} custom-call(f32[2,768,128]{2,1,0:T(8,128)} %bitcast.9, f32[384,128]{1,0:T(8,128)} %bitcast.11, f32[16,128]{1,0:T(8,128)} %get-tuple-element.20.t_ref, bf16[2,256,384]{2,1,0:T(8,128)(2,1)} %pad.4.w_ref), custom_call_target="tpu_custom_call" | custom-call | tf_op jit(solution)/shard_map/solve/pallas_call | solution.py:433
  311.5 42.4 %gather.1.i_ref = bf16[16,256,768]{2,1,0:T(8,128)(2,1)} custom-call(bf16[256,768]{1,0:T(8,128)(2,1)} %solve.1.p_ref), custom_call_target="tpu_custom_call" | custom-call | tf_op jit(solution)/shard_map/gather/pallas_call | solution.py:524
  353.9 6.7 %flatten.1 = bf16[256,11008]{1,0:T(8,128)(2,1)} custom-call(bf16[16,256,768]{2,1,0:T(8,128)(2,1)} %gather.1.i_ref), custom_call_target="tpu_custom_call" | custom-call | tf_op jit(solution)/shard_map/flatten/pallas_call | solution.py:544
Async XLA Ops:
  115.7 128.0 %copy-start = (bf16[256,688]{0,1:T(8,128)(2,1)S(1)}, bf16[256,688]{0,1:T(8,128)(2,1)}, u32[]{:S(2)}) copy-start(bf16[256,688]{0,1:T(8,128)(2,1)} %param.5) | copy-start | bytes 1056772

commit v2 on v1

--- a/solution.py
+++ b/solution.py
@@ -17,8 +17,8 @@
 MESH = pl.DeviceIdType.MESH
 HIGH = lax.Precision.HIGHEST
 F32 = jnp.float32
-GROWS = 96
-AROWS = 24
+GROWS = 64
+AROWS = 16
 CH = GROWS + AROWS
 HALF = 4 * CH
 VLIM = 56 * 1024 * 1024
@@ -30,28 +30,23 @@
     return dp, own
 
 
-def swap_kernel(a_ref, g_ref, ao_ref, go_ref, local, send, recv):
+def swap_kernel(a_ref, g_ref, ao_ref, go_ref, send, recv):
     dp, own = place()
     core = lax.rem(dp, 2)
     sib = dp + 1 - 2 * core
     barrier = pltpu.get_barrier_semaphore()
     pl.semaphore_signal(barrier, inc=1, device_id=(sib, own), device_id_type=MESH)
     pl.semaphore_wait(barrier, 1)
-    remote = []
-    locals_ = []
+    copies = []
     for i, (src, dst) in enumerate(((a_ref, ao_ref), (g_ref, go_ref))):
-        width = dst.shape[2]
+        width = dst.shape[1]
         theirs = pl.ds(pl.multiple_of((1 - core) * width, 128), width)
-        mine = pl.ds(pl.multiple_of(core * width, 128), width)
         copy = pltpu.make_async_remote_copy(
-            src_ref=src.at[:, theirs], dst_ref=dst.at[1], send_sem=send.at[i], recv_sem=recv.at[i],
+            src_ref=src.at[:, theirs], dst_ref=dst, send_sem=send.at[i], recv_sem=recv.at[i],
             device_id=(sib, own), device_id_type=MESH)
         copy.start()
-        remote.append(copy)
-        keep = pltpu.make_async_copy(src.at[:, mine], dst.at[0], local.at[i])
-        keep.start()
-        locals_.append(keep)
-    for copy in remote + locals_:
+        copies.append(copy)
+    for copy in copies:
         copy.wait()
 
 
@@ -59,11 +54,11 @@
     rows = acts.shape[0]
     return pl.pallas_call(
         swap_kernel,
-        out_shape=(jax.ShapeDtypeStruct((2, rows, D // 2), acts.dtype),
-                   jax.ShapeDtypeStruct((2, rows, FF // 2), acts.dtype)),
+        out_shape=(jax.ShapeDtypeStruct((rows, D // 2), acts.dtype),
+                   jax.ShapeDtypeStruct((rows, FF // 2), acts.dtype)),
         in_specs=[pl.BlockSpec(memory_space=pl.ANY)] * 2,
         out_specs=(pl.BlockSpec(memory_space=pl.ANY),) * 2,
-        scratch_shapes=[pltpu.SemaphoreType.DMA((2,))] * 3,
+        scratch_shapes=[pltpu.SemaphoreType.DMA((2,))] * 2,
         compiler_params=pltpu.CompilerParams(collective_id=0, has_side_effects=True),
         name="swap",
     )(acts, grads)
@@ -73,63 +68,92 @@
     return lax.dot_general(block, block, (((0,), (0,)), ((), ())), preferred_element_type=F32)
 
 
-def gram_kernel(a_ref, g_ref, x_ref, y_ref, t_ref):
-    def store(j, rows, start, value):
-        chunk = start // CH
+def gram_kernel(a_ref, g_ref, as_ref, gs_ref, x_ref, y_ref, t_ref, abuf, gbuf, sems):
+    core = lax.rem(lax.axis_index("dp"), 2)
+    rows = a_ref.shape[0]
+    cut = 22 * 128
+    copies = []
+    for i, (whole, other, buf, lo, hi) in enumerate((
+            (a_ref, as_ref, abuf, 0, D // 2), (g_ref, gs_ref, gbuf, 0, cut), (g_ref, gs_ref, gbuf, cut, FF // 2))):
+        mine = whole.at[:, pl.ds(pl.multiple_of(core * buf.shape[1] + lo, 128), hi - lo)]
+        here = pltpu.make_async_copy(mine, buf.at[pl.ds(0, rows), pl.ds(lo, hi - lo)], sems.at[2 * i])
+        there = pltpu.make_async_copy(other.at[:, pl.ds(lo, hi - lo)],
+                                      buf.at[pl.ds(rows, rows), pl.ds(lo, hi - lo)], sems.at[2 * i + 1])
+        here.start()
+        there.start()
+        copies.append((here, there))
+
+    def store(j, start, value):
         px, py = j // 4, j % 4
-        if chunk < 4:
-            x_ref[px * 4 + py, pl.ds(start, rows), :] = value
+        at = pl.ds(start % HALF, value.shape[0])
+        if start < HALF:
+            x_ref[px * 4 + py, at, :] = value
         else:
-            y_ref[py * 4 + px, pl.ds(start - HALF, rows), :] = value
-
-    zero = jnp.zeros((128, 128), F32)
-    grad_sum = jnp.zeros((8, 128), F32)
-    act_sum = jnp.zeros((8, 128), F32)
-    eye = (lax.broadcasted_iota(jnp.int32, (128, 128), 0)
-           == lax.broadcasted_iota(jnp.int32, (128, 128), 1))
+            y_ref[py * 4 + px, at, :] = value
+
+    def store_all(j, size, lead, row, value):
+        done = 0
+        while done < value.shape[0]:
+            at = row + done
+            n = min(size - at % size, value.shape[0] - done)
+            store(j, (at // size) * CH + lead + at % size, value[done:done + n])
+            done += n
+
+    r = lax.broadcasted_iota(jnp.int32, (128, 128), 0)
+    c = lax.broadcasted_iota(jnp.int32, (128, 128), 1)
 
     def diag(tile):
-        return jnp.sum(jnp.where(eye, tile, 0.0).reshape(16, 8, 128), axis=0)
-
+        return jnp.sum(jnp.where(r == c, tile, 0.0), axis=0, keepdims=True)
+
+    act_sum = jnp.zeros((1, 128), F32)
+    grad_sum = jnp.zeros((1, 128), F32)
+    for copy in copies[0]:
+        copy.wait()
+    for k in range(8):
+        g = gram(abuf[:, k * AB:(k + 1) * AB])
+        t0, t2 = g[0:128, 0:128], g[128:256, 128:256]
+        second = diag(t2)
+        act_sum += diag(t0) + second
+        t_ref[8 + k:9 + k, :] = second
+        store_all(2 * k, AROWS, GROWS, 0, g[128:256, 0:128])
+        store_all(2 * k + 1, AROWS, GROWS, 0, jnp.where(r >= c, t0, t2))
     for j in range(16):
-        g = gram(g_ref[:, j * GB:(j + 1) * GB])
-        low = jnp.concatenate([g[256:344, :], jnp.zeros((40, GB), F32)], axis=0)
-        low2 = jnp.concatenate([low[:, 256:344], jnp.zeros((128, 40), F32)], axis=1)
-        tiles = [g[0:128, 0:128], g[128:256, 0:128], g[128:256, 128:256], low[:, 0:128], low[:, 128:256], low2]
-        grad_sum += diag(tiles[0]) + diag(tiles[2]) + diag(tiles[5])
-        for u in range(24):
-            start = (u // 3) * CH + (u % 3) * 32
-            r = (u % 4) * 32
-            store(j, 32, start, tiles[u // 4][r:r + 32])
-    for k in range(8):
-        g = gram(a_ref[:, k * AB:(k + 1) * AB])
-        tiles = [g[0:128, 0:128], g[128:256, 0:128], g[128:256, 128:256]]
-        act_sum += diag(tiles[0]) + diag(tiles[2])
-        for u in range(48):
-            j = 2 * k + u // 24
-            v = u % 24
-            start = (v // 3) * CH + GROWS + (v % 3) * 8
-            r = (u % 16) * 8
-            store(j, 8, start, tiles[u // 16][r:r + 8])
-    t_ref[0:8, :] = act_sum
-    t_ref[8:16, :] = grad_sum
-
-
-def grams(acts, grads):
+        if j in (0, 8):
+            for copy in copies[1 + j // 8]:
+                copy.wait()
+        g = gram(gbuf[:, j * GB:(j + 1) * GB])
+        t0, t2 = g[0:128, 0:128], g[128:256, 128:256]
+        t5 = jnp.concatenate([g[256:344, 256:344], jnp.zeros((88, 40), F32)], axis=1)
+        second = diag(t2)
+        grad_sum += diag(t0) + second + jnp.sum(jnp.where(r[:88] == c[:88], t5, 0.0), axis=0, keepdims=True)
+        tail = jnp.concatenate([pltpu.roll(t5[48:88], 40, 1), jnp.zeros((8, 128), F32)], axis=0)
+        store_all(j, GROWS, 0, 0, g[128:256, 0:128])
+        store_all(j, GROWS, 0, 128, jnp.where(r >= c, t0, t2))
+        store_all(j, GROWS, 0, 256, g[256:344, 0:128])
+        store_all(j, GROWS, 0, 344, g[256:344, 128:256])
+        store_all(j, GROWS, 0, 432, jnp.where(c[:48] < 88, t5[0:48], tail))
+        store_all(j, GROWS, 0, 480, jnp.concatenate([second, jnp.zeros((31, 128), F32)], axis=0))
+    t_ref[0:8, :] = jnp.concatenate([act_sum, grad_sum, jnp.zeros((6, 128), F32)], axis=0)
+
+
+def grams(acts, grads, sib_acts, sib_grads):
     shape = jax.ShapeDtypeStruct((16, HALF, 128), F32)
     vmem = pl.BlockSpec(memory_space=pltpu.VMEM)
+    rows = acts.shape[0]
     return pl.pallas_call(
         gram_kernel,
         out_shape=(shape, shape, jax.ShapeDtypeStruct((16, 128), F32)),
-        in_specs=[vmem] * 2,
+        in_specs=[pl.BlockSpec(memory_space=pl.ANY)] * 4,
         out_specs=(vmem,) * 3,
+        scratch_shapes=[pltpu.VMEM((2 * rows, D // 2), acts.dtype), pltpu.VMEM((2 * rows, FF // 2), acts.dtype),
+                        pltpu.SemaphoreType.DMA((6,))],
         compiler_params=pltpu.CompilerParams(vmem_limit_bytes=VLIM),
         name="grams",
-    )(acts, grads)
+    )(acts, grads, sib_acts, sib_grads)
 
 
 def reduce_kernel(gx, gy, tr, fg_out, fa_out, t_out,
-                  sx, sy, rx, ry, rx2, ry2, st, rz, fin, fg, fa, t1, t2, t3, q1, q2, q3, q4,
+                  sx, sy, rx, ry, rx2, ry2, st, rz, fin, fg, fa, t1, t2, t3, q1, q2, q3, q4, tt,
                   local, s1, r1, s2, r2, s3, r3, sg, rg, sa, ra, s4, r4):
     dp, own = place()
     core = lax.rem(dp, 2)
@@ -284,7 +308,10 @@
     side.wait()
     fg_out[...] = fg[...]
     fa_out[...] = fa[...]
-    t_out[...] = t3[...] + q4[...]
+    tt[core] = t3[...]
+    tt[1 - core] = q4[...]
+    t_out[0:8, :] = tt[0, 0:8, :] + tt[1, 0:8, :]
+    t_out[8:16, :] = jnp.broadcast_to(tt[own // 8, pl.ds(8 + lax.rem(own, 8), 1), :], (8, 128))
 
 
 def reduce_all(gx, gy, tr):
@@ -305,7 +332,7 @@
             pltpu.VMEM((8, CH, 128), F32), pltpu.VMEM((7, CH, 128), F32), pltpu.VMEM((CH, 128), F32),
             pltpu.VMEM((2, 8, GROWS, 128), F32), pltpu.VMEM((2, 8, AROWS, 128), F32),
             tile, tile, tile,
-            pltpu.VMEM((3, 16, 128), F32), pltpu.VMEM((3, 16, 128), F32), pltpu.VMEM((7, 16, 128), F32), tile,
+            pltpu.VMEM((3, 16, 128), F32), pltpu.VMEM((3, 16, 128), F32), pltpu.VMEM((7, 16, 128), F32), tile, pltpu.VMEM((2, 16, 128), F32),
             dma((2,)), dma((9,)), dma((9,)), dma((9,)), dma((9,)), dma((14,)), dma((14,)),
             dma((16,)), dma((16,)), dma((16,)), dma((16,)), dma, dma,
         ],
@@ -318,61 +345,109 @@
     return lax.dot_general(a, b, (((ca,), (cb,)), ((), ())), precision=HIGH, preferred_element_type=F32)
 
 
+def split(v):
+    high = v.astype(jnp.bfloat16).astype(F32)
+    rest = v - high
+    mid = rest.astype(jnp.bfloat16).astype(F32)
+    return high, mid, rest - mid
+
+
+def outer(a, b):
+    ah, am, al = split(a)
+    bh, bm, bl = split(b)
+    left = jnp.concatenate([ah, ah, am, ah, am, al], axis=0).astype(jnp.bfloat16)
+    right = jnp.concatenate([bh, bm, bh, bl, bm, bh], axis=0).astype(jnp.bfloat16)
+    return lax.dot_general(left, right, (((0,), (0,)), ((), ())), preferred_element_type=F32)
+
+
+def sweep_four(now, at, row, sub, lane):
+    def full(v):
+        return jnp.broadcast_to(v, (8, 128))
+
+    four = range(4)
+    cols = [full(now[:, at + i:at + i + 1]) for i in four]
+    rows = [full(now[row + i:row + i + 1, :]) for i in four]
+    m = {(i, j): full(cols[j][row + i:row + i + 1, :]) for i in four for j in range(i + 1)}
+    for p in four:
+        inv = 1.0 / m[(p, p)]
+        line = {i: m[(max(i, p), min(i, p))] * inv for i in four if i != p}
+        new = {}
+        for i in four:
+            for j in range(i + 1):
+                if i == p and j == p:
+                    new[(i, j)] = -inv
+                elif i == p:
+                    new[(i, j)] = line[j]
+                elif j == p:
+                    new[(i, j)] = line[i]
+                else:
+                    new[(i, j)] = m[(i, j)] - m[(max(i, p), min(i, p))] * line[j]
+        m = new
+    in_rows = jnp.logical_and(sub >= row, sub < row + 4)
+    in_cols = jnp.logical_and(lane >= at, lane < at + 4)
+    out = jnp.where(jnp.logical_or(in_rows, in_cols), 0.0, now)
+    rows = [jnp.where(in_cols, jnp.where(lane == at + i, -1.0, 0.0), rows[i]) for i in four]
+    for i in four:
+        col = jnp.where(in_rows, jnp.where(sub == row + i, -1.0, 0.0), cols[i])
+        term = m[(i, 0)] * rows[0]
+        for j in range(1, 4):
+            term = term + m[(max(i, j), min(i, j))] * rows[j]
+        out = out + col * term
+    return out
+
+
 def sweep_tiles(refs, panels):
     sub = lax.broadcasted_iota(jnp.int32, (8, 128), 0)
     lane = lax.broadcasted_iota(jnp.int32, (8, 128), 1)
     lane_all = lax.broadcasted_iota(jnp.int32, (128, 128), 1)
-
-    def panel(p, _):
-        base = pl.multiple_of(p * 8, 8)
-        rows = pl.ds(base, 8)
-        back = lax.rem(128 - base, 128)
-        olds = [ref[rows, :] for ref in refs]
-        news = [pltpu.roll(old, back, 1) for old in olds]
-        for s in range(8):
-            for i, now in enumerate(news):
-                col = jnp.broadcast_to(now[:, s:s + 1], (8, 128))
-                row = jnp.broadcast_to(now[s:s + 1, :], (8, 128))
-                inv = 1.0 / jnp.broadcast_to(col[s:s + 1, :], (8, 128))
-                col = jnp.where(sub == s, -1.0, col)
-                row = jnp.where(lane == s, -1.0, row)
-                keep = jnp.where(jnp.logical_or(sub == s, lane == s), 0.0, now)
-                news[i] = keep - col * (row * inv)
+    for p in range(panels):
+        base = 8 * p
         inside = jnp.logical_and(lane_all >= base, lane_all < base + 8)
+        olds = [ref[base:base + 8, :] for ref in refs]
+        news = [sweep_four(old, base, 0, sub, lane) for old in olds]
+        news = [sweep_four(new, base + 4, 4, sub, lane) for new in news]
         for ref, old, new in zip(refs, olds, news):
-            new = pltpu.roll(new, base, 1)
-            ref[...] = jnp.where(inside, 0.0, ref[...]) - dot(old, new, 0, 0)
-            ref[rows, :] = new
-        return 0
-
-    lax.fori_loop(0, panels, panel, 0)
+            ref[...] = jnp.where(inside, 0.0, ref[...]) - outer(old, new)
+            ref[base:base + 8, :] = new
 
 
 def solve_kernel(fg_ref, fa_ref, t_ref, w_ref, p_ref, g_ref, a_ref, gi_ref, ai_ref):
-    act_trace = jnp.sum(t_ref[0:8, :], keepdims=True) / TOKENS
-    grad_trace = jnp.sum(t_ref[8:16, :], keepdims=True) / TOKENS
+    act_trace = jnp.sum(t_ref[0:1, :], keepdims=True) / TOKENS
+    grad_trace = jnp.sum(t_ref[1:2, :], keepdims=True) / TOKENS
     ratio = jnp.sqrt(act_trace / D / (grad_trace / FF))
     act_damp = ratio * DAMP
     grad_damp = DAMP / ratio
     r = lax.broadcasted_iota(jnp.int32, (128, 128), 0)
     c = lax.broadcasted_iota(jnp.int32, (128, 128), 1)
-    eye = jnp.where(r == c, 1.0, 0.0)
     last = GB - 256
+
+    def pair(both, second):
+        turned = both.T
+        first = jnp.where(r >= c, both, turned)
+        other = jnp.where(r < c, both, jnp.where(r == c, jnp.broadcast_to(second, (128, 128)), turned))
+        return first, other
+
+    def damped(tile, damp):
+        return tile / TOKENS + jnp.where(r == c, damp, 0.0)
+
+    zeros = jnp.zeros((128 - last, 128), F32)
     for b in range(2):
-        for t in range(6):
-            tile = fg_ref[b, t * 128:(t + 1) * 128, :] / TOKENS
-            if t in (0, 2):
-                tile = tile + grad_damp * eye
-            if t in (3, 4):
-                tile = jnp.where(r < last, tile, 0.0)
-            if t == 5:
-                tile = jnp.where(jnp.logical_and(r < last, c < last), tile + grad_damp * eye, eye)
-            g_ref[b * 6 + t] = tile
-    for t in range(3):
-        tile = fa_ref[t * 128:(t + 1) * 128, :] / TOKENS
-        if t != 1:
-            tile = tile + act_damp * eye
-        a_ref[t] = tile
+        first, second = pair(fg_ref[b, 128:256, :], fg_ref[b, 480:481, :])
+        g_ref[b * 6] = damped(first, grad_damp)
+        g_ref[b * 6 + 1] = fg_ref[b, 0:128, :] / TOKENS
+        g_ref[b * 6 + 2] = damped(second, grad_damp)
+        g_ref[b * 6 + 3] = jnp.concatenate([fg_ref[b, 256:344, :] / TOKENS, zeros], axis=0)
+        g_ref[b * 6 + 4] = jnp.concatenate([fg_ref[b, 344:432, :] / TOKENS, zeros], axis=0)
+        packed = fg_ref[b, 432:480, :]
+        low = pltpu.roll(packed[0:40], 88, 1)
+        upper = jnp.concatenate([packed, low, jnp.zeros((40, 128), F32)], axis=0)
+        corner = jnp.where(jnp.logical_and(r >= 48, c < 48), upper.T, upper)
+        inside = jnp.logical_and(r < last, c < last)
+        g_ref[b * 6 + 5] = jnp.where(inside, damped(corner, grad_damp), jnp.where(r == c, 1.0, 0.0))
+    first, second = pair(fa_ref[128:256, :], t_ref[8:9, :])
+    a_ref[0] = damped(first, act_damp)
+    a_ref[1] = fa_ref[0:128, :] / TOKENS
+    a_ref[2] = damped(second, act_damp)
     gs = [[g_ref.at[b * 6 + t] for t in range(6)] for b in range(2)]
     am = [a_ref.at[t] for t in range(3)]
     sweep_tiles([gs[0][0], gs[1][0], am[0]], 16)
@@ -553,9 +628,8 @@
 
 
 def shards(acts, grads_out, weight_grad):
-    a2, g2 = swap(acts, grads_out)
-    rows = 2 * acts.shape[0]
-    gx, gy, tr = grams(a2.reshape(rows, D // 2), g2.reshape(rows, FF // 2))
+    sib_acts, sib_grads = swap(acts, grads_out)
+    gx, gy, tr = grams(acts, grads_out, sib_acts, sib_grads)
     fg, fa, tr = reduce_all(gx, gy, tr)
     w = jnp.pad(weight_grad.reshape(256, 2, GB).transpose(1, 0, 2), ((0, 0), (0, 0), (0, 384 - GB)))
     p = solve(fg.reshape(2, 8 * GROWS, 128), fa.reshape(16 * AROWS, 128), tr, w)

time: 361 us -> 192 us (0.53)
  Pallas kernels: 360 us -> 189 us
    pallas_call x1, Pallas kernels: 104 us -> 6.68 us  [swap(): pl.pallas_call(swap_kernel, out_shape=(jax.ShapeDtypeStruct((rows, D // 2...]
    pallas_call x1, Pallas kernels: 66.8 us -> 28.1 us  [solve(): pl.pallas_call(solve_kernel, out_shape=jax.ShapeDtypeStruct((256, 768), j...]
    pallas_call x1, Pallas kernels: 128 us -> 95.2 us  [reduce_all(): pl.pallas_call(reduce_kernel, out_shape=(jax.ShapeDtypeStruct((2, 8, GROW...]
where the time goes in v2:
time: 192 us; the launch traced here: 191 us
  Pallas kernels  189 us (98%)
  local copies, waits for them, and re-layouts  1.98 us (1%)
    pallas_call x1, Pallas kernels, reduce_all(): pl.pallas_call(reduce_kernel, out_shape=(jax.ShapeDtypeStruct((2, 8, GROW...  95.2 us
    pallas_call x1, Pallas kernels, gather(): pl.pallas_call(gather_kernel, out_shape=jax.ShapeDtypeStruct((16, 256, 76...  42.4 us
    pallas_call x1, Pallas kernels, solve(): pl.pallas_call(solve_kernel, out_shape=jax.ShapeDtypeStruct((256, 768), j...  28.1 us
    pallas_call x1, Pallas kernels, grams(): pl.pallas_call(gram_kernel, out_shape=(shape, shape, jax.ShapeDtypeStruct...  10.2 us
    pallas_call x1, Pallas kernels, flatten(): pl.pallas_call(flat_kernel, out_shape=jax.ShapeDtypeStruct((256, FF), jnp...  6.68 us
    pallas_call x1, Pallas kernels, swap(): pl.pallas_call(swap_kernel, out_shape=(jax.ShapeDtypeStruct((rows, D // 2...  6.68 us

profile of v2, /device:TPU:33, one launch (start us, length us, event | category | flops | bytes accessed | tf_op | source)
XLA Modules:
  0.0 191.4 jit_solution(3493914015999139522)
XLA Ops:
  0.0 1.2 copy.4
  1.2 0.8 pad.4.w_ref
  2.0 6.7 %swap.1 = (bf16[224,2048]{1,0:T(8,128)(2,1)}, bf16[224,5504]{1,0:T(8,128)(2,1)}) custom-call(bf16[224,4096]{1,0:T(8,128)(2,1)} %a_ref.3, bf16[224,11008]{1,0:T(8,128)(2,1)} %g_ref.3), custom_call_target="tpu_custom_call" | custom-call | tf_op jit(solution)/shard_map/swap/pallas_call | solution.py:55
  8.7 10.2 %grams.1 = (f32[16,320,128]{2,1,0:T(8,128)}, f32[16,320,128]{2,1,0:T(8,128)}, f32[16,128]{1,0:T(8,128)}) custom-call(bf16[224,4096]{1,0:T(8,128)(2,1)} %a_ref.3, bf16[224,11008]{1,0:T(8,128)(2,1)} %g_ref.3, bf16[224,2048]{1,0:T(8,128)(2,1)} %get-tuple-element.13.as_ref, bf16[224,5504]{1,0:T(8,128)(2,1)} %get-tuple-element.14.gs_ref), custom_call_target="tpu_custom_call" | custom-call | tf_op jit(solution)/shard_map/grams/pallas_call | solution.py:143
  18.9 95.2 %reduce_all.1 = (f32[2,8,64,128]{3,2,1,0:T(8,128)}, f32[2,8,16,128]{3,2,1,0:T(8,128)}, f32[16,128]{1,0:T(8,128)}) custom-call(f32[16,320,128]{2,1,0:T(8,128)} %get-tuple-element.15.gx, f32[16,320,128]{2,1,0:T(8,128)} %get-tuple-element.16.gy, f32[16,128]{1,0:T(8,128)} %get-tuple-element.17.tr), custom_call_target="tpu_custom_call" | custom-call | tf_op jit(solution)/shard_map/reduce_all/pallas_call | solution.py:321
  114.1 28.1 %solve.1.p_ref = bf16[256,768]{1,0:T(8,128)(2,1)} custom-call(f32[2,512,128]{2,1,0:T(8,128)} %bitcast.5, f32[256,128]{1,0:T(8,128)} %bitcast.7, f32[16,128]{1,0:T(8,128)} %get-tuple-element.20.t_ref, bf16[2,256,384]{2,1,0:T(8,128)(2,1)} %pad.4.w_ref), custom_call_target="tpu_custom_call" | custom-call | tf_op jit(solution)/shard_map/solve/pallas_call | solution.py:508
  142.3 42.4 %gather.1.i_ref = bf16[16,256,768]{2,1,0:T(8,128)(2,1)} custom-call(bf16[256,768]{1,0:T(8,128)(2,1)} %solve.1.p_ref), custom_call_target="tpu_custom_call" | custom-call | tf_op jit(solution)/shard_map/gather/pallas_call | solution.py:599
  184.7 6.7 %flatten.1 = bf16[256,11008]{1,0:T(8,128)(2,1)} custom-call(bf16[16,256,768]{2,1,0:T(8,128)(2,1)} %gather.1.i_ref), custom_call_target="tpu_custom_call" | custom-call | tf_op jit(solution)/shard_map/flatten/pallas_call | solution.py:619

commit v3 on v2

--- a/solution.py
+++ b/solution.py
@@ -17,11 +17,18 @@
 MESH = pl.DeviceIdType.MESH
 HIGH = lax.Precision.HIGHEST
 F32 = jnp.float32
-GROWS = 64
-AROWS = 16
+NB = 2
+GROWS = 64 // NB
+AROWS = 16 // NB
 CH = GROWS + AROWS
 HALF = 4 * CH
 VLIM = 56 * 1024 * 1024
+
+
+def position(j):
+    x = 2 * (j // 2 % 2) + (j // 4 + j // 8) % 2
+    y = 2 * (j % 2) + j // 8
+    return x, y
 
 
 def place():
@@ -68,7 +75,7 @@
     return lax.dot_general(block, block, (((0,), (0,)), ((), ())), preferred_element_type=F32)
 
 
-def gram_kernel(a_ref, g_ref, as_ref, gs_ref, x_ref, y_ref, t_ref, abuf, gbuf, sems):
+def gram_kernel(a_ref, g_ref, as_ref, gs_ref, x_out, y_out, t_ref, abuf, gbuf, x_ref, y_ref, sems, out_sems):
     core = lax.rem(lax.axis_index("dp"), 2)
     rows = a_ref.shape[0]
     cut = 22 * 128
@@ -83,21 +90,28 @@
         there.start()
         copies.append((here, there))
 
-    def store(j, start, value):
-        px, py = j // 4, j % 4
-        at = pl.ds(start % HALF, value.shape[0])
-        if start < HALF:
-            x_ref[px * 4 + py, at, :] = value
-        else:
-            y_ref[py * 4 + px, at, :] = value
-
     def store_all(j, size, lead, row, value):
+        px, py = position(j)
         done = 0
         while done < value.shape[0]:
             at = row + done
             n = min(size - at % size, value.shape[0] - done)
-            store(j, (at // size) * CH + lead + at % size, value[done:done + n])
+            chunk, batch = at // size // NB, at // size % NB
+            rows_at = pl.ds(chunk % 4 * CH + lead + at % size, n)
+            if chunk < 4:
+                x_ref[batch, px * 4 + py, rows_at, :] = value[done:done + n]
+            else:
+                y_ref[batch, py * 4 + px, rows_at, :] = value[done:done + n]
             done += n
+
+    outs = []
+
+    def finish(j):
+        px, py = position(j)
+        for i, (src, dst, at) in enumerate(((x_ref, x_out, px * 4 + py), (y_ref, y_out, py * 4 + px))):
+            copy = pltpu.make_async_copy(src.at[:, at], dst.at[:, at], out_sems.at[i, j])
+            copy.start()
+            outs.append(copy)
 
     r = lax.broadcasted_iota(jnp.int32, (128, 128), 0)
     c = lax.broadcasted_iota(jnp.int32, (128, 128), 1)
@@ -133,28 +147,33 @@
         store_all(j, GROWS, 0, 344, g[256:344, 128:256])
         store_all(j, GROWS, 0, 432, jnp.where(c[:48] < 88, t5[0:48], tail))
         store_all(j, GROWS, 0, 480, jnp.concatenate([second, jnp.zeros((31, 128), F32)], axis=0))
+        finish(j)
     t_ref[0:8, :] = jnp.concatenate([act_sum, grad_sum, jnp.zeros((6, 128), F32)], axis=0)
+    for copy in outs:
+        copy.wait()
 
 
 def grams(acts, grads, sib_acts, sib_grads):
-    shape = jax.ShapeDtypeStruct((16, HALF, 128), F32)
+    shape = jax.ShapeDtypeStruct((NB, 16, HALF, 128), F32)
     vmem = pl.BlockSpec(memory_space=pltpu.VMEM)
+    anywhere = pl.BlockSpec(memory_space=pl.ANY)
     rows = acts.shape[0]
     return pl.pallas_call(
         gram_kernel,
         out_shape=(shape, shape, jax.ShapeDtypeStruct((16, 128), F32)),
-        in_specs=[pl.BlockSpec(memory_space=pl.ANY)] * 4,
-        out_specs=(vmem,) * 3,
+        in_specs=[anywhere] * 4,
+        out_specs=(anywhere, anywhere, vmem),
         scratch_shapes=[pltpu.VMEM((2 * rows, D // 2), acts.dtype), pltpu.VMEM((2 * rows, FF // 2), acts.dtype),
-                        pltpu.SemaphoreType.DMA((6,))],
+                        pltpu.VMEM(shape.shape, F32), pltpu.VMEM(shape.shape, F32),
+                        pltpu.SemaphoreType.DMA((6,)), pltpu.SemaphoreType.DMA((2, 16))],
         compiler_params=pltpu.CompilerParams(vmem_limit_bytes=VLIM),
         name="grams",
     )(acts, grads, sib_acts, sib_grads)
 
 
 def reduce_kernel(gx, gy, tr, fg_out, fa_out, t_out,
-                  sx, sy, rx, ry, rx2, ry2, st, rz, fin, fg, fa, t1, t2, t3, q1, q2, q3, q4, tt,
-                  local, s1, r1, s2, r2, s3, r3, sg, rg, sa, ra, s4, r4):
+                  ps, pk, pm, pr, rx2, ry2, st, rz, fin, ga, aa, fg, fa, t1, t2, t3, q1, q2, q3, q4, tt,
+                  local, s1, r1, s2, r2, s3, r3, s4, rg4, ra4, s5, rg5, ra5, ts, tr_sem):
     dp, own = place()
     core = lax.rem(dp, 2)
     zh = lax.rem(dp // 2, 2)
@@ -170,9 +189,17 @@
     xs = [at(lax.rem(x + k, 4), y, z, core) for k in (1, 2, 3)]
     ys = [at(x, lax.rem(y + k, 4), z, core) for k in (1, 2, 3)]
     zs = [at(x, y, lax.rem(z + k, 8), core) for k in range(1, 8)]
-    j = x * 4 + y
+    j = 8 * (y % 2) + 4 * ((x + y) % 2) + 2 * (x // 2) + y // 2
     unit = core * 8 + j // 2
     part = lax.rem(j, 2)
+    unit_zh = lax.rem(unit // 2, 2)
+    unit_zl = unit // 4
+    g_on = zh == unit_zh
+    a_on = zl == unit_zl
+    g_to = [(unit, zl * 4 + lax.rem(x + k, 4)) for k in range(4)]
+    a_to = [((lax.rem(y + k // 2, 4) * 2 + zh) * 2 + lax.rem(core + k, 2), unit) for k in range(8)]
+    g_self = unit == dp
+    a_self = unit == own
 
     barrier = pltpu.get_barrier_semaphore()
 
@@ -181,160 +208,239 @@
 
     for device in xs + ys + zs + [(sib, own)]:
         greet(device)
-
-    def greet_sources(base):
-        def body(i, _):
-            js = lax.rem(base, 8) * 2 + i // 8
-            device = at(js // 4, lax.rem(js, 4), lax.rem(i, 8), base // 8)
-
-            @pl.when(jnp.logical_or(device[0] != dp, device[1] != own))
+    for base in (dp, own):
+        for i in range(2):
+            js = lax.rem(base, 8) * 2 + i
+            source = at(*position(js), z, base // 8)
+
+            @pl.when(jnp.logical_or(source[0] != dp, source[1] != own))
             def _():
-                greet(device)
-            return 0
-        lax.fori_loop(0, 16, body, 0)
-
-    greet_sources(dp)
-    greet_sources(own)
-    self_g = jnp.where(unit == dp, 1, 0)
-    self_a = jnp.where(unit == own, 1, 0)
-    pl.semaphore_wait(barrier, 14 + 32 - self_g - self_a)
-
-    def send(src, dst, ssem, rsem, device):
-        copy = pltpu.make_async_remote_copy(src_ref=src, dst_ref=dst, send_sem=ssem, recv_sem=rsem,
+                greet(source)
+    g_count = jnp.where(g_on, 4 - jnp.where(g_self, 1, 0), 0)
+    a_count = jnp.where(a_on, 8 - jnp.where(a_self, 1, 0), 0)
+    pl.semaphore_wait(barrier, 14 + g_count + a_count)
+
+    def remote(src, dst, ssem, rsem, device):
+        return pltpu.make_async_remote_copy(src_ref=src, dst_ref=dst, send_sem=ssem, recv_sem=rsem,
                                             device_id=device, device_id_type=MESH)
-        copy.start()
-        return copy
-
-    copies = []
-    for k in range(3):
-        copies.append(send(gx.at[pl.ds(lax.rem(x + k + 1, 4) * 4, 4)], rx.at[k], s1.at[k], r1.at[k], xs[k]))
-        copies.append(send(gy.at[pl.ds(lax.rem(y + k + 1, 4) * 4, 4)], ry.at[k], s1.at[3 + k], r1.at[3 + k], ys[k]))
-        copies.append(send(tr, q1.at[k], s1.at[6 + k], r1.at[6 + k], xs[k]))
-    copies.append(pltpu.make_async_copy(gx.at[pl.ds(x * 4, 4)], sx, local.at[0]))
-    copies[-1].start()
-    copies.append(pltpu.make_async_copy(gy.at[pl.ds(y * 4, 4)], sy, local.at[1]))
-    copies[-1].start()
-    for copy in copies:
-        copy.wait()
-
-    @pl.loop(0, 16)
-    def _(i):
-        a = i // 4
-        rows = pl.ds(pl.multiple_of(lax.rem(i, 4) * CH, 8), CH)
-        sx[a, rows, :] = (sx[a, rows, :] + rx[0, a, rows, :]) + (rx[1, a, rows, :] + rx[2, a, rows, :])
-        sy[a, rows, :] = (sy[a, rows, :] + ry[0, a, rows, :]) + (ry[1, a, rows, :] + ry[2, a, rows, :])
+
+    def begin(copies):
+        for copy in copies:
+            copy.start()
+        return copies
+
+    def end(copies):
+        for copy in copies:
+            copy.wait()
+
+    axes = ((0, gx, x, (xs[0], xs[2])), (1, gy, y, (ys[0], ys[2])))
+
+    def plane(b):
+        copies = []
+        for a, g, me, (up, down) in axes:
+            over, under, opposite = lax.rem(me + 1, 4) * 4, lax.rem(me + 3, 4) * 4, lax.rem(me + 2, 4) * 4
+            copies.append(remote(g.at[b, pl.ds(opposite, 2)], pm.at[a, b, 0], s1.at[a, b, 0], r1.at[a, b, 0], up))
+            copies.append(remote(g.at[b, pl.ds(opposite + 2, 2)], pm.at[a, b, 1],
+                                 s1.at[a, b, 1], r1.at[a, b, 1], down))
+            copies.append(pltpu.make_async_copy(g.at[b, pl.ds(over, 2)], pk.at[a, b, 0], local.at[a, b, 0]))
+            copies.append(pltpu.make_async_copy(g.at[b, pl.ds(under + 2, 2)], pk.at[a, b, 1], local.at[a, b, 1]))
+        for a, g, me, (up, down) in axes:
+            over, under = lax.rem(me + 1, 4) * 4, lax.rem(me + 3, 4) * 4
+            copies.append(remote(g.at[b, pl.ds(over + 2, 2)], pr.at[a, b, 0, pl.ds(2, 2)],
+                                 s1.at[a, b, 2], r1.at[a, b, 2], up))
+            copies.append(remote(g.at[b, pl.ds(under, 2)], pr.at[a, b, 1, pl.ds(0, 2)],
+                                 s1.at[a, b, 3], r1.at[a, b, 3], down))
+            copies.append(pltpu.make_async_copy(g.at[b, pl.ds(me * 4, 4)], ps.at[a, b], local.at[a, b, 2]))
+        return begin(copies)
+
+    def plane_pass(b, copies):
+        end(copies[:8])
+        @pl.loop(0, 8)
+        def _(i):
+            h, rows = i // 4, pl.ds(pl.multiple_of(lax.rem(i, 4) * CH, 8), CH)
+            for a in range(2):
+                for d in range(2):
+                    pk[a, b, d, h, rows, :] += pm[a, b, d, h, rows, :]
+        for a, _, _, to in axes:
+            for d in range(2):
+                copies.append(remote(pk.at[a, b, d], pr.at[a, b, d, pl.ds(2 * d, 2)],
+                                     s1.at[a, b, 4 + d], r1.at[a, b, 4 + d], to[d]))
+                copies[-1].start()
+
+    def plane_sum(b, copies):
+        end(copies[8:])
+        @pl.loop(0, 16)
+        def _(i):
+            q, rows = i // 4, pl.ds(pl.multiple_of(lax.rem(i, 4) * CH, 8), CH)
+            for a in range(2):
+                ps[a, b, q, rows, :] += pr[a, b, 0, q, rows, :] + pr[a, b, 1, q, rows, :]
+
+    def cross(b):
+        copies = []
+        for k in range(3):
+            copies.append(remote(ps.at[0, b, lax.rem(y + k + 1, 4)], rx2.at[b, k], s2.at[b, k], r2.at[b, k], ys[k]))
+            copies.append(remote(ps.at[1, b, lax.rem(x + k + 1, 4)], ry2.at[b, k],
+                                 s2.at[b, 3 + k], r2.at[b, 3 + k], xs[k]))
+        return begin(copies)
+
+    def cross_sum(b):
+        @pl.loop(0, 4)
+        def _(i):
+            rows = pl.ds(pl.multiple_of(i * CH, 8), CH)
+            st[b, i] = (ps[0, b, y, rows, :] + rx2[b, 0, rows, :]) + (rx2[b, 1, rows, :] + rx2[b, 2, rows, :])
+            st[b, 4 + i] = (ps[1, b, x, rows, :] + ry2[b, 0, rows, :]) + (ry2[b, 1, rows, :] + ry2[b, 2, rows, :])
+
+    def along(b):
+        return begin([remote(st.at[b, lax.rem(z + k + 1, 8)], rz.at[b, k], s3.at[b, k], r3.at[b, k], zs[k])
+                      for k in range(7)])
+
+    def along_sum(b):
+        total = st[b, z]
+        for k in range(7):
+            total += rz[b, k]
+        fin[b] = total
+
+    def spread(b):
+        for i in range(6):
+            if i < 4:
+                to = unit_zh * 4 + i
+                src, dst, rsem = fin.at[b, pl.ds(0, GROWS)], ga.at[b, z], rg4.at[b, z]
+            else:
+                to = (i - 4) * 4 + unit_zl
+                src, dst, rsem = fin.at[b, pl.ds(GROWS, AROWS)], aa.at[b, z], ra4.at[b, z]
+
+            @pl.when(to == z)
+            def _():
+                pltpu.make_async_copy(src, dst, rsem).start()
+
+            @pl.when(to != z)
+            def _():
+                remote(src, dst, s4.at[b, i], rsem, at(x, y, to, core)).start()
+
+    def spread_sent(b):
+        for i in range(6):
+            to = unit_zh * 4 + i if i < 4 else (i - 4) * 4 + unit_zl
+            src = fin.at[b, pl.ds(0, GROWS)] if i < 4 else fin.at[b, pl.ds(GROWS, AROWS)]
+            dst, rsem = (ga.at[b, z], rg4.at[b, z]) if i < 4 else (aa.at[b, z], ra4.at[b, z])
+
+            @pl.when(to != z)
+            def _():
+                remote(src, dst, s4.at[b, i], rsem, at(x, y, to, core)).wait_send()
+
+    def give(b):
+        for on, mine, src, all_to, dst, rsem, first in (
+                (g_on, g_self, ga.at[b], g_to, fg.at[part, b], rg5.at[b, part], 0),
+                (a_on, a_self, aa.at[b], a_to, fa.at[part, b], ra5.at[b, part], 4)):
+            @pl.when(on)
+            def _():
+                for i in range(8):
+                    piece = fin.at[b, pl.ds(0, GROWS)] if first == 0 else fin.at[b, pl.ds(GROWS, AROWS)]
+                    arrive = (rg4 if first == 0 else ra4).at[b, i]
+                    pltpu.make_async_copy(piece, src.at[i], arrive).wait()
+                for i, device in enumerate(all_to):
+                    if i == 0:
+                        @pl.when(mine)
+                        def _():
+                            pltpu.make_async_copy(src, dst, rsem).start()
+
+                        @pl.when(jnp.logical_not(mine))
+                        def _():
+                            remote(src, dst, s5.at[b, first], rsem, device).start()
+                    else:
+                        remote(src, dst, s5.at[b, first + i], rsem, device).start()
+
+    def given(b):
+        for on, mine, src, all_to, dst, rsem, first in (
+                (g_on, g_self, ga.at[b], g_to, fg.at[part, b], rg5.at[b, part], 0),
+                (a_on, a_self, aa.at[b], a_to, fa.at[part, b], ra5.at[b, part], 4)):
+            @pl.when(on)
+            def _():
+                for i, device in enumerate(all_to):
+                    copy = remote(src, dst, s5.at[b, first + i], rsem, device)
+                    if i == 0:
+                        @pl.when(jnp.logical_not(mine))
+                        def _():
+                            copy.wait_send()
+                    else:
+                        copy.wait_send()
+
+    def taken(b):
+        for i in range(2):
+            pltpu.make_async_copy(ga.at[b], fg.at[i, b], rg5.at[b, i]).wait()
+            pltpu.make_async_copy(aa.at[b], fa.at[i, b], ra5.at[b, i]).wait()
+
+    batches = range(NB)
+    q = begin([remote(tr, q1.at[k], ts.at[k], tr_sem.at[k], xs[k]) for k in range(3)])
+    second, third = [], []
+    first = [plane(0)]
+    plane_pass(0, first[0])
+    for b in batches:
+        if b + 1 < NB:
+            first.append(plane(b + 1))
+        plane_sum(b, first[b])
+        second.append(cross(b))
+        if b + 1 < NB:
+            plane_pass(b + 1, first[b + 1])
+    end(q)
     t1[...] = (tr[...] + q1[0]) + (q1[1] + q1[2])
-
-    copies = []
-    for k in range(3):
-        copies.append(send(sx.at[lax.rem(y + k + 1, 4)], rx2.at[k], s2.at[k], r2.at[k], ys[k]))
-        copies.append(send(sy.at[lax.rem(x + k + 1, 4)], ry2.at[k], s2.at[3 + k], r2.at[3 + k], xs[k]))
-        copies.append(send(t1, q2.at[k], s2.at[6 + k], r2.at[6 + k], ys[k]))
-    for copy in copies:
-        copy.wait()
-
-    @pl.loop(0, 4)
-    def _(i):
-        rows = pl.ds(pl.multiple_of(i * CH, 8), CH)
-        st[i] = (sx[y, rows, :] + rx2[0, rows, :]) + (rx2[1, rows, :] + rx2[2, rows, :])
-        st[4 + i] = (sy[x, rows, :] + ry2[0, rows, :]) + (ry2[1, rows, :] + ry2[2, rows, :])
+    q = begin([remote(t1, q2.at[k], ts.at[3 + k], tr_sem.at[3 + k], ys[k]) for k in range(3)])
+    for b in batches:
+        end(second[b])
+        cross_sum(b)
+        third.append(along(b))
+    end(q)
     t2[...] = (t1[...] + q2[0]) + (q2[1] + q2[2])
-
-    copies = []
-    for k in range(7):
-        copies.append(send(st.at[lax.rem(z + k + 1, 8)], rz.at[k], s3.at[k], r3.at[k], zs[k]))
-        copies.append(send(t2, q3.at[k], s3.at[7 + k], r3.at[7 + k], zs[k]))
-    for copy in copies:
-        copy.wait()
-    total = st[z]
+    q = begin([remote(t2, q3.at[k], ts.at[6 + k], tr_sem.at[6 + k], zs[k]) for k in range(7)])
+    for b in batches:
+        end(third[b])
+        along_sum(b)
+        spread(b)
+    end(q)
     trace = t2[...]
     for k in range(7):
-        total += rz[k]
         trace += q3[k]
-    fin[...] = total
     t3[...] = trace
-
-    side = send(t3, q4, s4, r4, (sib, own))
-    gsrc = fin.at[pl.ds(0, GROWS)]
-    asrc = fin.at[pl.ds(GROWS, AROWS)]
-    gdst = fg.at[part, z]
-    adst = fa.at[part, z]
-    slot = part * 8 + z
-
-    def put(src, dst, ssem, rsem, device, mine):
-        @pl.when(mine)
-        def _():
-            pltpu.make_async_copy(src, dst, rsem).start()
-
-        @pl.when(jnp.logical_not(mine))
-        def _():
-            send(src, dst, ssem, rsem, device)
-
-    put(gsrc, gdst, sg.at[0], rg.at[slot], (unit, own), unit == dp)
-    put(asrc, adst, sa.at[0], ra.at[slot], (dp, unit), unit == own)
-
-    def out(k, _):
-        send(gsrc, gdst, sg.at[k], rg.at[slot], (unit, lax.rem(own + k, 16)))
-        send(asrc, adst, sa.at[k], ra.at[slot], (lax.rem(dp + k, 16), unit))
-        return 0
-    lax.fori_loop(1, 16, out, 0)
-
-    def sent(src, dst, ssem):
-        pltpu.make_async_remote_copy(src_ref=src, dst_ref=dst, send_sem=ssem, recv_sem=r4,
-                                     device_id=(sib, own), device_id_type=MESH).wait_send()
-
-    def got(dst, src, rsem):
-        pltpu.make_async_copy(src, dst, rsem).wait()
-
-    def arrive(k, _):
-        got(fg.at[k // 8, lax.rem(k, 8)], gsrc, rg.at[k])
-        got(fa.at[k // 8, lax.rem(k, 8)], asrc, ra.at[k])
-        return 0
-    lax.fori_loop(0, 16, arrive, 0)
-
-    def left(k, _):
-        sent(gsrc, gdst, sg.at[k])
-        sent(asrc, adst, sa.at[k])
-        return 0
-    lax.fori_loop(1, 16, left, 0)
-
-    @pl.when(unit != dp)
-    def _():
-        sent(gsrc, gdst, sg.at[0])
-
-    @pl.when(unit != own)
-    def _():
-        sent(asrc, adst, sa.at[0])
-    side.wait()
-    fg_out[...] = fg[...]
-    fa_out[...] = fa[...]
+    q = begin([remote(t3, q4, ts.at[13], tr_sem.at[13], (sib, own))])
+    for b in batches:
+        give(b)
+    end(q)
     tt[core] = t3[...]
     tt[1 - core] = q4[...]
     t_out[0:8, :] = tt[0, 0:8, :] + tt[1, 0:8, :]
     t_out[8:16, :] = jnp.broadcast_to(tt[own // 8, pl.ds(8 + lax.rem(own, 8), 1), :], (8, 128))
+    for b in batches:
+        taken(b)
+        for i in range(2):
+            for k in range(8):
+                fg_out[i, k, b * GROWS:(b + 1) * GROWS, :] = fg[i, b, k]
+                fa_out[i, k, b * AROWS:(b + 1) * AROWS, :] = fa[i, b, k]
+    for b in batches:
+        spread_sent(b)
+        given(b)
 
 
 def reduce_all(gx, gy, tr):
     vmem = pl.BlockSpec(memory_space=pltpu.VMEM)
     dma = pltpu.SemaphoreType.DMA
     tile = pltpu.VMEM((16, 128), F32)
+
+    def buf(*shape):
+        return pltpu.VMEM(shape + (128,), F32)
+
     return pl.pallas_call(
         reduce_kernel,
-        out_shape=(jax.ShapeDtypeStruct((2, 8, GROWS, 128), F32),
-                   jax.ShapeDtypeStruct((2, 8, AROWS, 128), F32),
+        out_shape=(jax.ShapeDtypeStruct((2, 8, NB * GROWS, 128), F32),
+                   jax.ShapeDtypeStruct((2, 8, NB * AROWS, 128), F32),
                    jax.ShapeDtypeStruct((16, 128), F32)),
         in_specs=[pl.BlockSpec(memory_space=pl.ANY)] * 2 + [vmem],
         out_specs=(vmem,) * 3,
         scratch_shapes=[
-            pltpu.VMEM((4, HALF, 128), F32), pltpu.VMEM((4, HALF, 128), F32),
-            pltpu.VMEM((3, 4, HALF, 128), F32), pltpu.VMEM((3, 4, HALF, 128), F32),
-            pltpu.VMEM((3, HALF, 128), F32), pltpu.VMEM((3, HALF, 128), F32),
-            pltpu.VMEM((8, CH, 128), F32), pltpu.VMEM((7, CH, 128), F32), pltpu.VMEM((CH, 128), F32),
-            pltpu.VMEM((2, 8, GROWS, 128), F32), pltpu.VMEM((2, 8, AROWS, 128), F32),
-            tile, tile, tile,
-            pltpu.VMEM((3, 16, 128), F32), pltpu.VMEM((3, 16, 128), F32), pltpu.VMEM((7, 16, 128), F32), tile, pltpu.VMEM((2, 16, 128), F32),
-            dma((2,)), dma((9,)), dma((9,)), dma((9,)), dma((9,)), dma((14,)), dma((14,)),
-            dma((16,)), dma((16,)), dma((16,)), dma((16,)), dma, dma,
+            buf(2, NB, 4, HALF), buf(2, NB, 2, 2, HALF), buf(2, NB, 2, 2, HALF), buf(2, NB, 2, 4, HALF),
+            buf(NB, 3, HALF), buf(NB, 3, HALF), buf(NB, 8, CH), buf(NB, 7, CH), buf(NB, CH),
+            buf(NB, 8, GROWS), buf(NB, 8, AROWS), buf(2, NB, 8, GROWS), buf(2, NB, 8, AROWS),
+            tile, tile, tile, buf(3, 16), buf(3, 16), buf(7, 16), tile, buf(2, 16),
+            dma((2, NB, 3)), dma((2, NB, 6)), dma((2, NB, 6)), dma((NB, 6)), dma((NB, 6)), dma((NB, 7)), dma((NB, 7)),
+            dma((NB, 6)), dma((NB, 8)), dma((NB, 8)), dma((NB, 12)), dma((NB, 2)), dma((NB, 2)), dma((14,)), dma((14,)),
         ],
         compiler_params=pltpu.CompilerParams(collective_id=1, has_side_effects=True, vmem_limit_bytes=VLIM),
         name="reduce_all",
@@ -499,7 +605,9 @@
             if i != j:
                 gi_ref[b, j * 128:(j + 1) * 128, i * 128:(i + 1) * 128] = tile.T
     for b in range(2):
-        left = dot(ai_ref[...], w_ref[b].astype(F32))
+        w = w_ref[...].astype(F32)[b * GB:(b + 1) * GB]
+        w = jnp.concatenate([w, jnp.zeros((384 - GB, 256), F32)], axis=0)
+        left = dot(ai_ref[...], w, 1, 1)
         p_ref[:, b * 384:(b + 1) * 384] = dot(left, gi_ref[b]).astype(jnp.bfloat16)
 
 
@@ -534,61 +642,77 @@
     def other(d):
         return d + 2 - 4 * lax.rem(d // 2, 2)
 
+    far = lax.rem(y + 2, 4) * 4 + lax.rem(dp, 4)
     waits = []
 
-    def send(d, ssem, rsem, device, src=None, half=None):
+    def half(ref, h):
+        return ref.at[pl.ds(h * 128, 128)]
+
+    def send(d, h, sems, i, device, src=None):
         src = o_ref.at[d] if src is None else src
-        dst = o_ref.at[d]
-        if half is not None:
-            src = src.at[pl.ds(half * 128, 128)]
-            dst = dst.at[pl.ds(half * 128, 128)]
-        copy = pltpu.make_async_remote_copy(src_ref=src, dst_ref=dst, send_sem=ssem, recv_sem=rsem,
-                                            device_id=(device, own), device_id_type=MESH)
+        copy = pltpu.make_async_remote_copy(
+            src_ref=half(src, h), dst_ref=half(o_ref.at[d], h), send_sem=sems[0].at[i], recv_sem=sems[1].at[i],
+            device_id=(device, own), device_id_type=MESH)
         copy.start()
         waits.append(copy)
 
-    def arrived(d, sem, half=None):
-        dst = o_ref.at[d]
-        if half is not None:
-            dst = dst.at[pl.ds(half * 128, 128)]
-        pltpu.make_async_remote_copy(src_ref=dst, dst_ref=dst, send_sem=sz, recv_sem=sem,
+    def arrived(d, h, sems, i):
+        dst = half(o_ref.at[d], h)
+        pltpu.make_async_remote_copy(src_ref=dst, dst_ref=dst, send_sem=sems[0].at[i], recv_sem=sems[1].at[i],
                                      device_id=(sib, own), device_id_type=MESH).wait_recv()
 
-    send(dp, sz, rz, anti, p_ref)
-    send(dp, sy.at[0], ry.at[0], up, p_ref)
-    send(dp, sy.at[1], ry.at[1], down, p_ref)
-    send(dp, sc.at[0], rc.at[0], sib, p_ref)
+    zsem, ysem, hsem, csem = (sz, rz), (sy, ry), (sh, rh), (sc, rc)
+    for h in range(2):
+        send(dp, h, zsem, h, anti, p_ref)
+        send(dp, h, ysem, h, up, p_ref)
+        send(dp, 1 - h, ysem, 3 - h, down, p_ref)
+    for h in range(2):
+        send(dp, h, csem, h, sib, p_ref)
     keep = pltpu.make_async_copy(p_ref, o_ref.at[dp], local)
     keep.start()
-    arrived(down, ry.at[0])
-    send(down, sh.at[0], rh.at[0], up, half=0)
-    send(down, sc.at[1], rc.at[1], sib)
-    arrived(up, ry.at[1])
-    send(up, sh.at[1], rh.at[1], down, half=1)
-    send(up, sc.at[2], rc.at[2], sib)
-    arrived(anti, rz)
-    send(anti, sy.at[2], ry.at[2], up)
-    send(anti, sy.at[3], ry.at[3], down)
-    send(anti, sc.at[3], rc.at[3], sib)
-    far = other(down) * 0 + lax.rem(y + 2, 4) * 4 + lax.rem(dp, 4)
-    arrived(other(down), ry.at[2])
-    send(other(down), sh.at[2], rh.at[2], up, half=0)
-    send(other(down), sc.at[4], rc.at[4], sib)
-    arrived(other(up), ry.at[3])
-    send(other(up), sh.at[3], rh.at[3], down, half=1)
-    send(other(up), sc.at[5], rc.at[5], sib)
-    arrived(far, rh.at[0], half=0)
-    arrived(far, rh.at[1], half=1)
-    send(far, sc.at[6], rc.at[6], sib)
-    arrived(other(far), rh.at[2], half=0)
-    arrived(other(far), rh.at[3], half=1)
-    send(other(far), sc.at[7], rc.at[7], sib)
+    arrived(down, 0, ysem, 0)
+    send(down, 0, hsem, 0, up)
+    arrived(up, 1, ysem, 3)
+    send(up, 1, hsem, 1, down)
+    send(down, 0, csem, 2, sib)
+    send(up, 1, csem, 5, sib)
+    arrived(down, 1, ysem, 1)
+    send(down, 1, csem, 3, sib)
+    arrived(up, 0, ysem, 2)
+    send(up, 0, csem, 4, sib)
+    arrived(anti, 0, zsem, 0)
+    send(anti, 0, ysem, 4, up)
+    send(anti, 0, ysem, 6, down)
+    send(anti, 0, csem, 6, sib)
+    arrived(far, 0, hsem, 0)
+    send(far, 0, csem, 8, sib)
+    arrived(far, 1, hsem, 1)
+    send(far, 1, csem, 9, sib)
+    arrived(anti, 1, zsem, 1)
+    send(anti, 1, ysem, 5, up)
+    send(anti, 1, ysem, 7, down)
+    send(anti, 1, csem, 7, sib)
+    arrived(other(down), 0, ysem, 4)
+    send(other(down), 0, hsem, 2, up)
+    send(other(down), 0, csem, 10, sib)
+    arrived(other(up), 0, ysem, 6)
+    send(other(up), 0, csem, 12, sib)
+    arrived(other(up), 1, ysem, 7)
+    send(other(up), 1, hsem, 3, down)
+    send(other(up), 1, csem, 13, sib)
+    arrived(other(down), 1, ysem, 5)
+    send(other(down), 1, csem, 11, sib)
+    arrived(other(far), 0, hsem, 2)
+    send(other(far), 0, csem, 14, sib)
+    arrived(other(far), 1, hsem, 3)
+    send(other(far), 1, csem, 15, sib)
 
     def twin(d):
         return d + 1 - 2 * lax.rem(d, 2)
 
-    for i, d in enumerate((dp, down, up, anti, other(down), other(up), far, other(far))):
-        arrived(twin(d), rc.at[i])
+    for i, d in enumerate((dp, down, up, anti, far, other(down), other(up), other(far))):
+        for h in range(2):
+            arrived(twin(d), h, csem, 2 * i + h)
     keep.wait()
     for copy in waits:
         copy.wait_send()
@@ -601,7 +725,7 @@
         out_shape=jax.ShapeDtypeStruct((16, 256, 768), jnp.bfloat16),
         in_specs=[pl.BlockSpec(memory_space=pl.ANY)],
         out_specs=pl.BlockSpec(memory_space=pl.ANY),
-        scratch_shapes=[dma, dma, dma, dma((4,)), dma((4,)), dma((4,)), dma((4,)), dma((8,)), dma((8,))],
+        scratch_shapes=[dma, dma((2,)), dma((2,)), dma((8,)), dma((8,)), dma((4,)), dma((4,)), dma((16,)), dma((16,))],
         compiler_params=pltpu.CompilerParams(collective_id=2, has_side_effects=True),
         name="gather",
     )(p)
@@ -631,8 +755,7 @@
     sib_acts, sib_grads = swap(acts, grads_out)
     gx, gy, tr = grams(acts, grads_out, sib_acts, sib_grads)
     fg, fa, tr = reduce_all(gx, gy, tr)
-    w = jnp.pad(weight_grad.reshape(256, 2, GB).transpose(1, 0, 2), ((0, 0), (0, 0), (0, 384 - GB)))
-    p = solve(fg.reshape(2, 8 * GROWS, 128), fa.reshape(16 * AROWS, 128), tr, w)
+    p = solve(fg.reshape(2, 512, 128), fa.reshape(256, 128), tr, weight_grad.T)
     return flatten(gather(p))
 
 

time: 192 us -> 164 us (0.85)
  Pallas kernels: 189 us -> 162 us
  local copies, waits for them, and re-layouts: 1.98 us -> 0 us
    pallas_call x1, Pallas kernels: 95.2 us -> 73.5 us  [reduce_all(): pl.pallas_call(reduce_kernel, out_shape=(jax.ShapeDtypeStruct((2, 8, NB *...]
    pallas_call x1, Pallas kernels: 42.4 us -> 37.1 us  [gather(): pl.pallas_call(gather_kernel, out_shape=jax.ShapeDtypeStruct((16, 256, 76...]
where the time goes in v3:
time: 164 us; the launch traced here: 162 us
  Pallas kernels  162 us (99%)
    pallas_call x1, Pallas kernels, reduce_all(): pl.pallas_call(reduce_kernel, out_shape=(jax.ShapeDtypeStruct((2, 8, NB *...  73.5 us
    pallas_call x1, Pallas kernels, gather(): pl.pallas_call(gather_kernel, out_shape=jax.ShapeDtypeStruct((16, 256, 76...  37.1 us
    pallas_call x1, Pallas kernels, solve(): pl.pallas_call(solve_kernel, out_shape=jax.ShapeDtypeStruct((256, 768), j...  28 us
    pallas_call x1, Pallas kernels, grams(): pl.pallas_call(gram_kernel, out_shape=(shape, shape, jax.ShapeDtypeStruct...  10.1 us
    pallas_call x1, Pallas kernels, flatten(): pl.pallas_call(flat_kernel, out_shape=jax.ShapeDtypeStruct((256, FF), jnp...  6.68 us
    pallas_call x1, Pallas kernels, swap(): pl.pallas_call(swap_kernel, out_shape=(jax.ShapeDtypeStruct((rows, D // 2...  6.68 us

profile of v3, /device:TPU:33, one launch (start us, length us, event | category | flops | bytes accessed | tf_op | source)
XLA Modules:
  0.0 162.1 jit_solution(7149183243930993265)
XLA Ops:
  0.0 6.7 %swap.1 = (bf16[224,2048]{1,0:T(8,128)(2,1)}, bf16[224,5504]{1,0:T(8,128)(2,1)}) custom-call(bf16[224,4096]{1,0:T(8,128)(2,1)} %a_ref.3, bf16[224,11008]{1,0:T(8,128)(2,1)} %g_ref.3), custom_call_target="tpu_custom_call" | custom-call | tf_op jit(solution)/shard_map/swap/pallas_call | solution.py:62
  6.7 10.1 %grams.1 = (f32[2,16,160,128]{3,2,1,0:T(8,128)}, f32[2,16,160,128]{3,2,1,0:T(8,128)}, f32[16,128]{1,0:T(8,128)}) custom-call(bf16[224,4096]{1,0:T(8,128)(2,1)} %a_ref.3, bf16[224,11008]{1,0:T(8,128)(2,1)} %g_ref.3, bf16[224,2048]{1,0:T(8,128)(2,1)} %get-tuple-element.13.as_ref, bf16[224,5504]{1,0:T(8,128)(2,1)} %get-tuple-element.14.gs_ref), custom_call_target="tpu_custom_call" | custom-call | tf_op jit(solution)/shard_map/grams/pallas_call | solution.py:161
  16.8 73.5 %reduce_all.1 = (f32[2,8,64,128]{3,2,1,0:T(8,128)}, f32[2,8,16,128]{3,2,1,0:T(8,128)}, f32[16,128]{1,0:T(8,128)}) custom-call(f32[2,16,160,128]{3,2,1,0:T(8,128)} %get-tuple-element.15.gx, f32[2,16,160,128]{3,2,1,0:T(8,128)} %get-tuple-element.16.gy, f32[16,128]{1,0:T(8,128)} %get-tuple-element.17.tr), custom_call_target="tpu_custom_call" | custom-call | tf_op jit(solution)/shard_map/reduce_all/pallas_call | solution.py:430
  90.3 28.0 %solve.1.p_ref = bf16[256,768]{1,0:T(8,128)(2,1)} custom-call(f32[2,512,128]{2,1,0:T(8,128)} %bitcast.3, f32[256,128]{1,0:T(8,128)} %bitcast.5, f32[16,128]{1,0:T(8,128)} %get-tuple-element.20.t_ref, bf16[688,256]{1,0:T(8,128)(2,1)} %bitcast.4), custom_call_target="tpu_custom_call" | custom-call | tf_op jit(solution)/shard_map/solve/pallas_call | solution.py:616
  118.3 37.1 %gather.1.i_ref = bf16[16,256,768]{2,1,0:T(8,128)(2,1)} custom-call(bf16[256,768]{1,0:T(8,128)(2,1)} %solve.1.p_ref), custom_call_target="tpu_custom_call" | custom-call | tf_op jit(solution)/shard_map/gather/pallas_call | solution.py:723
  155.4 6.7 %flatten.1 = bf16[256,11008]{1,0:T(8,128)(2,1)} custom-call(bf16[16,256,768]{2,1,0:T(8,128)(2,1)} %gather.1.i_ref), custom_call_target="tpu_custom_call" | custom-call | tf_op jit(solution)/shard_map/flatten/pallas_call | solution.py:743

commit v4 on v3

--- a/solution.py
+++ b/solution.py
@@ -23,12 +23,22 @@
 CH = GROWS + AROWS
 HALF = 4 * CH
 VLIM = 56 * 1024 * 1024
-
-
-def position(j):
-    x = 2 * (j // 2 % 2) + (j // 4 + j // 8) % 2
-    y = 2 * (j % 2) + j // 8
-    return x, y
+WIN = 7 * 128
+WIDTHS = [WIN] * 7 + [WIN - 128]
+CUT = (352, 336)
+
+
+def grad_position(p, part):
+    y = p // 2
+    return 2 * part + (p + y) % 2, y
+
+
+def act_position(k, part):
+    return k % 4, 2 * part + k // 4
+
+
+def window(d):
+    return 128 * (43 * d // 8)
 
 
 def place():
@@ -44,12 +54,15 @@
     barrier = pltpu.get_barrier_semaphore()
     pl.semaphore_signal(barrier, inc=1, device_id=(sib, own), device_id_type=MESH)
     pl.semaphore_wait(barrier, 1)
+    width = ao_ref.shape[1]
+    pieces = [(a_ref.at[:, pl.ds(pl.multiple_of((1 - core) * width, 128), width)], ao_ref)]
+    for p in range(8):
+        start = pl.multiple_of(window(2 * p + 1 - core), 128)
+        pieces.append((g_ref.at[:, pl.ds(start, WIDTHS[p])], go_ref.at[:, pl.ds(p * WIN, WIDTHS[p])]))
     copies = []
-    for i, (src, dst) in enumerate(((a_ref, ao_ref), (g_ref, go_ref))):
-        width = dst.shape[1]
-        theirs = pl.ds(pl.multiple_of((1 - core) * width, 128), width)
+    for i, (src, dst) in enumerate(pieces):
         copy = pltpu.make_async_remote_copy(
-            src_ref=src.at[:, theirs], dst_ref=dst, send_sem=send.at[i], recv_sem=recv.at[i],
+            src_ref=src, dst_ref=dst, send_sem=send.at[i], recv_sem=recv.at[i],
             device_id=(sib, own), device_id_type=MESH)
         copy.start()
         copies.append(copy)
@@ -62,10 +75,10 @@
     return pl.pallas_call(
         swap_kernel,
         out_shape=(jax.ShapeDtypeStruct((rows, D // 2), acts.dtype),
-                   jax.ShapeDtypeStruct((rows, FF // 2), acts.dtype)),
+                   jax.ShapeDtypeStruct((rows, 8 * WIN), acts.dtype)),
         in_specs=[pl.BlockSpec(memory_space=pl.ANY)] * 2,
         out_specs=(pl.BlockSpec(memory_space=pl.ANY),) * 2,
-        scratch_shapes=[pltpu.SemaphoreType.DMA((2,))] * 2,
+        scratch_shapes=[pltpu.SemaphoreType.DMA((9,))] * 2,
         compiler_params=pltpu.CompilerParams(collective_id=0, has_side_effects=True),
         name="swap",
     )(acts, grads)
@@ -75,28 +88,33 @@
     return lax.dot_general(block, block, (((0,), (0,)), ((), ())), preferred_element_type=F32)
 
 
-def gram_kernel(a_ref, g_ref, as_ref, gs_ref, x_out, y_out, t_ref, abuf, gbuf, x_ref, y_ref, sems, out_sems):
+def gram_kernel(a_ref, g_ref, as_ref, gs_ref, x_out, y_out, t_ref, abuf, gbuf, even, x_ref, y_ref, sems, out_sems):
     core = lax.rem(lax.axis_index("dp"), 2)
     rows = a_ref.shape[0]
-    cut = 22 * 128
+    mine, theirs = pl.ds(0, rows), pl.ds(rows, rows)
+    width = abuf.shape[1]
+    moves = [[(a_ref.at[:, pl.ds(pl.multiple_of(core * width, 128), width)], abuf.at[mine]), (as_ref, abuf.at[theirs])]]
+    for lo in (0, 4):
+        group = []
+        for p in range(lo, lo + 4):
+            start = pl.multiple_of(window(2 * p + core), 128)
+            group.append((g_ref.at[:, pl.ds(start, WIDTHS[p])], gbuf.at[mine, pl.ds(p * WIN, WIDTHS[p])]))
+        span = pl.ds(lo * WIN, 4 * WIN - WIN + WIDTHS[lo + 3])
+        group.append((gs_ref.at[:, span], gbuf.at[theirs, span]))
+        moves.append(group)
     copies = []
-    for i, (whole, other, buf, lo, hi) in enumerate((
-            (a_ref, as_ref, abuf, 0, D // 2), (g_ref, gs_ref, gbuf, 0, cut), (g_ref, gs_ref, gbuf, cut, FF // 2))):
-        mine = whole.at[:, pl.ds(pl.multiple_of(core * buf.shape[1] + lo, 128), hi - lo)]
-        here = pltpu.make_async_copy(mine, buf.at[pl.ds(0, rows), pl.ds(lo, hi - lo)], sems.at[2 * i])
-        there = pltpu.make_async_copy(other.at[:, pl.ds(lo, hi - lo)],
-                                      buf.at[pl.ds(rows, rows), pl.ds(lo, hi - lo)], sems.at[2 * i + 1])
-        here.start()
-        there.start()
-        copies.append((here, there))
-
-    def store_all(j, size, lead, row, value):
-        px, py = position(j)
+    for i, group in enumerate(moves):
+        copies.append([pltpu.make_async_copy(src, dst, sems.at[i, n]) for n, (src, dst) in enumerate(group)])
+        for copy in copies[i]:
+            copy.start()
+
+    def store_all(where, size, lead, row, value):
+        px, py = where
         done = 0
         while done < value.shape[0]:
             at = row + done
             n = min(size - at % size, value.shape[0] - done)
-            chunk, batch = at // size // NB, at // size % NB
+            batch, chunk = at // size // 8, at // size % 8
             rows_at = pl.ds(chunk % 4 * CH + lead + at % size, n)
             if chunk < 4:
                 x_ref[batch, px * 4 + py, rows_at, :] = value[done:done + n]
@@ -106,10 +124,10 @@
 
     outs = []
 
-    def finish(j):
-        px, py = position(j)
+    def finish(where):
+        px, py = where
         for i, (src, dst, at) in enumerate(((x_ref, x_out, px * 4 + py), (y_ref, y_out, py * 4 + px))):
-            copy = pltpu.make_async_copy(src.at[:, at], dst.at[:, at], out_sems.at[i, j])
+            copy = pltpu.make_async_copy(src.at[:, at], dst.at[:, at], out_sems.at[i, px * 4 + py])
             copy.start()
             outs.append(copy)
 
@@ -129,25 +147,34 @@
         second = diag(t2)
         act_sum += diag(t0) + second
         t_ref[8 + k:9 + k, :] = second
-        store_all(2 * k, AROWS, GROWS, 0, g[128:256, 0:128])
-        store_all(2 * k + 1, AROWS, GROWS, 0, jnp.where(r >= c, t0, t2))
+        store_all(act_position(k, 0), AROWS, GROWS, 0, g[128:256, 0:128])
+        store_all(act_position(k, 1), AROWS, GROWS, 0, jnp.where(r >= c, t0, t2))
     for j in range(16):
         if j in (0, 8):
             for copy in copies[1 + j // 8]:
                 copy.wait()
-        g = gram(gbuf[:, j * GB:(j + 1) * GB])
+            for odd in range(2):
+                @pl.when(core == odd)
+                def _():
+                    for i in range(j, j + 8):
+                        d = i // 2 * 2 + odd
+                        start = i // 2 * WIN + 2 * GB * d - window(d) + i % 2 * GB
+                        even[i, :, 0:GB] = gbuf[:, start:start + GB]
+        block = even[j, :, 0:GB]
+        g = lax.dot_general(block, block[:, 0:256], (((0,), (0,)), ((), ())), preferred_element_type=F32)
         t0, t2 = g[0:128, 0:128], g[128:256, 128:256]
-        t5 = jnp.concatenate([g[256:344, 256:344], jnp.zeros((88, 40), F32)], axis=1)
+        t5 = jnp.concatenate([gram(block[:, 256:GB]), jnp.zeros((88, 40), F32)], axis=1)
         second = diag(t2)
         grad_sum += diag(t0) + second + jnp.sum(jnp.where(r[:88] == c[:88], t5, 0.0), axis=0, keepdims=True)
         tail = jnp.concatenate([pltpu.roll(t5[48:88], 40, 1), jnp.zeros((8, 128), F32)], axis=0)
-        store_all(j, GROWS, 0, 0, g[128:256, 0:128])
-        store_all(j, GROWS, 0, 128, jnp.where(r >= c, t0, t2))
-        store_all(j, GROWS, 0, 256, g[256:344, 0:128])
-        store_all(j, GROWS, 0, 344, g[256:344, 128:256])
-        store_all(j, GROWS, 0, 432, jnp.where(c[:48] < 88, t5[0:48], tail))
-        store_all(j, GROWS, 0, 480, jnp.concatenate([second, jnp.zeros((31, 128), F32)], axis=0))
-        finish(j)
+        where = grad_position(j // 2, j % 2)
+        store_all(where, GROWS, 0, 0, g[128:256, 0:128])
+        store_all(where, GROWS, 0, 128, jnp.where(r >= c, t0, t2))
+        store_all(where, GROWS, 0, 256, g[256:344, 0:128])
+        store_all(where, GROWS, 0, 344, g[256:344, 128:256])
+        store_all(where, GROWS, 0, 432, jnp.where(c[:48] < 88, t5[0:48], tail))
+        store_all(where, GROWS, 0, 480, jnp.concatenate([second, jnp.zeros((31, 128), F32)], axis=0))
+        finish(where)
     t_ref[0:8, :] = jnp.concatenate([act_sum, grad_sum, jnp.zeros((6, 128), F32)], axis=0)
     for copy in outs:
         copy.wait()
@@ -163,16 +190,17 @@
         out_shape=(shape, shape, jax.ShapeDtypeStruct((16, 128), F32)),
         in_specs=[anywhere] * 4,
         out_specs=(anywhere, anywhere, vmem),
-        scratch_shapes=[pltpu.VMEM((2 * rows, D // 2), acts.dtype), pltpu.VMEM((2 * rows, FF // 2), acts.dtype),
+        scratch_shapes=[pltpu.VMEM((2 * rows, D // 2), acts.dtype), pltpu.VMEM((2 * rows, 8 * WIN), acts.dtype),
+                        pltpu.VMEM((16, 2 * rows, 384), acts.dtype),
                         pltpu.VMEM(shape.shape, F32), pltpu.VMEM(shape.shape, F32),
-                        pltpu.SemaphoreType.DMA((6,)), pltpu.SemaphoreType.DMA((2, 16))],
+                        pltpu.SemaphoreType.DMA((3, 5)), pltpu.SemaphoreType.DMA((2, 16))],
         compiler_params=pltpu.CompilerParams(vmem_limit_bytes=VLIM),
         name="grams",
     )(acts, grads, sib_acts, sib_grads)
 
 
-def reduce_kernel(gx, gy, tr, fg_out, fa_out, t_out,
-                  ps, pk, pm, pr, rx2, ry2, st, rz, fin, ga, aa, fg, fa, t1, t2, t3, q1, q2, q3, q4, tt,
+def reduce_kernel(gx, gy, tr, fg, fa, t_out,
+                  ps, pk, pm, pr, rx2, ry2, st, rz, fin, ga, aa, t1, t2, t3, q1, q2, q3, q4, tt,
                   local, s1, r1, s2, r2, s3, r3, s4, rg4, ra4, s5, rg5, ra5, ts, tr_sem):
     dp, own = place()
     core = lax.rem(dp, 2)
@@ -189,36 +217,17 @@
     xs = [at(lax.rem(x + k, 4), y, z, core) for k in (1, 2, 3)]
     ys = [at(x, lax.rem(y + k, 4), z, core) for k in (1, 2, 3)]
     zs = [at(x, y, lax.rem(z + k, 8), core) for k in range(1, 8)]
-    j = 8 * (y % 2) + 4 * ((x + y) % 2) + 2 * (x // 2) + y // 2
-    unit = core * 8 + j // 2
-    part = lax.rem(j, 2)
-    unit_zh = lax.rem(unit // 2, 2)
-    unit_zl = unit // 4
+    g_part, a_part = x // 2, y // 2
+    unit_zh = lax.rem(x + y, 2)
+    unit_zl = 2 * core + lax.rem(y, 2)
     g_on = zh == unit_zh
     a_on = zl == unit_zl
-    g_to = [(unit, zl * 4 + lax.rem(x + k, 4)) for k in range(4)]
-    a_to = [((lax.rem(y + k // 2, 4) * 2 + zh) * 2 + lax.rem(core + k, 2), unit) for k in range(8)]
-    g_self = unit == dp
-    a_self = unit == own
+    across = [at(x, lax.rem(y + k, 4), z, 1 - core) for k in range(4)]
 
     barrier = pltpu.get_barrier_semaphore()
-
-    def greet(device):
+    for device in xs + ys + zs + across:
         pl.semaphore_signal(barrier, inc=1, device_id=device, device_id_type=MESH)
-
-    for device in xs + ys + zs + [(sib, own)]:
-        greet(device)
-    for base in (dp, own):
-        for i in range(2):
-            js = lax.rem(base, 8) * 2 + i
-            source = at(*position(js), z, base // 8)
-
-            @pl.when(jnp.logical_or(source[0] != dp, source[1] != own))
-            def _():
-                greet(source)
-    g_count = jnp.where(g_on, 4 - jnp.where(g_self, 1, 0), 0)
-    a_count = jnp.where(a_on, 8 - jnp.where(a_self, 1, 0), 0)
-    pl.semaphore_wait(barrier, 14 + g_count + a_count)
+    pl.semaphore_wait(barrier, 17)
 
     def remote(src, dst, ssem, rsem, device):
         return pltpu.make_async_remote_copy(src_ref=src, dst_ref=dst, send_sem=ssem, recv_sem=rsem,
@@ -327,42 +336,28 @@
             def _():
                 remote(src, dst, s4.at[b, i], rsem, at(x, y, to, core)).wait_send()
 
+    def parts(b):
+        return ((g_on, ga.at[b], xs, fg.at[g_part, b], rg5.at[b, g_part], 0),
+                (a_on, aa.at[b], ys + across, fa.at[a_part, b], ra5.at[b, a_part], 3))
+
     def give(b):
-        for on, mine, src, all_to, dst, rsem, first in (
-                (g_on, g_self, ga.at[b], g_to, fg.at[part, b], rg5.at[b, part], 0),
-                (a_on, a_self, aa.at[b], a_to, fa.at[part, b], ra5.at[b, part], 4)):
+        for on, src, to, dst, rsem, first in parts(b):
             @pl.when(on)
             def _():
                 for i in range(8):
                     piece = fin.at[b, pl.ds(0, GROWS)] if first == 0 else fin.at[b, pl.ds(GROWS, AROWS)]
                     arrive = (rg4 if first == 0 else ra4).at[b, i]
                     pltpu.make_async_copy(piece, src.at[i], arrive).wait()
-                for i, device in enumerate(all_to):
-                    if i == 0:
-                        @pl.when(mine)
-                        def _():
-                            pltpu.make_async_copy(src, dst, rsem).start()
-
-                        @pl.when(jnp.logical_not(mine))
-                        def _():
-                            remote(src, dst, s5.at[b, first], rsem, device).start()
-                    else:
-                        remote(src, dst, s5.at[b, first + i], rsem, device).start()
+                for i, device in enumerate(to):
+                    remote(src, dst, s5.at[b, first + i], rsem, device).start()
+                pltpu.make_async_copy(src, dst, rsem).start()
 
     def given(b):
-        for on, mine, src, all_to, dst, rsem, first in (
-                (g_on, g_self, ga.at[b], g_to, fg.at[part, b], rg5.at[b, part], 0),
-                (a_on, a_self, aa.at[b], a_to, fa.at[part, b], ra5.at[b, part], 4)):
+        for on, src, to, dst, rsem, first in parts(b):
             @pl.when(on)
             def _():
-                for i, device in enumerate(all_to):
-                    copy = remote(src, dst, s5.at[b, first + i], rsem, device)
-                    if i == 0:
-                        @pl.when(jnp.logical_not(mine))
-                        def _():
-                            copy.wait_send()
-                    else:
-                        copy.wait_send()
+                for i, device in enumerate(to):
+                    remote(src, dst, s5.at[b, first + i], rsem, device).wait_send()
 
     def taken(b):
         for i in range(2):
@@ -410,10 +405,6 @@
     t_out[8:16, :] = jnp.broadcast_to(tt[own // 8, pl.ds(8 + lax.rem(own, 8), 1), :], (8, 128))
     for b in batches:
         taken(b)
-        for i in range(2):
-            for k in range(8):
-                fg_out[i, k, b * GROWS:(b + 1) * GROWS, :] = fg[i, b, k]
-                fa_out[i, k, b * AROWS:(b + 1) * AROWS, :] = fa[i, b, k]
     for b in batches:
         spread_sent(b)
         given(b)
@@ -429,18 +420,18 @@
 
     return pl.pallas_call(
         reduce_kernel,
-        out_shape=(jax.ShapeDtypeStruct((2, 8, NB * GROWS, 128), F32),
-                   jax.ShapeDtypeStruct((2, 8, NB * AROWS, 128), F32),
+        out_shape=(jax.ShapeDtypeStruct((2, NB, 8, GROWS, 128), F32),
+                   jax.ShapeDtypeStruct((2, NB, 8, AROWS, 128), F32),
                    jax.ShapeDtypeStruct((16, 128), F32)),
         in_specs=[pl.BlockSpec(memory_space=pl.ANY)] * 2 + [vmem],
         out_specs=(vmem,) * 3,
         scratch_shapes=[
             buf(2, NB, 4, HALF), buf(2, NB, 2, 2, HALF), buf(2, NB, 2, 2, HALF), buf(2, NB, 2, 4, HALF),
             buf(NB, 3, HALF), buf(NB, 3, HALF), buf(NB, 8, CH), buf(NB, 7, CH), buf(NB, CH),
-            buf(NB, 8, GROWS), buf(NB, 8, AROWS), buf(2, NB, 8, GROWS), buf(2, NB, 8, AROWS),
+            buf(NB, 8, GROWS), buf(NB, 8, AROWS),
             tile, tile, tile, buf(3, 16), buf(3, 16), buf(7, 16), tile, buf(2, 16),
             dma((2, NB, 3)), dma((2, NB, 6)), dma((2, NB, 6)), dma((NB, 6)), dma((NB, 6)), dma((NB, 7)), dma((NB, 7)),
-            dma((NB, 6)), dma((NB, 8)), dma((NB, 8)), dma((NB, 12)), dma((NB, 2)), dma((NB, 2)), dma((14,)), dma((14,)),
+            dma((NB, 6)), dma((NB, 8)), dma((NB, 8)), dma((NB, 10)), dma((NB, 2)), dma((NB, 2)), dma((14,)), dma((14,)),
         ],
         compiler_params=pltpu.CompilerParams(collective_id=1, has_side_effects=True, vmem_limit_bytes=VLIM),
         name="reduce_all",
@@ -604,18 +595,19 @@
             gi_ref[b, i * 128:(i + 1) * 128, j * 128:(j + 1) * 128] = tile
             if i != j:
                 gi_ref[b, j * 128:(j + 1) * 128, i * 128:(i + 1) * 128] = tile.T
+    out = []
     for b in range(2):
         w = w_ref[...].astype(F32)[b * GB:(b + 1) * GB]
         w = jnp.concatenate([w, jnp.zeros((384 - GB, 256), F32)], axis=0)
-        left = dot(ai_ref[...], w, 1, 1)
-        p_ref[:, b * 384:(b + 1) * 384] = dot(left, gi_ref[b]).astype(jnp.bfloat16)
+        out.append(dot(gi_ref[b], dot(w, ai_ref[...]))[0:GB])
+    p_ref[...] = jnp.concatenate(out, axis=0).astype(jnp.bfloat16)
 
 
 def solve(fg, fa, tr, w):
     vmem = pl.BlockSpec(memory_space=pltpu.VMEM)
     return pl.pallas_call(
         solve_kernel,
-        out_shape=jax.ShapeDtypeStruct((256, 768), jnp.bfloat16),
+        out_shape=jax.ShapeDtypeStruct((2 * GB, 256), jnp.bfloat16),
         in_specs=[vmem] * 4,
         out_specs=vmem,
         scratch_shapes=[pltpu.VMEM((12, 128, 128), F32), pltpu.VMEM((3, 128, 128), F32),
@@ -646,7 +638,7 @@
     waits = []
 
     def half(ref, h):
-        return ref.at[pl.ds(h * 128, 128)]
+        return ref.at[pl.ds(h * CUT[0], CUT[h])]
 
     def send(d, h, sems, i, device, src=None):
         src = o_ref.at[d] if src is None else src
@@ -722,7 +714,7 @@
     dma = pltpu.SemaphoreType.DMA
     return pl.pallas_call(
         gather_kernel,
-        out_shape=jax.ShapeDtypeStruct((16, 256, 768), jnp.bfloat16),
+        out_shape=jax.ShapeDtypeStruct((16, 2 * GB, 256), jnp.bfloat16),
         in_specs=[pl.BlockSpec(memory_space=pl.ANY)],
         out_specs=pl.BlockSpec(memory_space=pl.ANY),
         scratch_shapes=[dma, dma((2,)), dma((2,)), dma((8,)), dma((8,)), dma((4,)), dma((4,)), dma((16,)), dma((16,))],
@@ -731,23 +723,21 @@
     )(p)
 
 
-def flat_kernel(i_ref, o_ref):
-    for d in range(16):
-        for b in range(2):
-            start = (2 * d + b) * GB
-            o_ref[:, start:start + GB] = i_ref[d, :, b * 384:b * 384 + GB]
-
-
-def flatten(slices):
-    rows = 64
+def turn_kernel(i_ref, o_ref):
+    for k in range(i_ref.shape[0] // 128):
+        o_ref[:, k * 128:(k + 1) * 128] = i_ref[k * 128:(k + 1) * 128, :].T
+
+
+def turn(slices):
+    step = FF // 2
     return pl.pallas_call(
-        flat_kernel,
+        turn_kernel,
         out_shape=jax.ShapeDtypeStruct((256, FF), jnp.bfloat16),
-        grid=(256 // rows,),
-        in_specs=[pl.BlockSpec((16, rows, 768), lambda i: (0, i, 0))],
-        out_specs=pl.BlockSpec((rows, FF), lambda i: (i, 0)),
+        grid=(2, 2),
+        in_specs=[pl.BlockSpec((step, 128), lambda i, j: (j, i))],
+        out_specs=pl.BlockSpec((128, step), lambda i, j: (i, j)),
         compiler_params=pltpu.CompilerParams(vmem_limit_bytes=VLIM),
-        name="flatten",
+        name="turn",
     )(slices)
 
 
@@ -756,7 +746,7 @@
     gx, gy, tr = grams(acts, grads_out, sib_acts, sib_grads)
     fg, fa, tr = reduce_all(gx, gy, tr)
     p = solve(fg.reshape(2, 512, 128), fa.reshape(256, 128), tr, weight_grad.T)
-    return flatten(gather(p))
+    return turn(gather(p).reshape(FF, 256))
 
 
 def solution(mesh):

time: 164 us -> 153 us (0.933)
  Pallas kernels: 162 us -> 152 us
    pallas_call x4, Pallas kernels: 145 us -> 135 us  [the longest x1 64.1 us: reduce_all(): pl.pallas_call(reduce_kernel, out_shape=(jax.ShapeDtypeStruct((2, NB, 8,...]
where the time goes in v4:
time: 153 us; the launch traced here: 152 us
  Pallas kernels  152 us (99%)
    pallas_call x1, Pallas kernels, reduce_all(): pl.pallas_call(reduce_kernel, out_shape=(jax.ShapeDtypeStruct((2, NB, 8,...  64.1 us
    pallas_call x1, Pallas kernels, gather(): pl.pallas_call(gather_kernel, out_shape=jax.ShapeDtypeStruct((16, 2 * GB,...  37.2 us
    pallas_call x1, Pallas kernels, solve(): pl.pallas_call(solve_kernel, out_shape=jax.ShapeDtypeStruct((2 * GB, 256)...  27.7 us
    pallas_call x1, Pallas kernels, grams(): pl.pallas_call(gram_kernel, out_shape=(shape, shape, jax.ShapeDtypeStruct...  9.22 us
    pallas_call x1, Pallas kernels, swap(): pl.pallas_call(swap_kernel, out_shape=(jax.ShapeDtypeStruct((rows, D // 2...  7.79 us
    pallas_call x1, Pallas kernels, turn(): pl.pallas_call(turn_kernel, out_shape=jax.ShapeDtypeStruct((256, FF), jnp...  6.14 us

profile of v4, /device:TPU:33, one launch (start us, length us, event | category | flops | bytes accessed | tf_op | source)
XLA Modules:
  0.0 152.2 jit_solution(15101582648104667999)
XLA Ops:
  0.0 7.8 %swap.1 = (bf16[224,2048]{1,0:T(8,128)(2,1)}, bf16[224,7168]{1,0:T(8,128)(2,1)}) custom-call(bf16[224,4096]{1,0:T(8,128)(2,1)} %a_ref.3, bf16[224,11008]{1,0:T(8,128)(2,1)} %g_ref.3), custom_call_target="tpu_custom_call" | custom-call | tf_op jit(solution)/shard_map/swap/pallas_call | solution.py:75
  7.8 9.2 %grams.1 = (f32[2,16,160,128]{3,2,1,0:T(8,128)}, f32[2,16,160,128]{3,2,1,0:T(8,128)}, f32[16,128]{1,0:T(8,128)}) custom-call(bf16[224,4096]{1,0:T(8,128)(2,1)} %a_ref.3, bf16[224,11008]{1,0:T(8,128)(2,1)} %g_ref.3, bf16[224,2048]{1,0:T(8,128)(2,1)} %get-tuple-element.13.as_ref, bf16[224,7168]{1,0:T(8,128)(2,1)} %get-tuple-element.14.gs_ref), custom_call_target="tpu_custom_call" | custom-call | tf_op jit(solution)/shard_map/grams/pallas_call | solution.py:188
  17.0 64.1 %reduce_all.1 = (f32[2,2,8,32,128]{4,3,2,1,0:T(8,128)}, f32[2,2,8,8,128]{4,3,2,1,0:T(8,128)}, f32[16,128]{1,0:T(8,128)}) custom-call(f32[2,16,160,128]{3,2,1,0:T(8,128)} %get-tuple-element.15.gx, f32[2,16,160,128]{3,2,1,0:T(8,128)} %get-tuple-element.16.gy, f32[16,128]{1,0:T(8,128)} %get-tuple-element.17.tr), custom_call_target="tpu_custom_call" | custom-call | tf_op jit(solution)/shard_map/reduce_all/pallas_call | solution.py:421
  81.1 27.7 %solve.1.p_ref = bf16[688,256]{1,0:T(8,128)(2,1)} custom-call(f32[2,512,128]{2,1,0:T(8,128)} %bitcast.5, f32[256,128]{1,0:T(8,128)} %bitcast.7, f32[16,128]{1,0:T(8,128)} %get-tuple-element.20.t_ref, bf16[688,256]{1,0:T(8,128)(2,1)} %bitcast.6), custom_call_target="tpu_custom_call" | custom-call | tf_op jit(solution)/shard_map/solve/pallas_call | solution.py:608
  108.8 37.2 %gather.1 = bf16[16,688,256]{2,1,0:T(8,128)(2,1)} custom-call(bf16[688,256]{1,0:T(8,128)(2,1)} %solve.1.p_ref), custom_call_target="tpu_custom_call" | custom-call | tf_op jit(solution)/shard_map/gather/pallas_call | solution.py:715
  146.0 6.1 %turn.1 = bf16[256,11008]{1,0:T(8,128)(2,1)} custom-call(bf16[11008,256]{1,0:T(8,128)(2,1)} %bitcast.4), custom_call_target="tpu_custom_call" | custom-call | tf_op jit(solution)/shard_map/turn/pallas_call | solution.py:733

commit v5 on v4

--- a/solution.py
+++ b/solution.py
@@ -15,7 +15,6 @@
 TOKENS = 57344
 DAMP = math.sqrt(0.03)
 MESH = pl.DeviceIdType.MESH
-HIGH = lax.Precision.HIGHEST
 F32 = jnp.float32
 NB = 2
 GROWS = 64 // NB
@@ -28,9 +27,9 @@
 CUT = (352, 336)
 
 
-def grad_position(p, part):
+def grad_position(p, part, core):
     y = p // 2
-    return 2 * part + (p + y) % 2, y
+    return 2 * part + (p + y + core) % 2, y
 
 
 def act_position(k, part):
@@ -167,7 +166,7 @@
         second = diag(t2)
         grad_sum += diag(t0) + second + jnp.sum(jnp.where(r[:88] == c[:88], t5, 0.0), axis=0, keepdims=True)
         tail = jnp.concatenate([pltpu.roll(t5[48:88], 40, 1), jnp.zeros((8, 128), F32)], axis=0)
-        where = grad_position(j // 2, j % 2)
+        where = grad_position(j // 2, j % 2, core)
         store_all(where, GROWS, 0, 0, g[128:256, 0:128])
         store_all(where, GROWS, 0, 128, jnp.where(r >= c, t0, t2))
         store_all(where, GROWS, 0, 256, g[256:344, 0:128])
@@ -218,7 +217,7 @@
     ys = [at(x, lax.rem(y + k, 4), z, core) for k in (1, 2, 3)]
     zs = [at(x, y, lax.rem(z + k, 8), core) for k in range(1, 8)]
     g_part, a_part = x // 2, y // 2
-    unit_zh = lax.rem(x + y, 2)
+    unit_zh = lax.rem(x + y + core, 2)
     unit_zl = 2 * core + lax.rem(y, 2)
     g_on = zh == unit_zh
     a_on = zl == unit_zl
@@ -366,38 +365,41 @@
 
     batches = range(NB)
     q = begin([remote(tr, q1.at[k], ts.at[k], tr_sem.at[k], xs[k]) for k in range(3)])
-    second, third = [], []
-    first = [plane(0)]
+    first, second, third = {}, {}, {}
+    first[0] = plane(0)
     plane_pass(0, first[0])
-    for b in batches:
-        if b + 1 < NB:
-            first.append(plane(b + 1))
-        plane_sum(b, first[b])
-        second.append(cross(b))
-        if b + 1 < NB:
-            plane_pass(b + 1, first[b + 1])
+    first[1] = plane(1)
+    plane_sum(0, first[0])
+    second[0] = cross(0)
     end(q)
     t1[...] = (tr[...] + q1[0]) + (q1[1] + q1[2])
     q = begin([remote(t1, q2.at[k], ts.at[3 + k], tr_sem.at[3 + k], ys[k]) for k in range(3)])
-    for b in batches:
-        end(second[b])
-        cross_sum(b)
-        third.append(along(b))
+    plane_pass(1, first[1])
+    end(second[0])
+    cross_sum(0)
+    third[0] = along(0)
     end(q)
     t2[...] = (t1[...] + q2[0]) + (q2[1] + q2[2])
     q = begin([remote(t2, q3.at[k], ts.at[6 + k], tr_sem.at[6 + k], zs[k]) for k in range(7)])
-    for b in batches:
-        end(third[b])
-        along_sum(b)
-        spread(b)
+    plane_sum(1, first[1])
+    second[1] = cross(1)
+    end(third[0])
+    along_sum(0)
+    spread(0)
     end(q)
     trace = t2[...]
     for k in range(7):
         trace += q3[k]
     t3[...] = trace
     q = begin([remote(t3, q4, ts.at[13], tr_sem.at[13], (sib, own))])
-    for b in batches:
-        give(b)
+    end(second[1])
+    cross_sum(1)
+    third[1] = along(1)
+    give(0)
+    end(third[1])
+    along_sum(1)
+    spread(1)
+    give(1)
     end(q)
     tt[core] = t3[...]
     tt[1 - core] = q4[...]
@@ -438,10 +440,6 @@
     )(gx, gy, tr)
 
 
-def dot(a, b, ca=1, cb=0):
-    return lax.dot_general(a, b, (((ca,), (cb,)), ((), ())), precision=HIGH, preferred_element_type=F32)
-
-
 def split(v):
     high = v.astype(jnp.bfloat16).astype(F32)
     rest = v - high
@@ -449,12 +447,12 @@
     return high, mid, rest - mid
 
 
-def outer(a, b):
+def dot(a, b, ca=1, cb=0):
     ah, am, al = split(a)
     bh, bm, bl = split(b)
-    left = jnp.concatenate([ah, ah, am, ah, am, al], axis=0).astype(jnp.bfloat16)
-    right = jnp.concatenate([bh, bm, bh, bl, bm, bh], axis=0).astype(jnp.bfloat16)
-    return lax.dot_general(left, right, (((0,), (0,)), ((), ())), preferred_element_type=F32)
+    left = jnp.concatenate([ah, ah, am, ah, am, al], axis=ca).astype(jnp.bfloat16)
+    right = jnp.concatenate([bh, bm, bh, bl, bm, bh], axis=cb).astype(jnp.bfloat16)
+    return lax.dot_general(left, right, (((ca,), (cb,)), ((), ())), preferred_element_type=F32)
 
 
 def sweep_four(now, at, row, sub, lane):
@@ -493,7 +491,8 @@
     return out
 
 
-def sweep_tiles(refs, panels):
+def sweep_tiles(refs, panels, others=()):
+    others = list(others)
     sub = lax.broadcasted_iota(jnp.int32, (8, 128), 0)
     lane = lax.broadcasted_iota(jnp.int32, (8, 128), 1)
     lane_all = lax.broadcasted_iota(jnp.int32, (128, 128), 1)
@@ -504,11 +503,15 @@
         news = [sweep_four(old, base, 0, sub, lane) for old in olds]
         news = [sweep_four(new, base + 4, 4, sub, lane) for new in news]
         for ref, old, new in zip(refs, olds, news):
-            ref[...] = jnp.where(inside, 0.0, ref[...]) - outer(old, new)
+            ref[...] = jnp.where(inside, 0.0, ref[...]) - dot(old, new, 0, 0)
             ref[base:base + 8, :] = new
-
-
-def solve_kernel(fg_ref, fa_ref, t_ref, w_ref, p_ref, g_ref, a_ref, gi_ref, ai_ref):
+        count = -(-len(others) // (panels - p))
+        for step in others[:count]:
+            step()
+        others = others[count:]
+
+
+def solve_kernel(fg_ref, fa_ref, t_ref, w_ref, p_ref, g_ref, a_ref, l_ref, x_ref, ai_ref):
     act_trace = jnp.sum(t_ref[0:1, :], keepdims=True) / TOKENS
     grad_trace = jnp.sum(t_ref[1:2, :], keepdims=True) / TOKENS
     ratio = jnp.sqrt(act_trace / D / (grad_trace / FF))
@@ -548,58 +551,84 @@
     gs = [[g_ref.at[b * 6 + t] for t in range(6)] for b in range(2)]
     am = [a_ref.at[t] for t in range(3)]
     sweep_tiles([gs[0][0], gs[1][0], am[0]], 16)
-    for m in gs:
-        neg = m[0][...]
-        a10, a20 = m[1][...], m[3][...]
-        v10, v20 = -dot(a10, neg), -dot(a20, neg)
-        m[2][...] -= dot(v10, a10, 1, 1)
-        m[4][...] -= dot(v20, a10, 1, 1)
-        m[5][...] -= dot(v20, a20, 1, 1)
-        m[1][...] = v10
-        m[3][...] = v20
-    a10 = am[1][...]
-    v10 = -dot(a10, am[0][...])
-    am[2][...] -= dot(v10, a10, 1, 1)
-    am[1][...] = v10
-    sweep_tiles([gs[0][2], gs[1][2], am[2]], 16)
-    for m in gs:
-        neg = m[2][...]
-        a10, a21 = m[1][...], m[4][...]
-        v10, v21 = -dot(neg, a10), -dot(a21, neg)
-        m[0][...] -= dot(a10, v10, 0, 0)
-        m[3][...] -= dot(a21, v10)
-        m[5][...] -= dot(v21, a21, 1, 1)
-        m[1][...] = v10
-        m[4][...] = v21
-    a10 = am[1][...]
-    v10 = -dot(am[2][...], a10)
-    am[0][...] -= dot(a10, v10, 0, 0)
-    am[1][...] = v10
-    sweep_tiles([gs[0][5], gs[1][5]], last // 8)
-    for m in gs:
-        neg = m[5][...]
-        a20, a21 = m[3][...], m[4][...]
-        v20, v21 = -dot(neg, a20), -dot(neg, a21)
-        m[0][...] -= dot(a20, v20, 0, 0)
-        m[1][...] -= dot(a21, v20, 0, 0)
-        m[2][...] -= dot(a21, v21, 0, 0)
-        m[3][...] = v20
-        m[4][...] = v21
-    ai_ref[0:128, 0:128] = -am[0][...]
-    ai_ref[128:256, 0:128] = -am[1][...]
-    ai_ref[0:128, 128:256] = -am[1][...].T
-    ai_ref[128:256, 128:256] = -am[2][...]
+    for m in gs + [am]:
+        a10 = m[1][...]
+        l10 = -dot(a10, m[0][...])
+        m[2][...] -= dot(l10, a10, 1, 1)
+        l_ref[0 if m is gs[0] else 1 if m is gs[1] else 2] = l10
+
+    def row_two(b):
+        m = gs[b]
+        a20 = m[3][...]
+
+        def lower():
+            l_ref[3 + b] = -dot(a20, m[0][...])
+
+        def side():
+            m[4][...] -= dot(l_ref[3 + b], m[1][...], 1, 1)
+
+        def corner():
+            m[5][...] -= dot(l_ref[3 + b], a20, 1, 1)
+        return [lower, side, corner]
+
+    steps = [step for pair_of in zip(row_two(0), row_two(1)) for step in pair_of]
+    sweep_tiles([gs[0][2], gs[1][2], am[2]], 16, steps)
     for b, m in enumerate(gs):
-        for t, (i, j) in enumerate(((0, 0), (1, 0), (1, 1), (2, 0), (2, 1), (2, 2))):
-            tile = -m[t][...]
-            gi_ref[b, i * 128:(i + 1) * 128, j * 128:(j + 1) * 128] = tile
-            if i != j:
-                gi_ref[b, j * 128:(j + 1) * 128, i * 128:(i + 1) * 128] = tile.T
+        a21 = m[4][...]
+        l21 = -dot(a21, m[2][...])
+        m[5][...] -= dot(l21, a21, 1, 1)
+        l_ref[5 + b] = l21
+
+    def act_cross():
+        v10 = -dot(am[2][...], l_ref[2])
+        ai_ref[128:256, 0:128] = -v10
+        ai_ref[0:128, 128:256] = -v10.T
+        ai_ref[128:256, 128:256] = -am[2][...]
+
+    def act_first():
+        ai_ref[0:128, 0:128] = -am[0][...] - dot(l_ref[2], ai_ref[128:256, 0:128], 0, 0)
+
+    def right_side(b):
+        w = w_ref[...].astype(F32)[b * GB:(b + 1) * GB]
+        w = jnp.concatenate([w, jnp.zeros((384 - GB, 256), F32)], axis=0).astype(jnp.bfloat16)
+        pieces = jnp.concatenate(split(ai_ref[...]), axis=0).astype(jnp.bfloat16)
+        x_ref[b] = jnp.dot(jnp.concatenate([w, w, w], axis=1), pieces, preferred_element_type=F32)
+
+    def through(b):
+        x = [x_ref.at[b, pl.ds(128 * i, 128)] for i in range(3)]
+        l10, l20, l21 = l_ref.at[b], l_ref.at[3 + b], l_ref.at[5 + b]
+        m = gs[b]
+
+        def one():
+            x[1][...] -= dot(l10[...], x[0][...])
+
+        def two():
+            x[2][...] -= dot(l20[...], x[0][...])
+
+        def three():
+            x[2][...] -= dot(l21[...], x[1][...])
+
+        def four():
+            x[1][...] = -dot(m[2][...], x[1][...])
+
+        def five():
+            x[0][...] = -dot(m[0][...], x[0][...])
+
+        def six():
+            x[0][...] -= dot(l10[...], x[1][...], 0, 0)
+
+        def seven():
+            l20[...] -= dot(l21[...], l10[...])
+        return [one, two, three, four, five, six, seven]
+
+    steps = [act_cross, act_first, lambda: right_side(0), lambda: right_side(1)]
+    steps += [step for pair_of in zip(through(0), through(1)) for step in pair_of]
+    sweep_tiles([gs[0][5], gs[1][5]], last // 8, steps)
     out = []
-    for b in range(2):
-        w = w_ref[...].astype(F32)[b * GB:(b + 1) * GB]
-        w = jnp.concatenate([w, jnp.zeros((384 - GB, 256), F32)], axis=0)
-        out.append(dot(gi_ref[b], dot(w, ai_ref[...]))[0:GB])
+    for b, m in enumerate(gs):
+        y2 = -dot(m[5][...], x_ref[b, 256:384])
+        out += [x_ref[b, 0:128] - dot(l_ref[3 + b], y2, 0, 0),
+                x_ref[b, 128:256] - dot(l_ref[5 + b], y2, 0, 0), y2[0:last]]
     p_ref[...] = jnp.concatenate(out, axis=0).astype(jnp.bfloat16)
 
 
@@ -611,7 +640,8 @@
         in_specs=[vmem] * 4,
         out_specs=vmem,
         scratch_shapes=[pltpu.VMEM((12, 128, 128), F32), pltpu.VMEM((3, 128, 128), F32),
-                        pltpu.VMEM((2, 384, 384), F32), pltpu.VMEM((256, 256), F32)],
+                        pltpu.VMEM((7, 128, 128), F32), pltpu.VMEM((2, 384, 256), F32),
+                        pltpu.VMEM((256, 256), F32)],
         compiler_params=pltpu.CompilerParams(vmem_limit_bytes=VLIM),
         name="solve",
     )(fg, fa, tr, w)

time: 153 us -> 146 us (0.954)
  Pallas kernels: 152 us -> 144 us
    pallas_call x1, Pallas kernels: 64.1 us -> 59.6 us  [reduce_all(): pl.pallas_call(reduce_kernel, out_shape=(jax.ShapeDtypeStruct((2, NB, 8,...]
    pallas_call x1, Pallas kernels: 27.7 us -> 25.1 us  [solve(): pl.pallas_call(solve_kernel, out_shape=jax.ShapeDtypeStruct((2 * GB, 256)...]
where the time goes in v5:
time: 146 us; the launch traced here: 144 us
  Pallas kernels  144 us (99%)
    pallas_call x1, Pallas kernels, reduce_all(): pl.pallas_call(reduce_kernel, out_shape=(jax.ShapeDtypeStruct((2, NB, 8,...  59.6 us
    pallas_call x1, Pallas kernels, gather(): pl.pallas_call(gather_kernel, out_shape=jax.ShapeDtypeStruct((16, 2 * GB,...  36 us
    pallas_call x1, Pallas kernels, solve(): pl.pallas_call(solve_kernel, out_shape=jax.ShapeDtypeStruct((2 * GB, 256)...  25.1 us
    pallas_call x1, Pallas kernels, grams(): pl.pallas_call(gram_kernel, out_shape=(shape, shape, jax.ShapeDtypeStruct...  9.22 us
    pallas_call x1, Pallas kernels, swap(): pl.pallas_call(swap_kernel, out_shape=(jax.ShapeDtypeStruct((rows, D // 2...  7.79 us
    pallas_call x1, Pallas kernels, turn(): pl.pallas_call(turn_kernel, out_shape=jax.ShapeDtypeStruct((256, FF), jnp...  6.14 us

profile of v5, /device:TPU:33, one launch (start us, length us, event | category | flops | bytes accessed | tf_op | source)
XLA Modules:
  0.0 143.9 jit_solution(11831614350675437238)
XLA Ops:
  0.0 7.8 %swap.1 = (bf16[224,2048]{1,0:T(8,128)(2,1)}, bf16[224,7168]{1,0:T(8,128)(2,1)}) custom-call(bf16[224,4096]{1,0:T(8,128)(2,1)} %a_ref.3, bf16[224,11008]{1,0:T(8,128)(2,1)} %g_ref.3), custom_call_target="tpu_custom_call" | custom-call | tf_op jit(solution)/shard_map/swap/pallas_call | solution.py:74
  7.8 9.2 %grams.1 = (f32[2,16,160,128]{3,2,1,0:T(8,128)}, f32[2,16,160,128]{3,2,1,0:T(8,128)}, f32[16,128]{1,0:T(8,128)}) custom-call(bf16[224,4096]{1,0:T(8,128)(2,1)} %a_ref.3, bf16[224,11008]{1,0:T(8,128)(2,1)} %g_ref.3, bf16[224,2048]{1,0:T(8,128)(2,1)} %get-tuple-element.13.as_ref, bf16[224,7168]{1,0:T(8,128)(2,1)} %get-tuple-element.14.gs_ref), custom_call_target="tpu_custom_call" | custom-call | tf_op jit(solution)/shard_map/grams/pallas_call | solution.py:187
  17.0 59.6 %reduce_all.1 = (f32[2,2,8,32,128]{4,3,2,1,0:T(8,128)}, f32[2,2,8,8,128]{4,3,2,1,0:T(8,128)}, f32[16,128]{1,0:T(8,128)}) custom-call(f32[2,16,160,128]{3,2,1,0:T(8,128)} %get-tuple-element.15.gx, f32[2,16,160,128]{3,2,1,0:T(8,128)} %get-tuple-element.16.gy, f32[16,128]{1,0:T(8,128)} %get-tuple-element.17.tr), custom_call_target="tpu_custom_call" | custom-call | tf_op jit(solution)/shard_map/reduce_all/pallas_call | solution.py:423
  76.6 25.1 %solve.1.p_ref = bf16[688,256]{1,0:T(8,128)(2,1)} custom-call(f32[2,512,128]{2,1,0:T(8,128)} %bitcast.5, f32[256,128]{1,0:T(8,128)} %bitcast.7, f32[16,128]{1,0:T(8,128)} %get-tuple-element.20.t_ref, bf16[688,256]{1,0:T(8,128)(2,1)} %bitcast.6), custom_call_target="tpu_custom_call" | custom-call | tf_op jit(solution)/shard_map/solve/pallas_call | solution.py:637
  101.7 36.0 %gather.1 = bf16[16,688,256]{2,1,0:T(8,128)(2,1)} custom-call(bf16[688,256]{1,0:T(8,128)(2,1)} %solve.1.p_ref), custom_call_target="tpu_custom_call" | custom-call | tf_op jit(solution)/shard_map/gather/pallas_call | solution.py:745
  137.8 6.1 %turn.1 = bf16[256,11008]{1,0:T(8,128)(2,1)} custom-call(bf16[11008,256]{1,0:T(8,128)(2,1)} %bitcast.4), custom_call_target="tpu_custom_call" | custom-call | tf_op jit(solution)/shard_map/turn/pallas_call | solution.py:763

commit v6 on v5

--- a/solution.py
+++ b/solution.py
@@ -46,67 +46,39 @@
     return dp, own
 
 
-def swap_kernel(a_ref, g_ref, ao_ref, go_ref, send, recv):
-    dp, own = place()
-    core = lax.rem(dp, 2)
-    sib = dp + 1 - 2 * core
-    barrier = pltpu.get_barrier_semaphore()
-    pl.semaphore_signal(barrier, inc=1, device_id=(sib, own), device_id_type=MESH)
-    pl.semaphore_wait(barrier, 1)
-    width = ao_ref.shape[1]
-    pieces = [(a_ref.at[:, pl.ds(pl.multiple_of((1 - core) * width, 128), width)], ao_ref)]
-    for p in range(8):
-        start = pl.multiple_of(window(2 * p + 1 - core), 128)
-        pieces.append((g_ref.at[:, pl.ds(start, WIDTHS[p])], go_ref.at[:, pl.ds(p * WIN, WIDTHS[p])]))
-    copies = []
-    for i, (src, dst) in enumerate(pieces):
-        copy = pltpu.make_async_remote_copy(
-            src_ref=src, dst_ref=dst, send_sem=send.at[i], recv_sem=recv.at[i],
-            device_id=(sib, own), device_id_type=MESH)
-        copy.start()
-        copies.append(copy)
-    for copy in copies:
-        copy.wait()
-
-
-def swap(acts, grads):
-    rows = acts.shape[0]
-    return pl.pallas_call(
-        swap_kernel,
-        out_shape=(jax.ShapeDtypeStruct((rows, D // 2), acts.dtype),
-                   jax.ShapeDtypeStruct((rows, 8 * WIN), acts.dtype)),
-        in_specs=[pl.BlockSpec(memory_space=pl.ANY)] * 2,
-        out_specs=(pl.BlockSpec(memory_space=pl.ANY),) * 2,
-        scratch_shapes=[pltpu.SemaphoreType.DMA((9,))] * 2,
-        compiler_params=pltpu.CompilerParams(collective_id=0, has_side_effects=True),
-        name="swap",
-    )(acts, grads)
-
-
 def gram(block):
     return lax.dot_general(block, block, (((0,), (0,)), ((), ())), preferred_element_type=F32)
 
 
-def gram_kernel(a_ref, g_ref, as_ref, gs_ref, x_out, y_out, t_ref, abuf, gbuf, even, x_ref, y_ref, sems, out_sems):
-    core = lax.rem(lax.axis_index("dp"), 2)
+def fetch(a_ref, g_ref, abuf, gbuf, core, sibling, sems, send, recv):
     rows = a_ref.shape[0]
     mine, theirs = pl.ds(0, rows), pl.ds(rows, rows)
     width = abuf.shape[1]
-    moves = [[(a_ref.at[:, pl.ds(pl.multiple_of(core * width, 128), width)], abuf.at[mine]), (as_ref, abuf.at[theirs])]]
-    for lo in (0, 4):
-        group = []
-        for p in range(lo, lo + 4):
-            start = pl.multiple_of(window(2 * p + core), 128)
-            group.append((g_ref.at[:, pl.ds(start, WIDTHS[p])], gbuf.at[mine, pl.ds(p * WIN, WIDTHS[p])]))
-        span = pl.ds(lo * WIN, 4 * WIN - WIN + WIDTHS[lo + 3])
-        group.append((gs_ref.at[:, span], gbuf.at[theirs, span]))
-        moves.append(group)
-    copies = []
-    for i, group in enumerate(moves):
-        copies.append([pltpu.make_async_copy(src, dst, sems.at[i, n]) for n, (src, dst) in enumerate(group)])
-        for copy in copies[i]:
+
+    def half(c):
+        return a_ref.at[:, pl.ds(pl.multiple_of(c * width, 128), width)]
+
+    def columns(p, c):
+        return g_ref.at[:, pl.ds(pl.multiple_of(window(2 * p + c), 128), WIDTHS[p])]
+
+    here = [[(half(core), abuf.at[mine])], [], []]
+    away = [[(half(1 - core), abuf.at[theirs])], [], []]
+    for p in range(8):
+        at = pl.ds(p * WIN, WIDTHS[p])
+        here[1 + p // 4].append((columns(p, core), gbuf.at[mine, at]))
+        away[1 + p // 4].append((columns(p, 1 - core), gbuf.at[theirs, at]))
+    here = [[pltpu.make_async_copy(src, dst, sems.at[i, n]) for n, (src, dst) in enumerate(group)]
+            for i, group in enumerate(here)]
+    away = [[pltpu.make_async_remote_copy(src_ref=src, dst_ref=dst, send_sem=send.at[i, n], recv_sem=recv.at[i, n],
+                                          device_id=sibling, device_id_type=MESH)
+             for n, (src, dst) in enumerate(group)] for i, group in enumerate(away)]
+    for group in here:
+        for copy in group:
             copy.start()
-
+    return here, away
+
+
+def gram_step(copies, core, abuf, gbuf, even, x_ref, y_ref, t_ref):
     def store_all(where, size, lead, row, value):
         px, py = where
         done = 0
@@ -120,15 +92,6 @@
             else:
                 y_ref[batch, py * 4 + px, rows_at, :] = value[done:done + n]
             done += n
-
-    outs = []
-
-    def finish(where):
-        px, py = where
-        for i, (src, dst, at) in enumerate(((x_ref, x_out, px * 4 + py), (y_ref, y_out, py * 4 + px))):
-            copy = pltpu.make_async_copy(src.at[:, at], dst.at[:, at], out_sems.at[i, px * 4 + py])
-            copy.start()
-            outs.append(copy)
 
     r = lax.broadcasted_iota(jnp.int32, (128, 128), 0)
     c = lax.broadcasted_iota(jnp.int32, (128, 128), 1)
@@ -173,34 +136,12 @@
         store_all(where, GROWS, 0, 344, g[256:344, 128:256])
         store_all(where, GROWS, 0, 432, jnp.where(c[:48] < 88, t5[0:48], tail))
         store_all(where, GROWS, 0, 480, jnp.concatenate([second, jnp.zeros((31, 128), F32)], axis=0))
-        finish(where)
     t_ref[0:8, :] = jnp.concatenate([act_sum, grad_sum, jnp.zeros((6, 128), F32)], axis=0)
-    for copy in outs:
-        copy.wait()
-
-
-def grams(acts, grads, sib_acts, sib_grads):
-    shape = jax.ShapeDtypeStruct((NB, 16, HALF, 128), F32)
-    vmem = pl.BlockSpec(memory_space=pltpu.VMEM)
-    anywhere = pl.BlockSpec(memory_space=pl.ANY)
-    rows = acts.shape[0]
-    return pl.pallas_call(
-        gram_kernel,
-        out_shape=(shape, shape, jax.ShapeDtypeStruct((16, 128), F32)),
-        in_specs=[anywhere] * 4,
-        out_specs=(anywhere, anywhere, vmem),
-        scratch_shapes=[pltpu.VMEM((2 * rows, D // 2), acts.dtype), pltpu.VMEM((2 * rows, 8 * WIN), acts.dtype),
-                        pltpu.VMEM((16, 2 * rows, 384), acts.dtype),
-                        pltpu.VMEM(shape.shape, F32), pltpu.VMEM(shape.shape, F32),
-                        pltpu.SemaphoreType.DMA((3, 5)), pltpu.SemaphoreType.DMA((2, 16))],
-        compiler_params=pltpu.CompilerParams(vmem_limit_bytes=VLIM),
-        name="grams",
-    )(acts, grads, sib_acts, sib_grads)
-
-
-def reduce_kernel(gx, gy, tr, fg, fa, t_out,
-                  ps, pk, pm, pr, rx2, ry2, st, rz, fin, ga, aa, t1, t2, t3, q1, q2, q3, q4, tt,
-                  local, s1, r1, s2, r2, s3, r3, s4, rg4, ra4, s5, rg5, ra5, ts, tr_sem):
+
+
+def reduce_kernel(a_ref, g_ref, fg, fa, t_out,
+                  abuf, gbuf, even, gx, gy, tr, ps, pk, pm, pr, rx2, ry2, st, rz, fin, ga, aa, t1, t2, t3, q1, q2, q3, q4, tt,
+                  local, s0, r0, s1, r1, s2, r2, s3, r3, s4, rg4, ra4, s5, rg5, ra5, ts, tr_sem):
     dp, own = place()
     core = lax.rem(dp, 2)
     zh = lax.rem(dp // 2, 2)
@@ -223,10 +164,15 @@
     a_on = zl == unit_zl
     across = [at(x, lax.rem(y + k, 4), z, 1 - core) for k in range(4)]
 
+    here, away = fetch(a_ref, g_ref, abuf, gbuf, core, (sib, own), local, s0, r0)
     barrier = pltpu.get_barrier_semaphore()
     for device in xs + ys + zs + across:
         pl.semaphore_signal(barrier, inc=1, device_id=device, device_id_type=MESH)
     pl.semaphore_wait(barrier, 17)
+    for group in away:
+        for copy in group:
+            copy.start()
+    gram_step([h + a for h, a in zip(here, away)], core, abuf, gbuf, even, gx, gy, tr)
 
     def remote(src, dst, ssem, rsem, device):
         return pltpu.make_async_remote_copy(src_ref=src, dst_ref=dst, send_sem=ssem, recv_sem=rsem,
@@ -246,29 +192,27 @@
     def plane(b):
         copies = []
         for a, g, me, (up, down) in axes:
-            over, under, opposite = lax.rem(me + 1, 4) * 4, lax.rem(me + 3, 4) * 4, lax.rem(me + 2, 4) * 4
+            opposite = lax.rem(me + 2, 4) * 4
             copies.append(remote(g.at[b, pl.ds(opposite, 2)], pm.at[a, b, 0], s1.at[a, b, 0], r1.at[a, b, 0], up))
             copies.append(remote(g.at[b, pl.ds(opposite + 2, 2)], pm.at[a, b, 1],
                                  s1.at[a, b, 1], r1.at[a, b, 1], down))
-            copies.append(pltpu.make_async_copy(g.at[b, pl.ds(over, 2)], pk.at[a, b, 0], local.at[a, b, 0]))
-            copies.append(pltpu.make_async_copy(g.at[b, pl.ds(under + 2, 2)], pk.at[a, b, 1], local.at[a, b, 1]))
         for a, g, me, (up, down) in axes:
             over, under = lax.rem(me + 1, 4) * 4, lax.rem(me + 3, 4) * 4
             copies.append(remote(g.at[b, pl.ds(over + 2, 2)], pr.at[a, b, 0, pl.ds(2, 2)],
                                  s1.at[a, b, 2], r1.at[a, b, 2], up))
             copies.append(remote(g.at[b, pl.ds(under, 2)], pr.at[a, b, 1, pl.ds(0, 2)],
                                  s1.at[a, b, 3], r1.at[a, b, 3], down))
-            copies.append(pltpu.make_async_copy(g.at[b, pl.ds(me * 4, 4)], ps.at[a, b], local.at[a, b, 2]))
         return begin(copies)
 
     def plane_pass(b, copies):
-        end(copies[:8])
+        end(copies[:4])
         @pl.loop(0, 8)
         def _(i):
             h, rows = i // 4, pl.ds(pl.multiple_of(lax.rem(i, 4) * CH, 8), CH)
-            for a in range(2):
-                for d in range(2):
-                    pk[a, b, d, h, rows, :] += pm[a, b, d, h, rows, :]
+            for a, g, me, _ in axes:
+                over, under = lax.rem(me + 1, 4) * 4, lax.rem(me + 3, 4) * 4
+                pk[a, b, 0, h, rows, :] = g[b, over + h, rows, :] + pm[a, b, 0, h, rows, :]
+                pk[a, b, 1, h, rows, :] = g[b, under + 2 + h, rows, :] + pm[a, b, 1, h, rows, :]
         for a, _, _, to in axes:
             for d in range(2):
                 copies.append(remote(pk.at[a, b, d], pr.at[a, b, d, pl.ds(2 * d, 2)],
@@ -276,12 +220,12 @@
                 copies[-1].start()
 
     def plane_sum(b, copies):
-        end(copies[8:])
+        end(copies[4:])
         @pl.loop(0, 16)
         def _(i):
             q, rows = i // 4, pl.ds(pl.multiple_of(lax.rem(i, 4) * CH, 8), CH)
-            for a in range(2):
-                ps[a, b, q, rows, :] += pr[a, b, 0, q, rows, :] + pr[a, b, 1, q, rows, :]
+            for a, g, me, _ in axes:
+                ps[a, b, q, rows, :] = g[b, me * 4 + q, rows, :] + (pr[a, b, 0, q, rows, :] + pr[a, b, 1, q, rows, :])
 
     def cross(b):
         copies = []
@@ -412,7 +356,8 @@
         given(b)
 
 
-def reduce_all(gx, gy, tr):
+def reduce_all(acts, grads):
+    rows = acts.shape[0]
     vmem = pl.BlockSpec(memory_space=pltpu.VMEM)
     dma = pltpu.SemaphoreType.DMA
     tile = pltpu.VMEM((16, 128), F32)
@@ -425,19 +370,22 @@
         out_shape=(jax.ShapeDtypeStruct((2, NB, 8, GROWS, 128), F32),
                    jax.ShapeDtypeStruct((2, NB, 8, AROWS, 128), F32),
                    jax.ShapeDtypeStruct((16, 128), F32)),
-        in_specs=[pl.BlockSpec(memory_space=pl.ANY)] * 2 + [vmem],
+        in_specs=[pl.BlockSpec(memory_space=pl.ANY)] * 2,
         out_specs=(vmem,) * 3,
         scratch_shapes=[
+            pltpu.VMEM((2 * rows, D // 2), acts.dtype), pltpu.VMEM((2 * rows, 8 * WIN), acts.dtype),
+            pltpu.VMEM((16, 2 * rows, 384), acts.dtype),
+            buf(NB, 16, HALF), buf(NB, 16, HALF), tile,
             buf(2, NB, 4, HALF), buf(2, NB, 2, 2, HALF), buf(2, NB, 2, 2, HALF), buf(2, NB, 2, 4, HALF),
             buf(NB, 3, HALF), buf(NB, 3, HALF), buf(NB, 8, CH), buf(NB, 7, CH), buf(NB, CH),
             buf(NB, 8, GROWS), buf(NB, 8, AROWS),
             tile, tile, tile, buf(3, 16), buf(3, 16), buf(7, 16), tile, buf(2, 16),
-            dma((2, NB, 3)), dma((2, NB, 6)), dma((2, NB, 6)), dma((NB, 6)), dma((NB, 6)), dma((NB, 7)), dma((NB, 7)),
+            dma((3, 4)), dma((3, 4)), dma((3, 4)), dma((2, NB, 6)), dma((2, NB, 6)), dma((NB, 6)), dma((NB, 6)), dma((NB, 7)), dma((NB, 7)),
             dma((NB, 6)), dma((NB, 8)), dma((NB, 8)), dma((NB, 10)), dma((NB, 2)), dma((NB, 2)), dma((14,)), dma((14,)),
         ],
         compiler_params=pltpu.CompilerParams(collective_id=1, has_side_effects=True, vmem_limit_bytes=VLIM),
         name="reduce_all",
-    )(gx, gy, tr)
+    )(acts, grads)
 
 
 def split(v):
@@ -772,9 +720,7 @@
 
 
 def shards(acts, grads_out, weight_grad):
-    sib_acts, sib_grads = swap(acts, grads_out)
-    gx, gy, tr = grams(acts, grads_out, sib_acts, sib_grads)
-    fg, fa, tr = reduce_all(gx, gy, tr)
+    fg, fa, tr = reduce_all(acts, grads_out)
     p = solve(fg.reshape(2, 512, 128), fa.reshape(256, 128), tr, weight_grad.T)
     return turn(gather(p).reshape(FF, 256))
 

time: 146 us -> 140 us (0.959)
  the two profiles are of different devices: /device:TPU:33 before, /device:TPU:1 now
where the time goes in v6:
time: 140 us
  Pallas kernels  140 us (100%)
    pallas_call x1, Pallas kernels, reduce_all(): pl.pallas_call(reduce_kernel, out_shape=(jax.ShapeDtypeStruct((2, NB, 8,...  72.6 us
    pallas_call x1, Pallas kernels, gather(): pl.pallas_call(gather_kernel, out_shape=jax.ShapeDtypeStruct((16, 2 * GB,...  35.8 us
    pallas_call x1, Pallas kernels, solve(): pl.pallas_call(solve_kernel, out_shape=jax.ShapeDtypeStruct((2 * GB, 256)...  25.1 us
    pallas_call x1, Pallas kernels, turn(): pl.pallas_call(turn_kernel, out_shape=jax.ShapeDtypeStruct((256, FF), jnp...  6.14 us

profile of v6, /device:TPU:1, one launch (start us, length us, event | category | flops | bytes accessed | tf_op | source)
XLA Modules:
  0.0 139.6 jit_solution(16508029034106607915)
XLA Ops:
  0.0 72.6 %reduce_all.1 = (f32[2,2,8,32,128]{4,3,2,1,0:T(8,128)}, f32[2,2,8,8,128]{4,3,2,1,0:T(8,128)}, f32[16,128]{1,0:T(8,128)}) custom-call(bf16[224,4096]{1,0:T(8,128)(2,1)} %a_ref.1, bf16[224,11008]{1,0:T(8,128)(2,1)} %g_ref.1), custom_call_target="tpu_custom_call" | custom-call | tf_op jit(solution)/shard_map/reduce_all/pallas_call | solution.py:368
  72.6 25.1 %solve.1.p_ref = bf16[688,256]{1,0:T(8,128)(2,1)} custom-call(f32[2,512,128]{2,1,0:T(8,128)} %bitcast.5, f32[256,128]{1,0:T(8,128)} %bitcast.7, f32[16,128]{1,0:T(8,128)} %get-tuple-element.10.t_ref, bf16[688,256]{1,0:T(8,128)(2,1)} %bitcast.6), custom_call_target="tpu_custom_call" | custom-call | tf_op jit(solution)/shard_map/solve/pallas_call | solution.py:585
  97.7 35.8 %gather.1 = bf16[16,688,256]{2,1,0:T(8,128)(2,1)} custom-call(bf16[688,256]{1,0:T(8,128)(2,1)} %solve.1.p_ref), custom_call_target="tpu_custom_call" | custom-call | tf_op jit(solution)/shard_map/gather/pallas_call | solution.py:693
  133.5 6.1 %turn.1 = bf16[256,11008]{1,0:T(8,128)(2,1)} custom-call(bf16[11008,256]{1,0:T(8,128)(2,1)} %bitcast.4), custom_call_target="tpu_custom_call" | custom-call | tf_op jit(solution)/shard_map/turn/pallas_call | solution.py:711

commit v7 on v6

--- a/solution.py
+++ b/solution.py
@@ -122,21 +122,30 @@
                         d = i // 2 * 2 + odd
                         start = i // 2 * WIN + 2 * GB * d - window(d) + i % 2 * GB
                         even[i, :, 0:GB] = gbuf[:, start:start + GB]
-        block = even[j, :, 0:GB]
-        g = lax.dot_general(block, block[:, 0:256], (((0,), (0,)), ((), ())), preferred_element_type=F32)
+        g = gram(even[j, :, 0:256])
         t0, t2 = g[0:128, 0:128], g[128:256, 128:256]
-        t5 = jnp.concatenate([gram(block[:, 256:GB]), jnp.zeros((88, 40), F32)], axis=1)
         second = diag(t2)
-        grad_sum += diag(t0) + second + jnp.sum(jnp.where(r[:88] == c[:88], t5, 0.0), axis=0, keepdims=True)
-        tail = jnp.concatenate([pltpu.roll(t5[48:88], 40, 1), jnp.zeros((8, 128), F32)], axis=0)
+        grad_sum += diag(t0) + second
         where = grad_position(j // 2, j % 2, core)
         store_all(where, GROWS, 0, 0, g[128:256, 0:128])
         store_all(where, GROWS, 0, 128, jnp.where(r >= c, t0, t2))
-        store_all(where, GROWS, 0, 256, g[256:344, 0:128])
-        store_all(where, GROWS, 0, 344, g[256:344, 128:256])
-        store_all(where, GROWS, 0, 432, jnp.where(c[:48] < 88, t5[0:48], tail))
         store_all(where, GROWS, 0, 480, jnp.concatenate([second, jnp.zeros((31, 128), F32)], axis=0))
-    t_ref[0:8, :] = jnp.concatenate([act_sum, grad_sum, jnp.zeros((6, 128), F32)], axis=0)
+
+    def rest():
+        corner_sum = grad_sum
+        for j in range(16):
+            low = lax.dot_general(even[j, :, 256:GB], even[j, :, 0:GB], (((0,), (0,)), ((), ())),
+                                  preferred_element_type=F32)
+            t5 = jnp.concatenate([low[:, 256:GB], jnp.zeros((88, 40), F32)], axis=1)
+            corner_sum += jnp.sum(jnp.where(r[:88] == c[:88], t5, 0.0), axis=0, keepdims=True)
+            tail = jnp.concatenate([pltpu.roll(t5[48:88], 40, 1), jnp.zeros((8, 128), F32)], axis=0)
+            where = grad_position(j // 2, j % 2, core)
+            store_all(where, GROWS, 0, 256, low[:, 0:128])
+            store_all(where, GROWS, 0, 344, low[:, 128:256])
+            store_all(where, GROWS, 0, 432, jnp.where(c[:48] < 88, t5[0:48], tail))
+        t_ref[0:8, :] = jnp.concatenate([act_sum, corner_sum, jnp.zeros((6, 128), F32)], axis=0)
+
+    return rest
 
 
 def reduce_kernel(a_ref, g_ref, fg, fa, t_out,
@@ -172,7 +181,7 @@
     for group in away:
         for copy in group:
             copy.start()
-    gram_step([h + a for h, a in zip(here, away)], core, abuf, gbuf, even, gx, gy, tr)
+    rest = gram_step([h + a for h, a in zip(here, away)], core, abuf, gbuf, even, gx, gy, tr)
 
     def remote(src, dst, ssem, rsem, device):
         return pltpu.make_async_remote_copy(src_ref=src, dst_ref=dst, send_sem=ssem, recv_sem=rsem,
@@ -308,9 +317,10 @@
             pltpu.make_async_copy(aa.at[b], fa.at[i, b], ra5.at[b, i]).wait()
 
     batches = range(NB)
-    q = begin([remote(tr, q1.at[k], ts.at[k], tr_sem.at[k], xs[k]) for k in range(3)])
     first, second, third = {}, {}, {}
     first[0] = plane(0)
+    rest()
+    q = begin([remote(tr, q1.at[k], ts.at[k], tr_sem.at[k], xs[k]) for k in range(3)])
     plane_pass(0, first[0])
     first[1] = plane(1)
     plane_sum(0, first[0])
@@ -430,13 +440,12 @@
     in_cols = jnp.logical_and(lane >= at, lane < at + 4)
     out = jnp.where(jnp.logical_or(in_rows, in_cols), 0.0, now)
     rows = [jnp.where(in_cols, jnp.where(lane == at + i, -1.0, 0.0), rows[i]) for i in four]
+    terms = []
     for i in four:
         col = jnp.where(in_rows, jnp.where(sub == row + i, -1.0, 0.0), cols[i])
-        term = m[(i, 0)] * rows[0]
-        for j in range(1, 4):
-            term = term + m[(max(i, j), min(i, j))] * rows[j]
-        out = out + col * term
-    return out
+        t = [m[(max(i, j), min(i, j))] * rows[j] for j in four]
+        terms.append(col * ((t[0] + t[1]) + (t[2] + t[3])))
+    return (out + terms[0]) + (terms[1] + (terms[2] + terms[3]))
 
 
 def sweep_tiles(refs, panels, others=()):
@@ -701,19 +710,35 @@
     )(p)
 
 
-def turn_kernel(i_ref, o_ref):
-    for k in range(i_ref.shape[0] // 128):
-        o_ref[:, k * 128:(k + 1) * 128] = i_ref[k * 128:(k + 1) * 128, :].T
+def turn_kernel(i_ref, o_ref, ibuf, obuf, isem, osem):
+    tiles = FF // 128
+    parts = isem.shape[0]
+    cuts = [tiles * k // parts * 128 for k in range(parts + 1)]
+    ins = [pltpu.make_async_copy(i_ref.at[pl.ds(a, b - a)], ibuf.at[pl.ds(a, b - a)], isem.at[k])
+           for k, (a, b) in enumerate(zip(cuts, cuts[1:]))]
+    outs = [pltpu.make_async_copy(obuf.at[:, pl.ds(a, b - a)], o_ref.at[:, pl.ds(a, b - a)], osem.at[k])
+            for k, (a, b) in enumerate(zip(cuts, cuts[1:]))]
+    for copy in ins:
+        copy.start()
+    for k in range(parts):
+        ins[k].wait()
+        for at in range(cuts[k], cuts[k + 1], 128):
+            for half in (0, 128):
+                obuf[half:half + 128, at:at + 128] = ibuf[at:at + 128, half:half + 128].T
+        outs[k].start()
+    for copy in outs:
+        copy.wait()
 
 
 def turn(slices):
-    step = FF // 2
+    anywhere = pl.BlockSpec(memory_space=pl.ANY)
     return pl.pallas_call(
         turn_kernel,
         out_shape=jax.ShapeDtypeStruct((256, FF), jnp.bfloat16),
-        grid=(2, 2),
-        in_specs=[pl.BlockSpec((step, 128), lambda i, j: (j, i))],
-        out_specs=pl.BlockSpec((128, step), lambda i, j: (i, j)),
+        in_specs=[anywhere],
+        out_specs=anywhere,
+        scratch_shapes=[pltpu.VMEM((FF, 256), jnp.bfloat16), pltpu.VMEM((256, FF), jnp.bfloat16),
+                        pltpu.SemaphoreType.DMA((4,)), pltpu.SemaphoreType.DMA((4,))],
         compiler_params=pltpu.CompilerParams(vmem_limit_bytes=VLIM),
         name="turn",
     )(slices)

time: 140 us -> 137 us (0.979)
  Pallas kernels: 140 us -> 137 us
    pallas_call x1, Pallas kernels: 6.14 us -> 4.3 us  [turn(): pl.pallas_call(turn_kernel, out_shape=jax.ShapeDtypeStruct((256, FF), jnp...]
where the time goes in v7:
time: 137 us
  Pallas kernels  137 us (100%)
    pallas_call x1, Pallas kernels, reduce_all(): pl.pallas_call(reduce_kernel, out_shape=(jax.ShapeDtypeStruct((2, NB, 8,...  72.7 us
    pallas_call x1, Pallas kernels, gather(): pl.pallas_call(gather_kernel, out_shape=jax.ShapeDtypeStruct((16, 2 * GB,...  35 us
    pallas_call x1, Pallas kernels, solve(): pl.pallas_call(solve_kernel, out_shape=jax.ShapeDtypeStruct((2 * GB, 256)...  25 us
    pallas_call x1, Pallas kernels, turn(): pl.pallas_call(turn_kernel, out_shape=jax.ShapeDtypeStruct((256, FF), jnp...  4.3 us

profile of v7, /device:TPU:1, one launch (start us, length us, event | category | flops | bytes accessed | tf_op | source)
XLA Modules:
  0.0 137.3 jit_solution(938820668820131312)
XLA Ops:
  0.0 72.7 %reduce_all.1 = (f32[2,2,8,32,128]{4,3,2,1,0:T(8,128)}, f32[2,2,8,8,128]{4,3,2,1,0:T(8,128)}, f32[16,128]{1,0:T(8,128)}) custom-call(bf16[224,4096]{1,0:T(8,128)(2,1)} %a_ref.1, bf16[224,11008]{1,0:T(8,128)(2,1)} %g_ref.1), custom_call_target="tpu_custom_call" | custom-call | tf_op jit(solution)/shard_map/reduce_all/pallas_call | solution.py:378
  72.7 25.0 %solve.1.p_ref = bf16[688,256]{1,0:T(8,128)(2,1)} custom-call(f32[2,512,128]{2,1,0:T(8,128)} %bitcast.5, f32[256,128]{1,0:T(8,128)} %bitcast.7, f32[16,128]{1,0:T(8,128)} %get-tuple-element.10.t_ref, bf16[688,256]{1,0:T(8,128)(2,1)} %bitcast.6), custom_call_target="tpu_custom_call" | custom-call | tf_op jit(solution)/shard_map/solve/pallas_call | solution.py:594
  97.8 35.0 %gather.1 = bf16[16,688,256]{2,1,0:T(8,128)(2,1)} custom-call(bf16[688,256]{1,0:T(8,128)(2,1)} %solve.1.p_ref), custom_call_target="tpu_custom_call" | custom-call | tf_op jit(solution)/shard_map/gather/pallas_call | solution.py:702
  132.8 4.3 %turn.1 = bf16[256,11008]{1,0:T(8,128)(2,1)} custom-call(bf16[11008,256]{1,0:T(8,128)(2,1)} %bitcast.4), custom_call_target="tpu_custom_call" | custom-call | tf_op jit(solution)/shard_map/turn/pallas_call | solution.py:735

commit v8 on v7

--- a/solution.py
+++ b/solution.py
@@ -16,10 +16,13 @@
 DAMP = math.sqrt(0.03)
 MESH = pl.DeviceIdType.MESH
 F32 = jnp.float32
-NB = 2
-GROWS = 64 // NB
-AROWS = 16 // NB
-CH = GROWS + AROWS
+GROWS = (32, 16, 16)
+AROWS = (8, 8, 0)
+NB = len(GROWS)
+CHS = tuple(g + a for g, a in zip(GROWS, AROWS))
+GBASE = tuple(8 * sum(GROWS[:b]) for b in range(NB))
+ABASE = tuple(8 * sum(AROWS[:b]) for b in range(NB))
+CH = max(CHS)
 HALF = 4 * CH
 VLIM = 56 * 1024 * 1024
 WIN = 7 * 128
@@ -79,14 +82,17 @@
 
 
 def gram_step(copies, core, abuf, gbuf, even, x_ref, y_ref, t_ref):
-    def store_all(where, size, lead, row, value):
+    def store_all(where, sizes, bases, row, value):
         px, py = where
         done = 0
         while done < value.shape[0]:
             at = row + done
-            n = min(size - at % size, value.shape[0] - done)
-            batch, chunk = at // size // 8, at // size % 8
-            rows_at = pl.ds(chunk % 4 * CH + lead + at % size, n)
+            batch = max(b for b in range(NB) if bases[b] <= at and sizes[b])
+            size = sizes[batch]
+            chunk, left = divmod(at - bases[batch], size)
+            n = min(size - left, value.shape[0] - done)
+            lead = 0 if sizes is GROWS else GROWS[batch]
+            rows_at = pl.ds(chunk % 4 * CHS[batch] + lead + left, n)
             if chunk < 4:
                 x_ref[batch, px * 4 + py, rows_at, :] = value[done:done + n]
             else:
@@ -109,8 +115,8 @@
         second = diag(t2)
         act_sum += diag(t0) + second
         t_ref[8 + k:9 + k, :] = second
-        store_all(act_position(k, 0), AROWS, GROWS, 0, g[128:256, 0:128])
-        store_all(act_position(k, 1), AROWS, GROWS, 0, jnp.where(r >= c, t0, t2))
+        store_all(act_position(k, 0), AROWS, ABASE, 0, g[128:256, 0:128])
+        store_all(act_position(k, 1), AROWS, ABASE, 0, jnp.where(r >= c, t0, t2))
     for j in range(16):
         if j in (0, 8):
             for copy in copies[1 + j // 8]:
@@ -127,9 +133,9 @@
         second = diag(t2)
         grad_sum += diag(t0) + second
         where = grad_position(j // 2, j % 2, core)
-        store_all(where, GROWS, 0, 0, g[128:256, 0:128])
-        store_all(where, GROWS, 0, 128, jnp.where(r >= c, t0, t2))
-        store_all(where, GROWS, 0, 480, jnp.concatenate([second, jnp.zeros((31, 128), F32)], axis=0))
+        store_all(where, GROWS, GBASE, 0, g[128:256, 0:128])
+        store_all(where, GROWS, GBASE, 128, jnp.where(r >= c, t0, t2))
+        store_all(where, GROWS, GBASE, 480, jnp.concatenate([second, jnp.zeros((31, 128), F32)], axis=0))
 
     def rest():
         corner_sum = grad_sum
@@ -140,9 +146,9 @@
             corner_sum += jnp.sum(jnp.where(r[:88] == c[:88], t5, 0.0), axis=0, keepdims=True)
             tail = jnp.concatenate([pltpu.roll(t5[48:88], 40, 1), jnp.zeros((8, 128), F32)], axis=0)
             where = grad_position(j // 2, j % 2, core)
-            store_all(where, GROWS, 0, 256, low[:, 0:128])
-            store_all(where, GROWS, 0, 344, low[:, 128:256])
-            store_all(where, GROWS, 0, 432, jnp.where(c[:48] < 88, t5[0:48], tail))
+            store_all(where, GROWS, GBASE, 256, low[:, 0:128])
+            store_all(where, GROWS, GBASE, 344, low[:, 128:256])
+            store_all(where, GROWS, GBASE, 432, jnp.where(c[:48] < 88, t5[0:48], tail))
         t_ref[0:8, :] = jnp.concatenate([act_sum, corner_sum, jnp.zeros((6, 128), F32)], axis=0)
 
     return rest
@@ -198,18 +204,26 @@
 
     axes = ((0, gx, x, (xs[0], xs[2])), (1, gy, y, (ys[0], ys[2])))
 
+    def high(b):
+        return pl.ds(0, 4 * CHS[b])
+
+    def chunk_rows(b, i):
+        return pl.ds(pl.multiple_of(i * CHS[b], 8), CHS[b])
+
     def plane(b):
         copies = []
+        two, rows = pl.ds(0, 2), high(b)
         for a, g, me, (up, down) in axes:
             opposite = lax.rem(me + 2, 4) * 4
-            copies.append(remote(g.at[b, pl.ds(opposite, 2)], pm.at[a, b, 0], s1.at[a, b, 0], r1.at[a, b, 0], up))
-            copies.append(remote(g.at[b, pl.ds(opposite + 2, 2)], pm.at[a, b, 1],
+            copies.append(remote(g.at[b, pl.ds(opposite, 2), rows], pm.at[a, b, 0, two, rows],
+                                 s1.at[a, b, 0], r1.at[a, b, 0], up))
+            copies.append(remote(g.at[b, pl.ds(opposite + 2, 2), rows], pm.at[a, b, 1, two, rows],
                                  s1.at[a, b, 1], r1.at[a, b, 1], down))
         for a, g, me, (up, down) in axes:
             over, under = lax.rem(me + 1, 4) * 4, lax.rem(me + 3, 4) * 4
-            copies.append(remote(g.at[b, pl.ds(over + 2, 2)], pr.at[a, b, 0, pl.ds(2, 2)],
+            copies.append(remote(g.at[b, pl.ds(over + 2, 2), rows], pr.at[a, b, 0, pl.ds(2, 2), rows],
                                  s1.at[a, b, 2], r1.at[a, b, 2], up))
-            copies.append(remote(g.at[b, pl.ds(under, 2)], pr.at[a, b, 1, pl.ds(0, 2)],
+            copies.append(remote(g.at[b, pl.ds(under, 2), rows], pr.at[a, b, 1, two, rows],
                                  s1.at[a, b, 3], r1.at[a, b, 3], down))
         return begin(copies)
 
@@ -217,14 +231,14 @@
         end(copies[:4])
         @pl.loop(0, 8)
         def _(i):
-            h, rows = i // 4, pl.ds(pl.multiple_of(lax.rem(i, 4) * CH, 8), CH)
+            h, rows = i // 4, chunk_rows(b, lax.rem(i, 4))
             for a, g, me, _ in axes:
                 over, under = lax.rem(me + 1, 4) * 4, lax.rem(me + 3, 4) * 4
                 pk[a, b, 0, h, rows, :] = g[b, over + h, rows, :] + pm[a, b, 0, h, rows, :]
                 pk[a, b, 1, h, rows, :] = g[b, under + 2 + h, rows, :] + pm[a, b, 1, h, rows, :]
         for a, _, _, to in axes:
             for d in range(2):
-                copies.append(remote(pk.at[a, b, d], pr.at[a, b, d, pl.ds(2 * d, 2)],
+                copies.append(remote(pk.at[a, b, d, pl.ds(0, 2), high(b)], pr.at[a, b, d, pl.ds(2 * d, 2), high(b)],
                                      s1.at[a, b, 4 + d], r1.at[a, b, 4 + d], to[d]))
                 copies[-1].start()
 
@@ -232,128 +246,154 @@
         end(copies[4:])
         @pl.loop(0, 16)
         def _(i):
-            q, rows = i // 4, pl.ds(pl.multiple_of(lax.rem(i, 4) * CH, 8), CH)
+            q, rows = i // 4, chunk_rows(b, lax.rem(i, 4))
             for a, g, me, _ in axes:
                 ps[a, b, q, rows, :] = g[b, me * 4 + q, rows, :] + (pr[a, b, 0, q, rows, :] + pr[a, b, 1, q, rows, :])
 
     def cross(b):
         copies = []
+        rows = high(b)
         for k in range(3):
-            copies.append(remote(ps.at[0, b, lax.rem(y + k + 1, 4)], rx2.at[b, k], s2.at[b, k], r2.at[b, k], ys[k]))
-            copies.append(remote(ps.at[1, b, lax.rem(x + k + 1, 4)], ry2.at[b, k],
+            copies.append(remote(ps.at[0, b, lax.rem(y + k + 1, 4), rows], rx2.at[b, k, rows],
+                                 s2.at[b, k], r2.at[b, k], ys[k]))
+            copies.append(remote(ps.at[1, b, lax.rem(x + k + 1, 4), rows], ry2.at[b, k, rows],
                                  s2.at[b, 3 + k], r2.at[b, 3 + k], xs[k]))
         return begin(copies)
 
     def cross_sum(b):
+        n = CHS[b]
         @pl.loop(0, 4)
         def _(i):
-            rows = pl.ds(pl.multiple_of(i * CH, 8), CH)
-            st[b, i] = (ps[0, b, y, rows, :] + rx2[b, 0, rows, :]) + (rx2[b, 1, rows, :] + rx2[b, 2, rows, :])
-            st[b, 4 + i] = (ps[1, b, x, rows, :] + ry2[b, 0, rows, :]) + (ry2[b, 1, rows, :] + ry2[b, 2, rows, :])
+            rows = chunk_rows(b, i)
+            st[b, i, 0:n, :] = (ps[0, b, y, rows, :] + rx2[b, 0, rows, :]) + (rx2[b, 1, rows, :] + rx2[b, 2, rows, :])
+            st[b, 4 + i, 0:n, :] = ((ps[1, b, x, rows, :] + ry2[b, 0, rows, :])
+                                    + (ry2[b, 1, rows, :] + ry2[b, 2, rows, :]))
 
     def along(b):
-        return begin([remote(st.at[b, lax.rem(z + k + 1, 8)], rz.at[b, k], s3.at[b, k], r3.at[b, k], zs[k])
+        rows = pl.ds(0, CHS[b])
+        return begin([remote(st.at[b, lax.rem(z + k + 1, 8), rows], rz.at[b, k, rows], s3.at[b, k], r3.at[b, k], zs[k])
                       for k in range(7)])
 
     def along_sum(b):
-        total = st[b, z]
+        n = CHS[b]
+        total = st[b, z, 0:n, :]
         for k in range(7):
-            total += rz[b, k]
-        fin[b] = total
+            total += rz[b, k, 0:n, :]
+        fin[b, 0:n, :] = total
+
+    def pieces(b):
+        found = [(fin.at[b, pl.ds(0, GROWS[b])], ga, GBASE[b], GROWS[b], rg4, [unit_zh * 4 + i for i in range(4)], 0)]
+        if AROWS[b]:
+            found.append((fin.at[b, pl.ds(GROWS[b], AROWS[b])], aa, ABASE[b], AROWS[b], ra4,
+                          [i * 4 + unit_zl for i in range(2)], 4))
+        return found
+
+    def slot(buffer, base, size, i):
+        return buffer.at[pl.ds(pl.multiple_of(base + i * size, 8), size)]
 
     def spread(b):
-        for i in range(6):
-            if i < 4:
-                to = unit_zh * 4 + i
-                src, dst, rsem = fin.at[b, pl.ds(0, GROWS)], ga.at[b, z], rg4.at[b, z]
-            else:
-                to = (i - 4) * 4 + unit_zl
-                src, dst, rsem = fin.at[b, pl.ds(GROWS, AROWS)], aa.at[b, z], ra4.at[b, z]
-
-            @pl.when(to == z)
-            def _():
-                pltpu.make_async_copy(src, dst, rsem).start()
-
-            @pl.when(to != z)
-            def _():
-                remote(src, dst, s4.at[b, i], rsem, at(x, y, to, core)).start()
+        for src, buffer, base, size, rsem, planes, first in pieces(b):
+            dst = slot(buffer, base, size, z)
+            for i, to in enumerate(planes):
+                @pl.when(to == z)
+                def _():
+                    pltpu.make_async_copy(src, dst, rsem.at[b, z]).start()
+
+                @pl.when(to != z)
+                def _():
+                    remote(src, dst, s4.at[b, first + i], rsem.at[b, z], at(x, y, to, core)).start()
 
     def spread_sent(b):
-        for i in range(6):
-            to = unit_zh * 4 + i if i < 4 else (i - 4) * 4 + unit_zl
-            src = fin.at[b, pl.ds(0, GROWS)] if i < 4 else fin.at[b, pl.ds(GROWS, AROWS)]
-            dst, rsem = (ga.at[b, z], rg4.at[b, z]) if i < 4 else (aa.at[b, z], ra4.at[b, z])
-
-            @pl.when(to != z)
-            def _():
-                remote(src, dst, s4.at[b, i], rsem, at(x, y, to, core)).wait_send()
+        for src, buffer, base, size, rsem, planes, first in pieces(b):
+            dst = slot(buffer, base, size, z)
+            for i, to in enumerate(planes):
+                @pl.when(to != z)
+                def _():
+                    remote(src, dst, s4.at[b, first + i], rsem.at[b, z], at(x, y, to, core)).wait_send()
 
     def parts(b):
-        return ((g_on, ga.at[b], xs, fg.at[g_part, b], rg5.at[b, g_part], 0),
-                (a_on, aa.at[b], ys + across, fa.at[a_part, b], ra5.at[b, a_part], 3))
+        for (src, buffer, base, size, rsem, _, first), (on, to, out, part, sem, at_sem) in zip(
+                pieces(b), ((g_on, xs, fg, g_part, rg5, 0), (a_on, ys + across, fa, a_part, ra5, 3))):
+            rows = pl.ds(base, 8 * size)
+            yield src, buffer, base, size, rsem, on, to, buffer.at[rows], out, rows, part, sem, at_sem
 
     def give(b):
-        for on, src, to, dst, rsem, first in parts(b):
+        for piece, buffer, base, size, arrive, on, to, src, out, rows, part, sem, first in parts(b):
             @pl.when(on)
             def _():
                 for i in range(8):
-                    piece = fin.at[b, pl.ds(0, GROWS)] if first == 0 else fin.at[b, pl.ds(GROWS, AROWS)]
-                    arrive = (rg4 if first == 0 else ra4).at[b, i]
-                    pltpu.make_async_copy(piece, src.at[i], arrive).wait()
+                    pltpu.make_async_copy(piece, slot(buffer, base, size, i), arrive.at[b, i]).wait()
+                dst = out.at[part, rows]
                 for i, device in enumerate(to):
-                    remote(src, dst, s5.at[b, first + i], rsem, device).start()
-                pltpu.make_async_copy(src, dst, rsem).start()
+                    remote(src, dst, s5.at[b, first + i], sem.at[b, part], device).start()
+                pltpu.make_async_copy(src, dst, sem.at[b, part]).start()
 
     def given(b):
-        for on, src, to, dst, rsem, first in parts(b):
+        for piece, buffer, base, size, arrive, on, to, src, out, rows, part, sem, first in parts(b):
             @pl.when(on)
             def _():
                 for i, device in enumerate(to):
-                    remote(src, dst, s5.at[b, first + i], rsem, device).wait_send()
+                    remote(src, out.at[part, rows], s5.at[b, first + i], sem.at[b, part], device).wait_send()
 
     def taken(b):
-        for i in range(2):
-            pltpu.make_async_copy(ga.at[b], fg.at[i, b], rg5.at[b, i]).wait()
-            pltpu.make_async_copy(aa.at[b], fa.at[i, b], ra5.at[b, i]).wait()
+        for piece, buffer, base, size, arrive, on, to, src, out, rows, part, sem, first in parts(b):
+            for i in range(2):
+                pltpu.make_async_copy(src, out.at[i, rows], sem.at[b, i]).wait()
 
     batches = range(NB)
     first, second, third = {}, {}, {}
-    first[0] = plane(0)
+
+    def step(name, b):
+        if name == "plane":
+            first[b] = plane(b)
+        elif name == "pass":
+            plane_pass(b, first[b])
+        elif name == "cross":
+            plane_sum(b, first[b])
+            second[b] = cross(b)
+        elif name == "along":
+            end(second[b])
+            cross_sum(b)
+            third[b] = along(b)
+        elif name == "spread":
+            end(third[b])
+            along_sum(b)
+            spread(b)
+        else:
+            give(b)
+
+    step("plane", 0)
     rest()
     q = begin([remote(tr, q1.at[k], ts.at[k], tr_sem.at[k], xs[k]) for k in range(3)])
-    plane_pass(0, first[0])
-    first[1] = plane(1)
-    plane_sum(0, first[0])
-    second[0] = cross(0)
+    step("pass", 0)
+    step("plane", 1)
+    step("cross", 0)
     end(q)
     t1[...] = (tr[...] + q1[0]) + (q1[1] + q1[2])
     q = begin([remote(t1, q2.at[k], ts.at[3 + k], tr_sem.at[3 + k], ys[k]) for k in range(3)])
-    plane_pass(1, first[1])
-    end(second[0])
-    cross_sum(0)
-    third[0] = along(0)
+    step("pass", 1)
+    step("plane", 2)
+    step("along", 0)
     end(q)
     t2[...] = (t1[...] + q2[0]) + (q2[1] + q2[2])
     q = begin([remote(t2, q3.at[k], ts.at[6 + k], tr_sem.at[6 + k], zs[k]) for k in range(7)])
-    plane_sum(1, first[1])
-    second[1] = cross(1)
-    end(third[0])
-    along_sum(0)
-    spread(0)
+    step("cross", 1)
+    step("pass", 2)
+    step("spread", 0)
     end(q)
     trace = t2[...]
     for k in range(7):
         trace += q3[k]
     t3[...] = trace
     q = begin([remote(t3, q4, ts.at[13], tr_sem.at[13], (sib, own))])
-    end(second[1])
-    cross_sum(1)
-    third[1] = along(1)
-    give(0)
-    end(third[1])
-    along_sum(1)
-    spread(1)
-    give(1)
+    step("along", 1)
+    step("cross", 2)
+    step("give", 0)
+    step("spread", 1)
+    step("along", 2)
+    step("give", 1)
+    step("spread", 2)
+    step("give", 2)
     end(q)
     tt[core] = t3[...]
     tt[1 - core] = q4[...]
@@ -377,8 +417,8 @@
 
     return pl.pallas_call(
         reduce_kernel,
-        out_shape=(jax.ShapeDtypeStruct((2, NB, 8, GROWS, 128), F32),
-                   jax.ShapeDtypeStruct((2, NB, 8, AROWS, 128), F32),
+        out_shape=(jax.ShapeDtypeStruct((2, 8 * sum(GROWS), 128), F32),
+                   jax.ShapeDtypeStruct((2, 8 * sum(AROWS), 128), F32),
                    jax.ShapeDtypeStruct((16, 128), F32)),
         in_specs=[pl.BlockSpec(memory_space=pl.ANY)] * 2,
         out_specs=(vmem,) * 3,
@@ -388,7 +428,7 @@
             buf(NB, 16, HALF), buf(NB, 16, HALF), tile,
             buf(2, NB, 4, HALF), buf(2, NB, 2, 2, HALF), buf(2, NB, 2, 2, HALF), buf(2, NB, 2, 4, HALF),
             buf(NB, 3, HALF), buf(NB, 3, HALF), buf(NB, 8, CH), buf(NB, 7, CH), buf(NB, CH),
-            buf(NB, 8, GROWS), buf(NB, 8, AROWS),
+            buf(8 * sum(GROWS)), buf(8 * sum(AROWS)),
             tile, tile, tile, buf(3, 16), buf(3, 16), buf(7, 16), tile, buf(2, 16),
             dma((3, 4)), dma((3, 4)), dma((3, 4)), dma((2, NB, 6)), dma((2, NB, 6)), dma((NB, 6)), dma((NB, 6)), dma((NB, 7)), dma((NB, 7)),
             dma((NB, 6)), dma((NB, 8)), dma((NB, 8)), dma((NB, 10)), dma((NB, 2)), dma((NB, 2)), dma((14,)), dma((14,)),
@@ -746,7 +786,7 @@
 
 def shards(acts, grads_out, weight_grad):
     fg, fa, tr = reduce_all(acts, grads_out)
-    p = solve(fg.reshape(2, 512, 128), fa.reshape(256, 128), tr, weight_grad.T)
+    p = solve(fg, fa.reshape(256, 128), tr, weight_grad.T)
     return turn(gather(p).reshape(FF, 256))
 
 

time: 137 us -> 135 us (0.985)
  the two profiles are of different devices: /device:TPU:1 before, /device:TPU:33 now
where the time goes in v8:
time: 135 us; the launch traced here: 134 us
  Pallas kernels  133 us (99%)
    pallas_call x1, Pallas kernels, reduce_all(): pl.pallas_call(reduce_kernel, out_shape=(jax.ShapeDtypeStruct((2, 8 * sum...  66.7 us
    pallas_call x1, Pallas kernels, gather(): pl.pallas_call(gather_kernel, out_shape=jax.ShapeDtypeStruct((16, 2 * GB,...  37.3 us
    pallas_call x1, Pallas kernels, solve(): pl.pallas_call(solve_kernel, out_shape=jax.ShapeDtypeStruct((2 * GB, 256)...  25 us
    pallas_call x1, Pallas kernels, turn(): pl.pallas_call(turn_kernel, out_shape=jax.ShapeDtypeStruct((256, FF), jnp...  4.3 us

profile of v8, /device:TPU:33, one launch (start us, length us, event | category | flops | bytes accessed | tf_op | source)
XLA Modules:
  0.0 133.5 jit_solution(3687666736963954631)
XLA Ops:
  0.0 66.7 %reduce_all.1 = (f32[2,512,128]{2,1,0:T(8,128)}, f32[2,128,128]{2,1,0:T(8,128)}, f32[16,128]{1,0:T(8,128)}) custom-call(bf16[224,4096]{1,0:T(8,128)(2,1)} %a_ref.1, bf16[224,11008]{1,0:T(8,128)(2,1)} %g_ref.1), custom_call_target="tpu_custom_call" | custom-call | tf_op jit(solution)/shard_map/reduce_all/pallas_call | solution.py:418
  66.7 25.0 %solve.1.p_ref = bf16[688,256]{1,0:T(8,128)(2,1)} custom-call(f32[2,512,128]{2,1,0:T(8,128)} %get-tuple-element.8.fg_ref, f32[256,128]{1,0:T(8,128)} %bitcast.5, f32[16,128]{1,0:T(8,128)} %get-tuple-element.10.t_ref, bf16[688,256]{1,0:T(8,128)(2,1)} %bitcast.4), custom_call_target="tpu_custom_call" | custom-call | tf_op jit(solution)/shard_map/solve/pallas_call | solution.py:634
  91.7 37.3 %gather.1 = bf16[16,688,256]{2,1,0:T(8,128)(2,1)} custom-call(bf16[688,256]{1,0:T(8,128)(2,1)} %solve.1.p_ref), custom_call_target="tpu_custom_call" | custom-call | tf_op jit(solution)/shard_map/gather/pallas_call | solution.py:742
  129.0 4.3 %turn.1 = bf16[256,11008]{1,0:T(8,128)(2,1)} custom-call(bf16[11008,256]{1,0:T(8,128)(2,1)} %bitcast.3), custom_call_target="tpu_custom_call" | custom-call | tf_op jit(solution)/shard_map/turn/pallas_call | solution.py:775

commit v9 on v8

--- a/solution.py
+++ b/solution.py
@@ -17,7 +17,7 @@
 MESH = pl.DeviceIdType.MESH
 F32 = jnp.float32
 GROWS = (32, 16, 16)
-AROWS = (8, 8, 0)
+AROWS = (16, 0, 0)
 NB = len(GROWS)
 CHS = tuple(g + a for g, a in zip(GROWS, AROWS))
 GBASE = tuple(8 * sum(GROWS[:b]) for b in range(NB))
@@ -154,7 +154,7 @@
     return rest
 
 
-def reduce_kernel(a_ref, g_ref, fg, fa, t_out,
+def reduce_kernel(a_ref, g_ref, fg, fa, t_out, swept,
                   abuf, gbuf, even, gx, gy, tr, ps, pk, pm, pr, rx2, ry2, st, rz, fin, ga, aa, t1, t2, t3, q1, q2, q3, q4, tt,
                   local, s0, r0, s1, r1, s2, r2, s3, r3, s4, rg4, ra4, s5, rg5, ra5, ts, tr_sem):
     dp, own = place()
@@ -391,15 +391,26 @@
     step("give", 0)
     step("spread", 1)
     step("along", 2)
-    step("give", 1)
-    step("spread", 2)
-    step("give", 2)
     end(q)
     tt[core] = t3[...]
     tt[1 - core] = q4[...]
     t_out[0:8, :] = tt[0, 0:8, :] + tt[1, 0:8, :]
     t_out[8:16, :] = jnp.broadcast_to(tt[own // 8, pl.ds(8 + lax.rem(own, 8), 1), :], (8, 128))
-    for b in batches:
+    taken(0)
+    act_damp, grad_damp = dampings(t_out)
+    r = lax.broadcasted_iota(jnp.int32, (128, 128), 0)
+    c = lax.broadcasted_iota(jnp.int32, (128, 128), 1)
+    for i, both, damp in ((0, fg[0, 128:256, :], grad_damp), (1, fg[1, 128:256, :], grad_damp),
+                          (2, fa[1], act_damp)):
+        swept[i] = jnp.where(r >= c, both, both.T) / TOKENS + jnp.where(r == c, damp, 0.0)
+    tiles = [swept.at[i] for i in range(3)]
+    sweep_tiles(tiles, 4)
+    step("give", 1)
+    step("spread", 2)
+    sweep_tiles(tiles, 10, start=4)
+    step("give", 2)
+    sweep_tiles(tiles, 16, start=10)
+    for b in batches[1:]:
         taken(b)
     for b in batches:
         spread_sent(b)
@@ -419,9 +430,9 @@
         reduce_kernel,
         out_shape=(jax.ShapeDtypeStruct((2, 8 * sum(GROWS), 128), F32),
                    jax.ShapeDtypeStruct((2, 8 * sum(AROWS), 128), F32),
-                   jax.ShapeDtypeStruct((16, 128), F32)),
+                   jax.ShapeDtypeStruct((16, 128), F32), jax.ShapeDtypeStruct((3, 128, 128), F32)),
         in_specs=[pl.BlockSpec(memory_space=pl.ANY)] * 2,
-        out_specs=(vmem,) * 3,
+        out_specs=(vmem,) * 4,
         scratch_shapes=[
             pltpu.VMEM((2 * rows, D // 2), acts.dtype), pltpu.VMEM((2 * rows, 8 * WIN), acts.dtype),
             pltpu.VMEM((16, 2 * rows, 384), acts.dtype),
@@ -488,12 +499,12 @@
     return (out + terms[0]) + (terms[1] + (terms[2] + terms[3]))
 
 
-def sweep_tiles(refs, panels, others=()):
+def sweep_tiles(refs, panels, others=(), start=0):
     others = list(others)
     sub = lax.broadcasted_iota(jnp.int32, (8, 128), 0)
     lane = lax.broadcasted_iota(jnp.int32, (8, 128), 1)
     lane_all = lax.broadcasted_iota(jnp.int32, (128, 128), 1)
-    for p in range(panels):
+    for p in range(start, panels):
         base = 8 * p
         inside = jnp.logical_and(lane_all >= base, lane_all < base + 8)
         olds = [ref[base:base + 8, :] for ref in refs]
@@ -508,29 +519,29 @@
         others = others[count:]
 
 
-def solve_kernel(fg_ref, fa_ref, t_ref, w_ref, p_ref, g_ref, a_ref, l_ref, x_ref, ai_ref):
+def dampings(t_ref):
     act_trace = jnp.sum(t_ref[0:1, :], keepdims=True) / TOKENS
     grad_trace = jnp.sum(t_ref[1:2, :], keepdims=True) / TOKENS
     ratio = jnp.sqrt(act_trace / D / (grad_trace / FF))
-    act_damp = ratio * DAMP
-    grad_damp = DAMP / ratio
+    return ratio * DAMP, DAMP / ratio
+
+
+def solve_kernel(fg_ref, fa_ref, t_ref, s_ref, w_ref, p_ref, g_ref, a_ref, l_ref, x_ref, ai_ref):
+    act_damp, grad_damp = dampings(t_ref)
     r = lax.broadcasted_iota(jnp.int32, (128, 128), 0)
     c = lax.broadcasted_iota(jnp.int32, (128, 128), 1)
     last = GB - 256
 
-    def pair(both, second):
-        turned = both.T
-        first = jnp.where(r >= c, both, turned)
-        other = jnp.where(r < c, both, jnp.where(r == c, jnp.broadcast_to(second, (128, 128)), turned))
-        return first, other
+    def second_of(both, second):
+        return jnp.where(r < c, both, jnp.where(r == c, jnp.broadcast_to(second, (128, 128)), both.T))
 
     def damped(tile, damp):
         return tile / TOKENS + jnp.where(r == c, damp, 0.0)
 
     zeros = jnp.zeros((128 - last, 128), F32)
     for b in range(2):
-        first, second = pair(fg_ref[b, 128:256, :], fg_ref[b, 480:481, :])
-        g_ref[b * 6] = damped(first, grad_damp)
+        second = second_of(fg_ref[b, 128:256, :], fg_ref[b, 480:481, :])
+        g_ref[b * 6] = s_ref[b]
         g_ref[b * 6 + 1] = fg_ref[b, 0:128, :] / TOKENS
         g_ref[b * 6 + 2] = damped(second, grad_damp)
         g_ref[b * 6 + 3] = jnp.concatenate([fg_ref[b, 256:344, :] / TOKENS, zeros], axis=0)
@@ -541,13 +552,12 @@
         corner = jnp.where(jnp.logical_and(r >= 48, c < 48), upper.T, upper)
         inside = jnp.logical_and(r < last, c < last)
         g_ref[b * 6 + 5] = jnp.where(inside, damped(corner, grad_damp), jnp.where(r == c, 1.0, 0.0))
-    first, second = pair(fa_ref[128:256, :], t_ref[8:9, :])
-    a_ref[0] = damped(first, act_damp)
+    second = second_of(fa_ref[128:256, :], t_ref[8:9, :])
+    a_ref[0] = s_ref[2]
     a_ref[1] = fa_ref[0:128, :] / TOKENS
     a_ref[2] = damped(second, act_damp)
     gs = [[g_ref.at[b * 6 + t] for t in range(6)] for b in range(2)]
     am = [a_ref.at[t] for t in range(3)]
-    sweep_tiles([gs[0][0], gs[1][0], am[0]], 16)
     for m in gs + [am]:
         a10 = m[1][...]
         l10 = -dot(a10, m[0][...])
@@ -629,19 +639,19 @@
     p_ref[...] = jnp.concatenate(out, axis=0).astype(jnp.bfloat16)
 
 
-def solve(fg, fa, tr, w):
+def solve(fg, fa, tr, swept, w):
     vmem = pl.BlockSpec(memory_space=pltpu.VMEM)
     return pl.pallas_call(
         solve_kernel,
         out_shape=jax.ShapeDtypeStruct((2 * GB, 256), jnp.bfloat16),
-        in_specs=[vmem] * 4,
+        in_specs=[vmem] * 5,
         out_specs=vmem,
         scratch_shapes=[pltpu.VMEM((12, 128, 128), F32), pltpu.VMEM((3, 128, 128), F32),
                         pltpu.VMEM((7, 128, 128), F32), pltpu.VMEM((2, 384, 256), F32),
                         pltpu.VMEM((256, 256), F32)],
         compiler_params=pltpu.CompilerParams(vmem_limit_bytes=VLIM),
         name="solve",
-    )(fg, fa, tr, w)
+    )(fg, fa, tr, swept, w)
 
 
 def gather_kernel(p_ref, o_ref, local, sz, rz, sy, ry, sh, rh, sc, rc):
@@ -785,8 +795,8 @@
 
 
 def shards(acts, grads_out, weight_grad):
-    fg, fa, tr = reduce_all(acts, grads_out)
-    p = solve(fg, fa.reshape(256, 128), tr, weight_grad.T)
+    fg, fa, tr, swept = reduce_all(acts, grads_out)
+    p = solve(fg, fa.reshape(256, 128), tr, swept, weight_grad.T)
     return turn(gather(p).reshape(FF, 256))
 
 

time: 135 us -> 130 us (0.963)
  Pallas kernels: 133 us -> 128 us
    pallas_call x1, Pallas kernels: 25 us -> 17 us  [solve(): pl.pallas_call(solve_kernel, out_shape=jax.ShapeDtypeStruct((2 * GB, 256)...]
    pallas_call x1, Pallas kernels: 66.7 us -> 71.2 us  [reduce_all(): pl.pallas_call(reduce_kernel, out_shape=(jax.ShapeDtypeStruct((2, 8 * sum...]
    pallas_call x1, Pallas kernels: 37.3 us -> 35.5 us  [gather(): pl.pallas_call(gather_kernel, out_shape=jax.ShapeDtypeStruct((16, 2 * GB,...]
where the time goes in v9:
time: 130 us; the launch traced here: 128 us
  Pallas kernels  128 us (98%)
    pallas_call x1, Pallas kernels, reduce_all(): pl.pallas_call(reduce_kernel, out_shape=(jax.ShapeDtypeStruct((2, 8 * sum...  71.2 us
    pallas_call x1, Pallas kernels, gather(): pl.pallas_call(gather_kernel, out_shape=jax.ShapeDtypeStruct((16, 2 * GB,...  35.5 us
    pallas_call x1, Pallas kernels, solve(): pl.pallas_call(solve_kernel, out_shape=jax.ShapeDtypeStruct((2 * GB, 256)...  17 us
    pallas_call x1, Pallas kernels, turn(): pl.pallas_call(turn_kernel, out_shape=jax.ShapeDtypeStruct((256, FF), jnp...  4.3 us

profile of v9, /device:TPU:33, one launch (start us, length us, event | category | flops | bytes accessed | tf_op | source)
XLA Modules:
  0.0 128.3 jit_solution(3871538447969251808)
XLA Ops:
  0.0 71.2 %reduce_all.1 = (f32[2,512,128]{2,1,0:T(8,128)}, f32[2,128,128]{2,1,0:T(8,128)}, f32[16,128]{1,0:T(8,128)}, f32[3,128,128]{2,1,0:T(8,128)}) custom-call(bf16[224,4096]{1,0:T(8,128)(2,1)} %a_ref.1, bf16[224,11008]{1,0:T(8,128)(2,1)} %g_ref.1), custom_call_target="tpu_custom_call" | custom-call | tf_op jit(solution)/shard_map/reduce_all/pallas_call | solution.py:429
  71.3 17.0 %solve.1.p_ref = bf16[688,256]{1,0:T(8,128)(2,1)} custom-call(f32[2,512,128]{2,1,0:T(8,128)} %get-tuple-element.9.fg_ref, f32[256,128]{1,0:T(8,128)} %bitcast.5, f32[16,128]{1,0:T(8,128)} %get-tuple-element.11.t_ref, f32[3,128,128]{2,1,0:T(8,128)} %get-tuple-element.12.s_ref, bf16[688,256]{1,0:T(8,128)(2,1)} %bitcast.4), custom_call_target="tpu_custom_call" | custom-call | tf_op jit(solution)/shard_map/solve/pallas_call | solution.py:644
  88.3 35.5 %gather.1 = bf16[16,688,256]{2,1,0:T(8,128)(2,1)} custom-call(bf16[688,256]{1,0:T(8,128)(2,1)} %solve.1.p_ref), custom_call_target="tpu_custom_call" | custom-call | tf_op jit(solution)/shard_map/gather/pallas_call | solution.py:752
  123.8 4.3 %turn.1 = bf16[256,11008]{1,0:T(8,128)(2,1)} custom-call(bf16[11008,256]{1,0:T(8,128)(2,1)} %bitcast.3), custom_call_target="tpu_custom_call" | custom-call | tf_op jit(solution)/shard_map/turn/pallas_call | solution.py:785

commit v10 on v9

--- a/solution.py
+++ b/solution.py
@@ -26,7 +26,7 @@
 HALF = 4 * CH
 VLIM = 56 * 1024 * 1024
 WIN = 7 * 128
-WIDTHS = [WIN] * 7 + [WIN - 128]
+WIDTHS = [WIN - 128 * (p % 4 in (0, 3)) for p in range(8)]
 CUT = (352, 336)
 
 

time: 130 us -> 130 us (level)
  no operation moved by 1% of the time
where the time goes in v10:
time: 130 us; the launch traced here: 128 us
  Pallas kernels  128 us (98%)
    pallas_call x1, Pallas kernels, reduce_all(): pl.pallas_call(reduce_kernel, out_shape=(jax.ShapeDtypeStruct((2, 8 * sum...  71.3 us
    pallas_call x1, Pallas kernels, gather(): pl.pallas_call(gather_kernel, out_shape=jax.ShapeDtypeStruct((16, 2 * GB,...  35.2 us
    pallas_call x1, Pallas kernels, solve(): pl.pallas_call(solve_kernel, out_shape=jax.ShapeDtypeStruct((2 * GB, 256)...  17 us
    pallas_call x1, Pallas kernels, turn(): pl.pallas_call(turn_kernel, out_shape=jax.ShapeDtypeStruct((256, FF), jnp...  4.3 us

profile of v10, /device:TPU:33, one launch (start us, length us, event | category | flops | bytes accessed | tf_op | source)
XLA Modules:
  0.0 128.1 jit_solution(5411356071395301387)
XLA Ops:
  0.0 71.3 %reduce_all.1 = (f32[2,512,128]{2,1,0:T(8,128)}, f32[2,128,128]{2,1,0:T(8,128)}, f32[16,128]{1,0:T(8,128)}, f32[3,128,128]{2,1,0:T(8,128)}) custom-call(bf16[224,4096]{1,0:T(8,128)(2,1)} %a_ref.1, bf16[224,11008]{1,0:T(8,128)(2,1)} %g_ref.1), custom_call_target="tpu_custom_call" | custom-call | tf_op jit(solution)/shard_map/reduce_all/pallas_call | solution.py:429
  71.3 17.0 %solve.1.p_ref = bf16[688,256]{1,0:T(8,128)(2,1)} custom-call(f32[2,512,128]{2,1,0:T(8,128)} %get-tuple-element.9.fg_ref, f32[256,128]{1,0:T(8,128)} %bitcast.5, f32[16,128]{1,0:T(8,128)} %get-tuple-element.11.t_ref, f32[3,128,128]{2,1,0:T(8,128)} %get-tuple-element.12.s_ref, bf16[688,256]{1,0:T(8,128)(2,1)} %bitcast.4), custom_call_target="tpu_custom_call" | custom-call | tf_op jit(solution)/shard_map/solve/pallas_call | solution.py:644
  88.4 35.2 %gather.1 = bf16[16,688,256]{2,1,0:T(8,128)(2,1)} custom-call(bf16[688,256]{1,0:T(8,128)(2,1)} %solve.1.p_ref), custom_call_target="tpu_custom_call" | custom-call | tf_op jit(solution)/shard_map/gather/pallas_call | solution.py:752
  123.6 4.3 %turn.1 = bf16[256,11008]{1,0:T(8,128)(2,1)} custom-call(bf16[11008,256]{1,0:T(8,128)(2,1)} %bitcast.3), custom_call_target="tpu_custom_call" | custom-call | tf_op jit(solution)/shard_map/turn/pallas_call | solution.py:785
